TPU v7x, 32 devices: a whole 2x2x4 slice. The times are simulated.
32 devices in a mesh: seq: 4 (over y, core), dp: 8 (over z, x).
Axes of the slice: x: 2, y: 2, z: 4, core: 2. Of those that a mesh axis runs over, the one named last changes fastest.
Arguments:
- tokens: bfloat16 [8, 768, 768], P('dp', 'seq'), may hold values from -6 to 6
- lengths: int32 [8], P('dp'), may hold values from 192 to 768, as said below
- norm_one: bfloat16 [768], P(('seq', 'dp')), may hold values from 0.099609375 to 1.8984375
- query_one: bfloat16 [768, 768], P(('seq', 'dp')), may hold values from -0.21875 to 0.21875
- key_one: bfloat16 [768, 768], P(('seq', 'dp')), may hold values from -0.21875 to 0.21875
- value_one: bfloat16 [768, 768], P(('seq', 'dp')), may hold values from -0.21875 to 0.21875
- shift_taps: bfloat16 [768, 64], P(('seq', 'dp')), may hold values from -0.75 to 0.75
- decay_log: bfloat16 [768, 64], P(('seq', 'dp')), may hold values from -9 to -1.1953125
- turn_angle: bfloat16 [768, 64], P(('seq', 'dp')), may hold values from -3.140625 to 3.140625
- mix_real: bfloat16 [768, 64], P(('seq', 'dp')), may hold values from -0.059814453 to 0.059814453
- mix_imag: bfloat16 [768, 64], P(('seq', 'dp')), may hold values from -0.059814453 to 0.059814453
- skip_gain: bfloat16 [768], P(('seq', 'dp')), may hold values from -4 to 4
- out_one: bfloat16 [768, 768], P(('seq', 'dp')), may hold values from -0.21875 to 0.21875
- norm_two: bfloat16 [768], P(('seq', 'dp')), may hold values from 0.099609375 to 1.8984375
- up_one: bfloat16 [768, 3072], P(('seq', 'dp')), may hold values from -0.21875 to 0.21875
- down_one: bfloat16 [3072, 768], P(('seq', 'dp')), may hold values from -0.109375 to 0.109375
- norm_three: bfloat16 [768], P(('seq', 'dp')), may hold values from 0.099609375 to 1.8984375
- qkv_weight: bfloat16 [768, 2304], P(('seq', 'dp')), may hold values from -0.21875 to 0.21875
- out_two: bfloat16 [768, 768], P(('seq', 'dp')), may hold values from -3 to 3
- norm_four: bfloat16 [768], P(('seq', 'dp')), may hold values from 0.099609375 to 1.8984375
- up_two: bfloat16 [768, 3072], P(('seq', 'dp')), may hold values from -0.21875 to 0.21875
- down_two: bfloat16 [3072, 768], P(('seq', 'dp')), may hold values from -0.109375 to 0.109375
- cotangent: bfloat16 [8, 768, 768], P('dp', 'seq'), may hold values from -6 to 6
Outputs:
- activations: bfloat16 [8, 768, 768], P('dp', 'seq')
- input_grad: float32 [8, 768, 768], P('dp', 'seq')
- grad_norm_one: float32 [768], P(('seq', 'dp'))
- grad_query_one: float32 [768, 768], P(('seq', 'dp'))
- grad_key_one: float32 [768, 768], P(('seq', 'dp'))
- grad_value_one: float32 [768, 768], P(('seq', 'dp'))
- grad_shift_taps: float32 [768, 64], P(('seq', 'dp'))
- grad_decay_log: float32 [768, 64], P(('seq', 'dp'))
- grad_turn_angle: float32 [768, 64], P(('seq', 'dp'))
- grad_mix_real: float32 [768, 64], P(('seq', 'dp'))
- grad_mix_imag: float32 [768, 64], P(('seq', 'dp'))
- grad_skip_gain: float32 [768], P(('seq', 'dp'))
- grad_out_one: float32 [768, 768], P(('seq', 'dp'))
- grad_norm_two: float32 [768], P(('seq', 'dp'))
- grad_up_one: float32 [768, 3072], P(('seq', 'dp'))
- grad_down_one: float32 [3072, 768], P(('seq', 'dp'))
- grad_norm_three: float32 [768], P(('seq', 'dp'))
- grad_qkv_weight: float32 [768, 2304], P(('seq', 'dp'))
- grad_out_two: float32 [768, 768], P(('seq', 'dp'))
- grad_norm_four: float32 [768], P(('seq', 'dp'))
- grad_up_two: float32 [768, 3072], P(('seq', 'dp'))
- grad_down_two: float32 [3072, 768], P(('seq', 'dp'))
Inputs may be any that keep to these rules, and one draw needn't show every extreme that they name: `lengths`: in each aligned run of four sequences exactly one, which one drawn from the seed, has 192 tokens and the other three have 768.
All inputs are finite; a program needn't handle non-finite values.
Results may differ from a plain program's by a relative error of at most 0.024.
Values may be sent and summed in bfloat16 or wider, within the bound.
A program may use at most 320 MiB of HBM per device.

v0:
```python
from functools import partial
import math

import jax
import jax.numpy as jnp
from jax import lax
from jax.sharding import PartitionSpec as P

HEADS = 12
HDIM = 64


EPSILON = 1e-05
HIGHEST = lax.Precision.HIGHEST
MASKED = -1e30


def passed_along(value, axis, steps):
    count = lax.axis_size(axis)
    leading, last = (max(0, -steps), min(count, count - steps))
    return lax.ppermute(value, axis, [(source, source + steps) for source in range(leading, last)])


def carried_in(value, axis, join, neutral):
    place = lax.axis_index(axis)
    gathered = jax.tree.map(
        lambda a, kind: lax.all_gather(a.astype(kind), axis),
        value,
        (jnp.bfloat16, jnp.bfloat16, jnp.bfloat16, jnp.bfloat16),
    )
    state = jax.tree.map(lambda a, e: jnp.zeros_like(a) + jnp.asarray(e, a.dtype), value, neutral)

    def carried_one(lap, state):
        return join(
            state,
            jax.tree.map(
                lambda a, own: lax.dynamic_index_in_dim(a, lap, 0, False).astype(own.dtype),
                gathered,
                value,
            ),
        )

    return lax.fori_loop(0, place, carried_one, state)


def entering(value, axis, join, neutral):
    count = lax.axis_size(axis)
    place = lax.axis_index(axis)
    ahead = count - 1 - place
    gathered = jax.tree.map(
        lambda a, kind: lax.all_gather(a.astype(kind), axis),
        value,
        jax.tree.map(lambda a: jnp.bfloat16 if a.dtype == jnp.float32 else a.dtype, value),
    )
    state = jax.tree.map(lambda a, e: jnp.zeros_like(a) + jnp.asarray(e, a.dtype), value, neutral)

    def entering_one(lap, state):
        source = count - 1 - lap
        return join(
            state,
            jax.tree.map(
                lambda a, own: lax.dynamic_index_in_dim(a, source, 0, False).astype(own.dtype),
                gathered,
                value,
            ),
        )

    return lax.fori_loop(0, ahead, entering_one, state)


def layer_norm(residual, scale_gain):
    average = jnp.mean(residual, axis=-1, keepdims=True)
    centered = residual - average
    variance = jnp.mean(centered * centered, axis=-1, keepdims=True)
    return centered * lax.rsqrt(variance + EPSILON) * scale_gain


def product(left_side, right_side):
    return jnp.dot(left_side, right_side, preferred_element_type=jnp.float32)


def product_back(left_side, right_side):
    return lax.dot_general(
        left_side, right_side, (((1,), (1,)), ((), ())), preferred_element_type=jnp.float32
    )


def product_sum(left_side, right_side):
    return lax.dot_general(
        left_side, right_side, (((0,), (0,)), ((), ())), preferred_element_type=jnp.float32
    )


def feed_forward(residual, scale_gain, up_weight, down_weight):
    normed = layer_norm(residual, scale_gain).astype(jnp.bfloat16)
    pre_act = product(normed, up_weight)
    activated = jax.nn.gelu(pre_act).astype(jnp.bfloat16)
    return (residual + product(activated, down_weight), (normed, pre_act, activated))


def feed_back(residual, scale_gain, up_weight, down_weight, stored, grad_residual):
    normed, pre_act, activated = stored
    grad_branch = grad_residual.astype(jnp.bfloat16)
    grad_down = product_sum(activated, grad_branch)
    grad_activated = product_back(grad_branch, down_weight)
    gelu_pull = jax.vjp(jax.nn.gelu, pre_act)[1]
    grad_pre = gelu_pull(grad_activated)[0].astype(jnp.bfloat16)
    grad_up = product_sum(normed, grad_pre)
    grad_normed = product_back(grad_pre, up_weight)
    norm_pull = jax.vjp(layer_norm, residual, scale_gain)[1]
    grad_input, grad_gain = norm_pull(grad_normed)
    return (grad_residual + grad_input, grad_gain, grad_up, grad_down)


def apply_taps(extended, tap_gains, tok_rows):
    tap_count = tap_gains.shape[1]

    def add_tap(offset, running):
        window = lax.dynamic_slice_in_dim(extended, tap_count - 1 - offset, tok_rows, 0)
        return running + window * lax.dynamic_slice_in_dim(tap_gains, offset, 1, 1)[:, 0]

    return lax.fori_loop(
        0, tap_count, add_tap, jnp.zeros((tok_rows, tap_gains.shape[0]), jnp.float32)
    )


def apply_taps_back(extended_grad, tap_gains, tok_rows):
    tap_count = tap_gains.shape[1]

    def add_tap(offset, running):
        window = lax.dynamic_slice_in_dim(extended_grad, offset, tok_rows, 0)
        return running + window * lax.dynamic_slice_in_dim(tap_gains, offset, 1, 1)[:, 0]

    return lax.fori_loop(
        0, tap_count, add_tap, jnp.zeros((tok_rows, tap_gains.shape[0]), jnp.float32)
    )


def tap_grads(extended, shifted_grad):
    tok_rows = shifted_grad.shape[0]
    tap_count = extended.shape[0] - tok_rows + 1

    def one_tap(offset):
        window = lax.dynamic_slice_in_dim(extended, tap_count - 1 - offset, tok_rows, 0)
        return jnp.sum(window * shifted_grad, axis=0)

    return lax.map(one_tap, jnp.arange(tap_count, dtype=jnp.int32)).T


def power_table(decay_rate, rotation, exponents):
    scaled = exponents[:, None, None]
    magnitude = jnp.exp(-scaled * decay_rate[None])
    return (
        magnitude * jnp.cos(scaled * rotation[None]),
        magnitude * jnp.sin(scaled * rotation[None]),
    )


def read_table(decay_rate, rotation, real_mix, imag_mix, block_rows):
    power_real, power_imag = power_table(
        decay_rate, rotation, jnp.arange(1, block_rows + 1, dtype=jnp.float32)
    )
    return (
        real_mix * power_real - imag_mix * power_imag,
        real_mix * power_imag + imag_mix * power_real,
    )


def local_ssm(signal, decay_log, rotation, real_mix, imag_mix, skip_gain, block_rows):
    tok_rows, features = signal.shape
    decay_rate = jnp.exp(decay_log)
    steps_in = jnp.arange(block_rows, dtype=jnp.float32)
    power_real, power_imag = power_table(decay_rate, rotation, steps_in)
    kernel = jnp.sum(power_real * real_mix[None] - power_imag * imag_mix[None], axis=2)
    lag_table = jnp.arange(block_rows)[:, None] - jnp.arange(block_rows)[None, :]
    toeplitz = jnp.where((lag_table >= 0)[:, :, None], kernel[jnp.maximum(lag_table, 0)], 0.0)
    pieces = signal.reshape(tok_rows // block_rows, block_rows, features)
    inside = jnp.einsum("tsc,bsc->btc", toeplitz, pieces, precision=HIGHEST)
    end_real, end_imag = power_table(decay_rate, rotation, block_rows - 1 - steps_in)
    state_real = jnp.einsum("bsc,scn->bcn", pieces, end_real, precision=HIGHEST)
    state_imag = jnp.einsum("bsc,scn->bcn", pieces, end_imag, precision=HIGHEST)
    jump_real, jump_imag = power_table(
        decay_rate, rotation, jnp.full((1,), block_rows, jnp.float32)
    )

    def carry_block(carried, item):
        carried_real, carried_imag = carried
        item_real, item_imag = item
        next_real = jump_real[0] * carried_real - jump_imag[0] * carried_imag + item_real
        next_imag = jump_real[0] * carried_imag + jump_imag[0] * carried_real + item_imag
        return ((next_real, next_imag), (carried_real, carried_imag))

    nothing = jnp.zeros_like(decay_rate)
    (final_real, final_imag), (start_real, start_imag) = lax.scan(
        carry_block, (nothing, nothing), (state_real, state_imag)
    )
    out_real, out_imag = read_table(decay_rate, rotation, real_mix, imag_mix, block_rows)
    across = jnp.einsum("tcn,bcn->btc", out_real, start_real, precision=HIGHEST) - jnp.einsum(
        "tcn,bcn->btc", out_imag, start_imag, precision=HIGHEST
    )
    result = (inside + across).reshape(tok_rows, features) + skip_gain * signal
    return (result, final_real, final_imag)


def inject_ssm(
    enter_real, enter_imag, decay_log, rotation, real_mix, imag_mix, tok_rows, block_rows
):
    decay_rate = jnp.exp(decay_log)
    lift_real, lift_imag = power_table(
        decay_rate, rotation, block_rows * jnp.arange(tok_rows // block_rows, dtype=jnp.float32)
    )
    start_real = lift_real * enter_real - lift_imag * enter_imag
    start_imag = lift_real * enter_imag + lift_imag * enter_real
    out_real, out_imag = read_table(decay_rate, rotation, real_mix, imag_mix, block_rows)
    across = jnp.einsum("tcn,bcn->btc", out_real, start_real, precision=HIGHEST) - jnp.einsum(
        "tcn,bcn->btc", out_imag, start_imag, precision=HIGHEST
    )
    return across.reshape(tok_rows, decay_log.shape[0])


def device_decay(decay_log, rotation, tok_rows):
    table_real, table_imag = power_table(
        jnp.exp(decay_log), rotation, jnp.full((1,), tok_rows, jnp.float32)
    )
    return (table_real[0], table_imag[0])


def chain_states(earlier, later):
    first_real, first_imag, first_state_real, first_state_imag = earlier
    second_real, second_imag, second_state_real, second_state_imag = later
    return (
        first_real * second_real - first_imag * second_imag,
        first_real * second_imag + first_imag * second_real,
        second_real * first_state_real - second_imag * first_state_imag + second_state_real,
        second_real * first_state_imag + second_imag * first_state_real + second_state_imag,
    )


def masked_scores(queries, key_block, row_places, key_places, length):
    scores = jnp.einsum(
        "qhd,khd->hqk", queries, key_block, preferred_element_type=jnp.float32
    ) * HDIM ** (-0.5)
    allowed = (key_places[None, :] <= row_places[:, None]) & (key_places[None, :] < length)
    return jnp.where(allowed[None], scores, MASKED)


def row_log_total(queries, all_keys, row_places, length, block_keys, block_limit):
    key_count = all_keys.shape[0]
    key_heads = all_keys.reshape(key_count, HEADS, HDIM)

    def step_block(block_index, carried):
        running_max, running_sum = carried
        first_row = block_index * block_keys
        key_block = lax.dynamic_slice_in_dim(key_heads, first_row, block_keys, 0)
        key_places = first_row + jnp.arange(block_keys, dtype=jnp.int32)
        scores = masked_scores(queries, key_block, row_places, key_places, length)
        new_max = jnp.maximum(running_max, jnp.max(scores, axis=2))
        new_sum = running_sum * jnp.exp(running_max - new_max) + jnp.sum(
            jnp.exp(scores - new_max[:, :, None]), axis=2
        )
        return (new_max, new_sum)

    start_max = jnp.full((HEADS, queries.shape[0]), MASKED, jnp.float32)
    start_sum = jnp.zeros((HEADS, queries.shape[0]), jnp.float32)
    final_max, final_sum = lax.fori_loop(0, block_limit, step_block, (start_max, start_sum))
    return final_max + jnp.log(final_sum)


def attend_rows(
    queries, all_keys, all_values, row_places, length, log_total, block_keys, block_limit
):
    key_count = all_keys.shape[0]
    key_heads = all_keys.reshape(key_count, HEADS, HDIM)
    value_heads = all_values.reshape(key_count, HEADS, HDIM)

    def step_block(block_index, output):
        first_row = block_index * block_keys
        key_block = lax.dynamic_slice_in_dim(key_heads, first_row, block_keys, 0)
        value_block = lax.dynamic_slice_in_dim(value_heads, first_row, block_keys, 0)
        key_places = first_row + jnp.arange(block_keys, dtype=jnp.int32)
        scores = masked_scores(queries, key_block, row_places, key_places, length)
        att_weights = jnp.exp(scores - log_total[:, :, None]).astype(jnp.bfloat16)
        return output + jnp.einsum(
            "hqk,khd->qhd", att_weights, value_block, preferred_element_type=jnp.float32
        )

    output = lax.fori_loop(0, block_limit, step_block, jnp.zeros(queries.shape, jnp.float32))
    return output.reshape(queries.shape[0], HEADS * HDIM)


def attend_back(
    queries,
    all_keys,
    all_values,
    row_places,
    length,
    log_total,
    grad_heads,
    delta,
    block_keys,
    block_limit,
):
    key_count = all_keys.shape[0]
    key_heads = all_keys.reshape(key_count, HEADS, HDIM)
    value_heads = all_values.reshape(key_count, HEADS, HDIM)

    def step_block(block_index, carried):
        grad_query, key_store, value_store = carried
        first_row = block_index * block_keys
        key_block = lax.dynamic_slice_in_dim(key_heads, first_row, block_keys, 0)
        value_block = lax.dynamic_slice_in_dim(value_heads, first_row, block_keys, 0)
        key_places = first_row + jnp.arange(block_keys, dtype=jnp.int32)
        scores = masked_scores(queries, key_block, row_places, key_places, length)
        probs = jnp.exp(scores - log_total[:, :, None])
        prob_grad = jnp.einsum(
            "qhd,khd->hqk", grad_heads, value_block, preferred_element_type=jnp.float32
        )
        grad_scores = (probs * (prob_grad - delta[:, :, None])).astype(jnp.bfloat16)
        grad_query = grad_query + jnp.einsum(
            "hqk,khd->qhd", grad_scores, key_block, preferred_element_type=jnp.float32
        )
        key_term = jnp.einsum(
            "hqk,qhd->khd", grad_scores, queries, preferred_element_type=jnp.float32
        )
        value_term = jnp.einsum(
            "hqk,qhd->khd",
            probs.astype(jnp.bfloat16),
            grad_heads,
            preferred_element_type=jnp.float32,
        )
        key_store = lax.dynamic_update_slice_in_dim(key_store, key_term, first_row, 0)
        value_store = lax.dynamic_update_slice_in_dim(value_store, value_term, first_row, 0)
        return (grad_query, key_store, value_store)

    empty_store = jnp.zeros((key_count, HEADS, HDIM), jnp.float32)
    grad_query, key_store, value_store = lax.fori_loop(
        0,
        block_limit,
        step_block,
        (jnp.zeros(queries.shape, jnp.float32), empty_store, empty_store),
    )
    return (
        grad_query,
        key_store.reshape(key_store.shape[0], HEADS * HDIM),
        value_store.reshape(value_store.shape[0], HEADS * HDIM),
    )


def shards(
    tokens,
    lengths,
    norm_one,
    query_one,
    key_one,
    value_one,
    shift_taps,
    decay_log,
    turn_angle,
    mix_real,
    mix_imag,
    skip_gain,
    out_one,
    norm_two,
    up_one,
    down_one,
    norm_three,
    qkv_weight,
    out_two,
    norm_four,
    up_two,
    down_two,
    cotangent,
):
    (
        norm_one,
        query_one,
        key_one,
        value_one,
        shift_taps,
        decay_log,
        turn_angle,
        mix_real,
        mix_imag,
        skip_gain,
        out_one,
        norm_two,
        up_one,
        down_one,
        norm_three,
        qkv_weight,
        out_two,
        norm_four,
        up_two,
        down_two,
    ) = (
        lax.all_gather(norm_one, ("seq", "dp"), axis=0, tiled=True),
        lax.all_gather(query_one, ("seq", "dp"), axis=0, tiled=True),
        lax.all_gather(key_one, ("seq", "dp"), axis=0, tiled=True),
        lax.all_gather(value_one, ("seq", "dp"), axis=0, tiled=True),
        lax.all_gather(shift_taps, ("seq", "dp"), axis=0, tiled=True),
        lax.all_gather(decay_log, ("seq", "dp"), axis=0, tiled=True),
        lax.all_gather(turn_angle, ("seq", "dp"), axis=0, tiled=True),
        lax.all_gather(mix_real, ("seq", "dp"), axis=0, tiled=True),
        lax.all_gather(mix_imag, ("seq", "dp"), axis=0, tiled=True),
        lax.all_gather(skip_gain, ("seq", "dp"), axis=0, tiled=True),
        lax.all_gather(out_one, ("seq", "dp"), axis=0, tiled=True),
        lax.all_gather(norm_two, ("seq", "dp"), axis=0, tiled=True),
        lax.all_gather(up_one, ("seq", "dp"), axis=0, tiled=True),
        lax.all_gather(down_one, ("seq", "dp"), axis=0, tiled=True),
        lax.all_gather(norm_three, ("seq", "dp"), axis=0, tiled=True),
        lax.all_gather(qkv_weight, ("seq", "dp"), axis=0, tiled=True),
        lax.all_gather(out_two, ("seq", "dp"), axis=0, tiled=True),
        lax.all_gather(norm_four, ("seq", "dp"), axis=0, tiled=True),
        lax.all_gather(up_two, ("seq", "dp"), axis=0, tiled=True),
        lax.all_gather(down_two, ("seq", "dp"), axis=0, tiled=True),
    )
    tok_rows = tokens.shape[1]
    features = tokens.shape[2]
    key_count = tok_rows * lax.axis_size("seq")
    block_rows = min(32, tok_rows)
    block_keys = math.gcd(key_count, 512)
    seq_place = lax.axis_index("seq")
    row_places = seq_place * tok_rows + jnp.arange(tok_rows, dtype=jnp.int32)
    block_limit = ((seq_place + 1) * tok_rows + block_keys - 1) // block_keys
    length = lengths[0]
    live_mask = (row_places < length).astype(jnp.float32)[:, None]
    residual_zero = tokens[0].astype(jnp.float32)
    gain_one = norm_one.astype(jnp.float32)
    gain_two = norm_two.astype(jnp.float32)
    gain_three = norm_three.astype(jnp.float32)
    gain_four = norm_four.astype(jnp.float32)
    tap_gains = shift_taps.astype(jnp.float32)
    tap_count = tap_gains.shape[1]
    decay_value = decay_log.astype(jnp.float32)
    rotation = turn_angle.astype(jnp.float32)
    real_mix = mix_real.astype(jnp.float32)
    imag_mix = mix_imag.astype(jnp.float32)
    skip_value = skip_gain.astype(jnp.float32)
    normed_one = layer_norm(residual_zero, gain_one).astype(jnp.bfloat16)
    queries_h3 = product(normed_one, query_one)
    keys_h3 = product(normed_one, key_one)
    values_h3 = product(normed_one, value_one)
    earlier_rows = passed_along(
        keys_h3[tok_rows - tap_count + 1 :].astype(jnp.bfloat16), "seq", 1
    ).astype(jnp.float32)
    extended = jnp.concatenate([earlier_rows, keys_h3], axis=0)
    shifted = apply_taps(extended, tap_gains, tok_rows)
    signal = live_mask * shifted * values_h3
    local_out, last_real, last_imag = local_ssm(
        signal, decay_value, rotation, real_mix, imag_mix, skip_value, block_rows
    )
    span_real, span_imag = device_decay(decay_value, rotation, tok_rows)
    unit_real = jnp.ones_like(span_real)
    nothing = jnp.zeros_like(span_real)
    incoming = carried_in(
        (span_real, span_imag, last_real, last_imag),
        "seq",
        chain_states,
        (unit_real, nothing, nothing, nothing),
    )
    enter_real = incoming[2]
    enter_imag = incoming[3]
    ssm_out = local_out + inject_ssm(
        enter_real, enter_imag, decay_value, rotation, real_mix, imag_mix, tok_rows, block_rows
    )
    gated = (queries_h3 * ssm_out).astype(jnp.bfloat16)
    residual_one = residual_zero + product(gated, out_one)
    residual_two, stored_two = feed_forward(residual_one, gain_two, up_one, down_one)
    normed_three = layer_norm(residual_two, gain_three).astype(jnp.bfloat16)
    joint = product(normed_three, qkv_weight).astype(jnp.bfloat16)
    att_q = joint[:, :features].reshape(tok_rows, HEADS, HDIM)
    own_keys = joint[:, features : 2 * features]
    own_values = joint[:, 2 * features :]
    all_keys, all_values = (
        lax.all_gather(own_keys, "seq", axis=0, tiled=True),
        lax.all_gather(own_values, "seq", axis=0, tiled=True),
    )
    log_total = row_log_total(att_q, all_keys, row_places, length, block_keys, block_limit)
    attended_full = attend_rows(
        att_q, all_keys, all_values, row_places, length, log_total, block_keys, block_limit
    )
    attended = attended_full.astype(jnp.bfloat16)
    residual_three = residual_two + product(attended, out_two)
    residual_four, stored_four = feed_forward(residual_three, gain_four, up_two, down_two)
    activations = (live_mask * residual_four).astype(jnp.bfloat16)
    grad_four = live_mask * cotangent[0].astype(jnp.float32)
    grad_three, grad_norm_four, grad_up_two, grad_down_two = feed_back(
        residual_three, gain_four, up_two, down_two, stored_four, grad_four
    )
    branch_three = grad_three.astype(jnp.bfloat16)
    grad_out_two = product_sum(attended, branch_three)
    grad_attended = product_back(branch_three, out_two).astype(jnp.bfloat16)
    grad_heads = grad_attended.reshape(tok_rows, HEADS, HDIM)
    delta = jnp.sum(
        (grad_attended.astype(jnp.float32) * attended_full).reshape(tok_rows, HEADS, HDIM), axis=2
    ).T
    back_keys, back_values = (
        lax.all_gather(own_keys, "seq", axis=0, tiled=True),
        lax.all_gather(own_values, "seq", axis=0, tiled=True),
    )
    grad_query, key_terms, value_terms = attend_back(
        att_q,
        back_keys,
        back_values,
        row_places,
        length,
        log_total,
        grad_heads,
        delta,
        block_keys,
        block_limit,
    )
    key_part, value_part = (
        lax.psum_scatter(
            key_terms.astype(jnp.bfloat16), "seq", scatter_dimension=0, tiled=True
        ).astype(jnp.float32),
        lax.psum_scatter(
            value_terms.astype(jnp.bfloat16), "seq", scatter_dimension=0, tiled=True
        ).astype(jnp.float32),
    )
    score_scale = HDIM ** (-0.5)
    grad_joint = jnp.concatenate(
        [grad_query.reshape(tok_rows, features) * score_scale, key_part * score_scale, value_part],
        axis=1,
    ).astype(jnp.bfloat16)
    grad_qkv_weight = product_sum(normed_three, grad_joint)
    grad_normed_three = product_back(grad_joint, qkv_weight)
    norm_pull_three = jax.vjp(layer_norm, residual_two, gain_three)[1]
    grad_from_three, grad_norm_three = norm_pull_three(grad_normed_three)
    grad_two = grad_three + grad_from_three
    grad_one, grad_norm_two, grad_up_one, grad_down_one = feed_back(
        residual_one, gain_two, up_one, down_one, stored_two, grad_two
    )
    branch_one = grad_one.astype(jnp.bfloat16)
    grad_out_one = product_sum(gated, branch_one)
    gated_grad = product_back(branch_one, out_one)
    grad_queries = (gated_grad * ssm_out).astype(jnp.bfloat16)
    ssm_grad = gated_grad * queries_h3
    inject_pull = jax.vjp(
        partial(inject_ssm, tok_rows=tok_rows, block_rows=block_rows),
        enter_real,
        enter_imag,
        decay_value,
        rotation,
        real_mix,
        imag_mix,
    )[1]
    (
        back_real,
        back_imag,
        decay_grad_first,
        rotation_grad_first,
        real_grad_first,
        imag_grad_first,
    ) = inject_pull(ssm_grad)
    outgoing = entering(
        (span_real, -span_imag, back_real, back_imag),
        "seq",
        chain_states,
        (unit_real, nothing, nothing, nothing),
    )
    adjoint_real = outgoing[2]
    adjoint_imag = outgoing[3]
    decay_pull = jax.vjp(partial(device_decay, tok_rows=tok_rows), decay_value, rotation)[1]
    decay_grad_second, rotation_grad_second = decay_pull(
        (
            adjoint_real * enter_real + adjoint_imag * enter_imag,
            adjoint_imag * enter_real - adjoint_real * enter_imag,
        )
    )
    local_pull = jax.vjp(
        partial(local_ssm, block_rows=block_rows),
        signal,
        decay_value,
        rotation,
        real_mix,
        imag_mix,
        skip_value,
    )[1]
    (
        signal_grad,
        decay_grad_third,
        rotation_grad_third,
        real_grad_third,
        imag_grad_third,
        grad_skip_gain,
    ) = local_pull((ssm_grad, adjoint_real, adjoint_imag))
    grad_decay_log = decay_grad_first + decay_grad_second + decay_grad_third
    grad_turn_angle = rotation_grad_first + rotation_grad_second + rotation_grad_third
    grad_mix_real = real_grad_first + real_grad_third
    grad_mix_imag = imag_grad_first + imag_grad_third
    shifted_grad = signal_grad * live_mask * values_h3
    grad_values = (signal_grad * live_mask * shifted).astype(jnp.bfloat16)
    later_rows = passed_along(shifted_grad[: tap_count - 1].astype(jnp.bfloat16), "seq", -1).astype(
        jnp.float32
    )
    grad_keys = apply_taps_back(
        jnp.concatenate([shifted_grad, later_rows], axis=0), tap_gains, tok_rows
    ).astype(jnp.bfloat16)
    grad_shift_taps = tap_grads(extended, shifted_grad)
    grad_query_one = product_sum(normed_one, grad_queries)
    grad_key_one = product_sum(normed_one, grad_keys)
    grad_value_one = product_sum(normed_one, grad_values)
    grad_normed_one = (
        product_back(grad_queries, query_one)
        + product_back(grad_keys, key_one)
        + product_back(grad_values, value_one)
    )
    norm_pull_one = jax.vjp(layer_norm, residual_zero, gain_one)[1]
    grad_from_one, grad_norm_one = norm_pull_one(grad_normed_one)
    input_grad = grad_one + grad_from_one
    (
        grad_norm_one,
        grad_query_one,
        grad_key_one,
        grad_value_one,
        grad_shift_taps,
        grad_decay_log,
        grad_turn_angle,
        grad_mix_real,
        grad_mix_imag,
        grad_skip_gain,
        grad_out_one,
        grad_norm_two,
        grad_up_one,
        grad_down_one,
        grad_norm_three,
        grad_qkv_weight,
        grad_out_two,
        grad_norm_four,
        grad_up_two,
        grad_down_two,
    ) = (
        lax.psum_scatter(grad_norm_one, ("seq", "dp"), scatter_dimension=0, tiled=True),
        lax.psum_scatter(grad_query_one, ("seq", "dp"), scatter_dimension=0, tiled=True),
        lax.psum_scatter(grad_key_one, ("seq", "dp"), scatter_dimension=0, tiled=True),
        lax.psum_scatter(grad_value_one, ("seq", "dp"), scatter_dimension=0, tiled=True),
        lax.psum_scatter(grad_shift_taps, ("seq", "dp"), scatter_dimension=0, tiled=True),
        lax.psum_scatter(grad_decay_log, ("seq", "dp"), scatter_dimension=0, tiled=True),
        lax.psum_scatter(grad_turn_angle, ("seq", "dp"), scatter_dimension=0, tiled=True),
        lax.psum_scatter(grad_mix_real, ("seq", "dp"), scatter_dimension=0, tiled=True),
        lax.psum_scatter(grad_mix_imag, ("seq", "dp"), scatter_dimension=0, tiled=True),
        lax.psum_scatter(grad_skip_gain, ("seq", "dp"), scatter_dimension=0, tiled=True),
        lax.psum_scatter(grad_out_one, ("seq", "dp"), scatter_dimension=0, tiled=True),
        lax.psum_scatter(grad_norm_two, ("seq", "dp"), scatter_dimension=0, tiled=True),
        lax.psum_scatter(grad_up_one, ("seq", "dp"), scatter_dimension=0, tiled=True),
        lax.psum_scatter(grad_down_one, ("seq", "dp"), scatter_dimension=0, tiled=True),
        lax.psum_scatter(grad_norm_three, ("seq", "dp"), scatter_dimension=0, tiled=True),
        lax.psum_scatter(grad_qkv_weight, ("seq", "dp"), scatter_dimension=0, tiled=True),
        lax.psum_scatter(grad_out_two, ("seq", "dp"), scatter_dimension=0, tiled=True),
        lax.psum_scatter(grad_norm_four, ("seq", "dp"), scatter_dimension=0, tiled=True),
        lax.psum_scatter(grad_up_two, ("seq", "dp"), scatter_dimension=0, tiled=True),
        lax.psum_scatter(grad_down_two, ("seq", "dp"), scatter_dimension=0, tiled=True),
    )
    return (
        activations[None],
        input_grad[None],
        grad_norm_one,
        grad_query_one,
        grad_key_one,
        grad_value_one,
        grad_shift_taps,
        grad_decay_log,
        grad_turn_angle,
        grad_mix_real,
        grad_mix_imag,
        grad_skip_gain,
        grad_out_one,
        grad_norm_two,
        grad_up_one,
        grad_down_one,
        grad_norm_three,
        grad_qkv_weight,
        grad_out_two,
        grad_norm_four,
        grad_up_two,
        grad_down_two,
    )


def solution(mesh):
    placed = (
        P("dp", "seq", None),
        P("dp"),
        P(("seq", "dp")),
        P(("seq", "dp"), None),
        P(("seq", "dp"), None),
        P(("seq", "dp"), None),
        P(("seq", "dp"), None),
        P(("seq", "dp"), None),
        P(("seq", "dp"), None),
        P(("seq", "dp"), None),
        P(("seq", "dp"), None),
        P(("seq", "dp")),
        P(("seq", "dp"), None),
        P(("seq", "dp")),
        P(("seq", "dp"), None),
        P(("seq", "dp"), None),
        P(("seq", "dp")),
        P(("seq", "dp"), None),
        P(("seq", "dp"), None),
        P(("seq", "dp")),
        P(("seq", "dp"), None),
        P(("seq", "dp"), None),
        P("dp", "seq", None),
    )
    return jax.shard_map(
        shards,
        mesh=mesh,
        in_specs=placed,
        out_specs=(
            P("dp", "seq", None),
            P("dp", "seq", None),
            P(("seq", "dp")),
            P(("seq", "dp"), None),
            P(("seq", "dp"), None),
            P(("seq", "dp"), None),
            P(("seq", "dp"), None),
            P(("seq", "dp"), None),
            P(("seq", "dp"), None),
            P(("seq", "dp"), None),
            P(("seq", "dp"), None),
            P(("seq", "dp")),
            P(("seq", "dp"), None),
            P(("seq", "dp")),
            P(("seq", "dp"), None),
            P(("seq", "dp"), None),
            P(("seq", "dp")),
            P(("seq", "dp"), None),
            P(("seq", "dp"), None),
            P(("seq", "dp")),
            P(("seq", "dp"), None),
            P(("seq", "dp"), None),
        ),
        check_vma=False,
    )
```

profile of v0, /device:TPU:0, one launch (start us, length us, event | category | flops | bytes accessed | tf_op | source)
XLA Modules:
  0.0 4056.2 jit_solution(9565988924966226027)
XLA Ops:
  61.7 67.7 %all_gather.108 = bf16[768,64]{1,0:T(8,128)(2,1)S(1)} all-gather(bf16[24,64]{1,0:T(8,128)(2,1)} %param.53), channel_id=1, replica_groups=mesh['seq'=4,'dp'=8] {'seq','dp'}, dimensions={0}, use_global_device_ids=true | all-gather | bytes 101376 | tf_op jit(solution)/shard_map/all_gather | solution.py:402
  129.4 64.9 %all_gather.107 = bf16[768,64]{1,0:T(8,128)(2,1)S(1)} all-gather(bf16[24,64]{1,0:T(8,128)(2,1)} %param.52), channel_id=1, replica_groups=mesh['seq'=4,'dp'=8] {'seq','dp'}, dimensions={0}, use_global_device_ids=true | all-gather | bytes 101376 | tf_op jit(solution)/shard_map/all_gather | solution.py:401
  194.3 67.0 %all_gather.105 = bf16[768,64]{1,0:T(8,128)(2,1)S(1)} all-gather(bf16[24,64]{1,0:T(8,128)(2,1)} %param.51), channel_id=1, replica_groups=mesh['seq'=4,'dp'=8] {'seq','dp'}, dimensions={0}, use_global_device_ids=true | all-gather | bytes 101376 | tf_op jit(solution)/shard_map/all_gather | solution.py:400
  262.0 65.4 %all_gather.109 = bf16[768,64]{1,0:T(8,128)(2,1)S(1)} all-gather(bf16[24,64]{1,0:T(8,128)(2,1)} %param.54), channel_id=1, replica_groups=mesh['seq'=4,'dp'=8] {'seq','dp'}, dimensions={0}, use_global_device_ids=true | all-gather | bytes 101376 | tf_op jit(solution)/shard_map/all_gather | solution.py:403
  327.5 67.5 %all_gather.110 = bf16[768,64]{1,0:T(8,128)(2,1)S(1)} all-gather(bf16[24,64]{1,0:T(8,128)(2,1)} %param.55), channel_id=1, replica_groups=mesh['seq'=4,'dp'=8] {'seq','dp'}, dimensions={0}, use_global_device_ids=true | all-gather | bytes 101376 | tf_op jit(solution)/shard_map/all_gather | solution.py:404
  490.3 66.6 %while.180 = (s32[]{:T(128)}, f32[192,768]{1,0:T(8,128)S(1)}, f32[255,768]{1,0:T(8,128)S(1)}, f32[768,64]{0,1:T(8,128)}, s32[]{:T(128)}, /*index=5*/s32[]{:T(128)}, s32[]{:T(128)}, s32[]{:T(128)}) while((s32[]{:T(128)}, f32[192,768]{1,0:T(8,128)S(1)}, f32[255,768]{1,0:T(8,128)S(1)}, f32[768,64]{0,1:T(8,128)}, s32[]{:T(128)}, ...), condition=%wide.region_3.4_spmd.clone, body=%wide.region_2.3_spmd.clone.sunk | while | flops 442375 | bytes 1778845 | solution.py:122
  676.0 154.2 %while.181 = (s32[]{:T(128)}, f32[768,64]{1,0:T(8,128)S(1)}, f32[768,64]{1,0:T(8,128)S(1)}, f32[6,768,64]{2,0,1:T(8,128)}, f32[6,768,64]{2,0,1:T(8,128)}, /*inde...) while((s32[]{:T(128)}, f32[768,64]{1,0:T(8,128)S(1)}, ...), condition=%wide.region_6.7_spmd.clone, body=%wide.region_5.6_spmd.clone.sunk | while | flops 491523 | bytes 3539087 | solution.py:194
  851.1 79.6 %fusion.155 = f32[768,6,32]{2,1,0:T(8,128)S(1)} fusion(f32[32]{0:T(128)S(1)} %get-tuple-element.1803, f32[32]{0:T(128)S(1)} %get-tuple-element.1804, f32[768,64]{1,0:T(8,128)} %copy-done.118, f32[768,64]{1,0:T(8,128)} %copy-done.114, f32[768,64]{1,0:T(8,128)S(1)} %copy-done.64, f32[768,64]{1,0:T(8,128)S(1)} %copy-done.71, ...), kind=kOutput, calls=%fused_computation.243 | convolution fusion | flops 126320640 | bytes 1769776 | tf_op jit(solution)/shard_map/tcn,bcn->btc/dot_general | solution.py:215
  930.8 79.2 %subtract_bitcast_fusion = f32[6,32,768]{1,0,2:T(8,128)} fusion(f32[768,6,32]{2,1,0:T(8,128)S(1)} %fusion.155, f32[32]{0:T(128)S(1)} %get-tuple-element.1803, f32[32]{0:T(128)S(1)} %get-tuple-element.1804, f32[768,64]{1,0:T(8,128)S(1)} %copy-done.119, f32[768,64]{1,0:T(8,128)S(1)} %copy-done.115, f32[768,64]{1,0:T(8,128)S(1)} %copy-done.64, ...), kind=kOutput, calls=%fused_computation.288 | convolution fusion | flops 126468096 | bytes 2359600 | tf_op jit(solution)/shard_map/tcn,bcn->btc/dot_general | solution.py:215
  1035.4 66.5 %fusion.156 = f32[768,6,32]{2,1,0:T(8,128)S(1)} fusion(f32[6,768,64]{2,0,1:T(8,128)S(1)} %copy-done.176, f32[32]{0:T(128)S(1)} %get-tuple-element.1803, f32[32]{0:T(128)S(1)} %get-tuple-element.1804, f32[768,64]{1,0:T(8,128)S(1)} %copy-done.120, f32[768,64]{1,0:T(8,128)S(1)} %copy-done.116, f32[768,64]{1,0:T(8,128)S(1)} %copy-done.65, ...), kind=kOutput, calls=%fused_computation.244 | convolution fusion | flops 124256256 | bytes 2556160 | tf_op jit(solution)/shard_map/tcn,bcn->btc/dot_general | solution.py:198
  1101.9 67.8 %add_bitcast_fusion.1 = f32[6,32,768]{1,0,2:T(8,128)} fusion(f32[768,6,32]{2,1,0:T(8,128)S(1)} %fusion.134, f32[768,6,32]{2,1,0:T(8,128)S(1)} %fusion.156, f32[6,768,64]{2,0,1:T(8,128)S(1)} %copy-done.175, f32[32]{0:T(128)S(1)} %get-tuple-element.1803, f32[32]{0:T(128)S(1)} %get-tuple-element.1804, f32[768,64]{1,0:T(8,128)S(1)} %copy-done.120, ...), kind=kOutput, calls=%fused_computation.292 | convolution fusion | flops 124551168 | bytes 3735808 | tf_op jit(solution)/shard_map/tcn,bcn->btc/dot_general | solution.py:198
  1286.6 63.3 %all-gather.40.cloned.1.call-done = bf16[768,3072]{1,0:T(8,128)(2,1)} async-done(((bf16[24,3072]{1,0:T(8,128)(2,1)}), bf16[768,3072]{1,0:T(8,128)(2,1)}) %all-gather.40.cloned.1.call-update) | async-done | bytes 4718608 | tf_op jit(solution)/shard_map/all_gather | solution.py:414
  1354.8 60.4 %all-gather.42.cloned.1.call-done = bf16[3072,768]{1,0:T(8,128)(2,1)} async-done(((bf16[96,768]{1,0:T(8,128)(2,1)}), bf16[3072,768]{1,0:T(8,128)(2,1)}) %all-gather.42.cloned.1.call-update) | async-done | bytes 4718608 | tf_op jit(solution)/shard_map/all_gather | solution.py:415
  1625.9 59.8 %fusion.206 = f32[6,768,64]{2,0,1:T(8,128)S(1)} fusion(f32[768,6,32]{2,1,0:T(8,128)} %copy.176, f32[32]{0:T(128)S(1)} %copy-done.182, f32[32]{0:T(128)S(1)} %copy-done.185, f32[768,64]{1,0:T(8,128)} %copy-done.118, f32[768,64]{1,0:T(8,128)} %copy-done.114, f32[768,64]{1,0:T(8,128)} %copy-done.62, f32[768,64]{1,0:T(8,128)} %copy-done.69), kind=kOutput, calls=%fused_computation.311 | convolution fusion | flops 124256256 | bytes 2556160 | tf_op jit(solution)/shard_map/transpose(jvp(tcn,bcn->btc))/dot_general | solution.py:215
  1719.0 78.5 %fusion.181 = (f32[768,64]{1,0:T(8,128)}, f32[768,64]{1,0:T(8,128)}, f32[768,64]{1,0:T(8,128)}, f32[768,64]{1,0:T(8,128)S(1)}, f32[768,64]{1,0:T(8,128)S(1)}, /*...) fusion(f32[768,64]{1,0:T(8,128)S(1)} %copy-done.66, f32[6]{0:T(128)S(1)} %copy-done.171, ...), kind=kOutput, calls=%fused_computation.276 | convolution fusion | flops 133939200 | bytes 5505328 | tf_op jit(solution)/shard_map/transpose(jvp(tcn,bcn->btc))/dot_general | solution.py:215
  1914.6 63.7 %fusion.120 = f32[768,6,32]{2,1,0:T(8,128)S(1)} fusion(f32[32]{0:T(128)S(1)} %copy-done.178, f32[32]{0:T(128)S(1)} %copy-done.180, f32[768,64]{1,0:T(8,128)S(1)} %copy-done.67, f32[768,64]{1,0:T(8,128)} %copy-done.69, f32[768,64,6]{1,0,2:T(8,128)} %bitcast.613), kind=kOutput, calls=%fused_computation.209 | convolution fusion | flops 117964800 | bytes 2162944 | tf_op jit(solution)/shard_map/transpose(jvp(bsc,scn->bcn))/dot_general | solution.py:181
  2001.3 62.8 %add_bitcast_fusion = f32[6,32,768]{1,0,2:T(8,128)} fusion(f32[768,6,32]{2,1,0:T(8,128)S(1)} %copy-done.76, f32[768,6,32]{2,1,0:T(8,128)S(1)} %fusion.120, f32[32]{0:T(128)S(1)} %copy-done.178, f32[32]{0:T(128)S(1)} %copy-done.180, f32[768,64]{1,0:T(8,128)S(1)} %copy-done.67, f32[768,64]{1,0:T(8,128)S(1)} %copy-done.74, f32[768,64,6]{1,0,2:T(8,128)S(1)} %bitcast.594), kind=kOutput, calls=%fused_computation.283 | convolution fusion | flops 118259712 | bytes 3342592 | tf_op jit(solution)/shard_map/transpose(jvp(bsc,scn->bcn))/dot_general | solution.py:180
  2069.4 135.8 %while.176 = (s32[]{:T(128)}, f32[64,768]{1,0:T(8,128)S(1)}, s32[64]{0:T(128)S(1)}, f32[255,768]{1,0:T(8,128)S(1)}, f32[192,768]{1,0:T(8,128)S(1)}, /*index=5*/s32[]{:T(128)}, s32[1]{0:T(128)}, s32[]{:T(128)}, s32[1]{0:T(128)}) while((s32[]{:T(128)}, f32[64,768]{1,0:T(8,128)S(1)}, s32[64]{0:T(128)S(1)}, f32[255,768]{1,0:T(8,128)S(1)}, ...), condition=%wide.region_53.54_spmd, body=%wide.region_51.53_spmd.sunk | while | flops 294150 | bytes 1195175 | solution.py:147
  2206.4 232.0 %fusion.81 = (f32[768,64]{1,0:T(8,128)S(1)}, f32[768,64]{1,0:T(8,128)}, f32[768,64]{1,0:T(8,128)S(1)}, f32[768,64]{1,0:T(8,128)}, f32[768,64]{1,0:T(8,128)S(1)},...) fusion(f32[32]{0:T(128)S(1)} %copy-done.178, ...), kind=kOutput, calls=%fused_computation.145 | convolution fusion | flops 278888448 | bytes 38535808 | tf_op jit(solution)/shard_map/transpose(jvp(bsc,scn->bcn))/dot_general | solution.py:181
  2462.5 66.3 %while.184 = (s32[]{:T(128)}, f32[192,768]{1,0:T(8,128)S(1)}, f32[255,768]{1,0:T(8,128)S(1)}, f32[768,64]{0,1:T(8,128)}, s32[]{:T(128)}, /*index=5*/s32[]{:T(128)}) while((s32[]{:T(128)}, f32[192,768]{1,0:T(8,128)S(1)}, f32[255,768]{1,0:T(8,128)S(1)}, f32[768,64]{0,1:T(8,128)}, s32[]{:T(128)}, /*index=5*/s32[]{:T(128)}) %tuple.525), condition=%wide.region_43.44_spmd.clone, body=%wide.region_42.43_spmd.clone.sunk | while | flops 442371 | bytes 1778783 | solution.py:134
  2637.0 100.1 %reduce-scatter.64.cloned.1.call-done = f32[24,64]{1,0:T(8,128)} async-done(((f32[768,64]{1,0:T(8,128)}), f32[24,64]{1,0:T(8,128)}) %reduce-scatter.64.cloned.1.call-update) | async-done | bytes 6160
  2737.2 99.4 %reduce-scatter.62.cloned.1.call-done = f32[24,64]{1,0:T(8,128)} async-done(((f32[768,64]{1,0:T(8,128)}), f32[24,64]{1,0:T(8,128)}) %reduce-scatter.62.cloned.1.call-update) | async-done | bytes 6160
  2836.6 104.8 %reduce-scatter.46.cloned.1.call-done = f32[24,768]{1,0:T(8,128)} async-done(((f32[768,768]{1,0:T(8,128)}), f32[24,768]{1,0:T(8,128)}) %reduce-scatter.46.cloned.1.call-update) | async-done | bytes 73744 | tf_op jit(solution)/shard_map/reduce_scatter | solution.py:650
  2941.3 103.8 %reduce-scatter.38.cloned.1.call-done = f32[24,768]{1,0:T(8,128)} async-done(((f32[768,768]{1,0:T(8,128)}), f32[24,768]{1,0:T(8,128)}) %reduce-scatter.38.cloned.1.call-update) | async-done | bytes 73744 | tf_op jit(solution)/shard_map/reduce_scatter | solution.py:644
  3045.2 104.8 %reduce-scatter.32.cloned.1.call-done = f32[24,768]{1,0:T(8,128)} async-done(((f32[768,768]{1,0:T(8,128)}), f32[24,768]{1,0:T(8,128)}) %reduce-scatter.32.cloned.1.call-update) | async-done | bytes 73744 | tf_op jit(solution)/shard_map/reduce_scatter | solution.py:635
  3150.0 104.0 %reduce-scatter.36.cloned.1.call-done = f32[24,768]{1,0:T(8,128)} async-done(((f32[768,768]{1,0:T(8,128)}), f32[24,768]{1,0:T(8,128)}) %reduce-scatter.36.cloned.1.call-update) | async-done | bytes 73744 | tf_op jit(solution)/shard_map/reduce_scatter | solution.py:637
  3254.0 104.5 %reduce-scatter.34.cloned.1.call-done = f32[24,768]{1,0:T(8,128)} async-done(((f32[768,768]{1,0:T(8,128)}), f32[24,768]{1,0:T(8,128)}) %reduce-scatter.34.cloned.1.call-update) | async-done | bytes 73744 | tf_op jit(solution)/shard_map/reduce_scatter | solution.py:636
  3358.5 124.4 %reduce-scatter.44.cloned.1.call-done = f32[24,2304]{1,0:T(8,128)} async-done(((f32[768,2304]{1,0:T(8,128)}), f32[24,2304]{1,0:T(8,128)}) %reduce-scatter.44.cloned.1.call-update) | async-done | bytes 221200 | tf_op jit(solution)/shard_map/reduce_scatter | solution.py:649
  3482.9 142.1 %reduce-scatter.50.cloned.1.call-done = f32[96,768]{1,0:T(8,128)} async-done(((f32[3072,768]{1,0:T(8,128)}), f32[96,768]{1,0:T(8,128)}) %reduce-scatter.50.cloned.1.call-update) | async-done | bytes 294928 | tf_op jit(solution)/shard_map/reduce_scatter | solution.py:653
  3625.1 141.0 %reduce-scatter.48.cloned.1.call-done = f32[24,3072]{1,0:T(8,128)} async-done(((f32[768,3072]{1,0:T(8,128)}), f32[24,3072]{1,0:T(8,128)}) %reduce-scatter.48.cloned.1.call-update) | async-done | bytes 294928 | tf_op jit(solution)/shard_map/reduce_scatter | solution.py:652
  3766.0 142.1 %reduce-scatter.42.cloned.1.call-done = f32[96,768]{1,0:T(8,128)} async-done(((f32[3072,768]{1,0:T(8,128)}), f32[96,768]{1,0:T(8,128)}) %reduce-scatter.42.cloned.1.call-update) | async-done | bytes 294928 | tf_op jit(solution)/shard_map/reduce_scatter | solution.py:647
  3908.1 141.3 %reduce-scatter.40.cloned.1.call-done = f32[24,3072]{1,0:T(8,128)} async-done(((f32[768,3072]{1,0:T(8,128)}), f32[24,3072]{1,0:T(8,128)}) %reduce-scatter.40.cloned.1.call-update) | async-done | bytes 294928 | tf_op jit(solution)/shard_map/reduce_scatter | solution.py:646
  (1244 shorter events, 1363.6 us)
Async XLA Ops:
  7.2 478.1 %all-gather.22.cloned.1.call-start = ((), (), s32[]{:S(2)}) async-start(), calls=%async_computation.18 | async-start | bytes 1216512 | tf_op jit(solution)/shard_map/all_gather | solution.py:398
  7.9 549.1 %all-gather.24.cloned.1.call-start = ((), (), s32[]{:S(2)}) async-start(), calls=%async_computation.19 | async-start | bytes 1216512 | tf_op jit(solution)/shard_map/all_gather | solution.py:399
  8.7 1163.6 %all-gather.20.cloned.1.call-start = ((), (), s32[]{:S(2)}) async-start(), calls=%async_computation.17 | async-start | bytes 1216512 | tf_op jit(solution)/shard_map/all_gather | solution.py:397
  9.4 1165.6 %all-gather.26.cloned.1.call-start = ((), (), s32[]{:S(2)}) async-start(), calls=%async_computation.20 | async-start | bytes 1216512 | tf_op jit(solution)/shard_map/all_gather | solution.py:406
  10.0 1167.2 %all-gather.28.cloned.1.call-start = ((), (), s32[]{:S(2)}) async-start(), calls=%async_computation.21 | async-start | bytes 4866048 | tf_op jit(solution)/shard_map/all_gather | solution.py:408
  10.6 1170.2 %all-gather.30.cloned.1.call-start = ((), (), s32[]{:S(2)}) async-start(), calls=%async_computation.22 | async-start | bytes 4866048 | tf_op jit(solution)/shard_map/all_gather | solution.py:409
  11.1 1174.7 %all-gather.32.cloned.1.call-start = ((), (), s32[]{:S(2)}) async-start(), calls=%async_computation.23 | async-start | bytes 3649536 | tf_op jit(solution)/shard_map/all_gather | solution.py:411
  11.9 1195.7 %all-gather.36.cloned.1.call-start = ((), (), s32[]{:S(2)}) async-start(), calls=%async_computation.25 | async-start | bytes 1474560 | tf_op jit(solution)/shard_map/all_gather | solution.py:475
  61.5 1460.8 %copy-start.104 = (f32[768]{0:T(1024)}, f32[768]{0:T(1024)S(1)}, u32[]{:S(2)}) copy-start(f32[768]{0:T(1024)S(1)} %convert_element_type.287) | copy-start | bytes 9220
  487.1 3.2 collective-permute-start
  1189.7 37.5 all-gather.34.cloned.1.call-start
  1190.4 93.8 %all-gather.38.cloned.1.call-start = ((), (), s32[]{:S(2)}) async-start(), calls=%async_computation.26 | async-start | bytes 1216512 | tf_op jit(solution)/shard_map/all_gather | solution.py:412
  1191.0 158.9 %all-gather.40.cloned.1.call-start = ((), (), s32[]{:S(2)}) async-start(), calls=%async_computation.27 | async-start | bytes 4866048 | tf_op jit(solution)/shard_map/all_gather | solution.py:414
  1191.7 223.5 %all-gather.42.cloned.1.call-start = ((), (), s32[]{:S(2)}) async-start(), calls=%async_computation.28 | async-start | bytes 4866048 | tf_op jit(solution)/shard_map/all_gather | solution.py:415
  1192.3 292.1 %reduce-scatter.52.cloned.1.call-start = ((), (), s32[]{:S(2)}) async-start(), calls=%async_computation.39 | async-start | bytes 1474560
  1441.6 65.7 %reduce-scatter.54.cloned.1.call-start = ((), (), s32[]{:S(2)}) async-start(), calls=%async_computation.40 | async-start | bytes 1474560
  1465.9 1153.1 %reduce-scatter.56.cloned.1.call-start = ((), (), s32[]{:S(2)}) async-start(), calls=%async_computation.41 | async-start | bytes 405504
  2206.1 412.9 %reduce-scatter.60.cloned.1.call-start = ((), (), s32[]{:S(2)}) async-start(), calls=%async_computation.43 | async-start | bytes 405504
  2442.7 194.4 %reduce-scatter.58.cloned.1.call-start = ((), (), s32[]{:S(2)}) async-start(), calls=%async_computation.42 | async-start | bytes 405504
  2448.0 289.2 %reduce-scatter.64.cloned.1.call-start = ((), (), s32[]{:S(2)}) async-start(), calls=%async_computation.45 | async-start | bytes 405504
  2450.5 386.1 %reduce-scatter.62.cloned.1.call-start = ((), (), s32[]{:S(2)}) async-start(), calls=%async_computation.44 | async-start | bytes 405504
  2452.5 488.9 %reduce-scatter.46.cloned.1.call-start = ((), (), s32[]{:S(2)}) async-start(), calls=%async_computation.36 | async-start | bytes 2433024 | tf_op jit(solution)/shard_map/reduce_scatter | solution.py:650
  2454.7 590.5 %reduce-scatter.38.cloned.1.call-start = ((), (), s32[]{:S(2)}) async-start(), calls=%async_computation.32 | async-start | bytes 2433024 | tf_op jit(solution)/shard_map/reduce_scatter | solution.py:644
  2456.7 693.2 %reduce-scatter.32.cloned.1.call-start = ((), (), s32[]{:S(2)}) async-start(), calls=%async_computation.29 | async-start | bytes 2433024 | tf_op jit(solution)/shard_map/reduce_scatter | solution.py:635
  2458.9 795.0 %reduce-scatter.36.cloned.1.call-start = ((), (), s32[]{:S(2)}) async-start(), calls=%async_computation.31 | async-start | bytes 2433024 | tf_op jit(solution)/shard_map/reduce_scatter | solution.py:637
  2459.0 3.4 collective-permute-start.1
  2462.3 896.2 %reduce-scatter.34.cloned.1.call-start = ((), (), s32[]{:S(2)}) async-start(), calls=%async_computation.30 | async-start | bytes 2433024 | tf_op jit(solution)/shard_map/reduce_scatter | solution.py:636
  2530.9 952.0 %reduce-scatter.44.cloned.1.call-start = ((), (), s32[]{:S(2)}) async-start(), calls=%async_computation.35 | async-start | bytes 7299072 | tf_op jit(solution)/shard_map/reduce_scatter | solution.py:649
  2535.2 1089.9 %reduce-scatter.50.cloned.1.call-start = ((), (), s32[]{:S(2)}) async-start(), calls=%async_computation.38 | async-start | bytes 9732096 | tf_op jit(solution)/shard_map/reduce_scatter | solution.py:653
  2543.5 1222.5 %reduce-scatter.48.cloned.1.call-start = ((), (), s32[]{:S(2)}) async-start(), calls=%async_computation.37 | async-start | bytes 9732096 | tf_op jit(solution)/shard_map/reduce_scatter | solution.py:652
  2551.0 1357.1 %reduce-scatter.42.cloned.1.call-start = ((), (), s32[]{:S(2)}) async-start(), calls=%async_computation.34 | async-start | bytes 9732096 | tf_op jit(solution)/shard_map/reduce_scatter | solution.py:647
  2559.3 1490.1 %reduce-scatter.40.cloned.1.call-start = ((), (), s32[]{:S(2)}) async-start(), calls=%async_computation.33 | async-start | bytes 9732096 | tf_op jit(solution)/shard_map/reduce_scatter | solution.py:646
  (188 other events, 18507.9 us)
Sparse Core Ops, SparseCore 0:
  11.0 57.0 all-gather.21
  71.1 53.4 all-gather.23
  127.5 53.2 all-gather.19
  183.7 53.3 all-gather.25
  239.9 63.5 all-gather.27
  306.3 63.3 all-gather.29
  372.8 59.2 all-gather.31
  1189.8 17.7 all-gather.35
  1209.7 17.4 all-gather.33
  1230.1 54.1 all-gather.37
  1287.2 62.6 all-gather.39
  1352.7 62.4 all-gather.41
  1441.8 37.2 reduce-scatter.51
  1481.6 25.6 reduce-scatter.53
  2206.2 94.8 reduce-scatter.55
  2442.8 94.8 reduce-scatter.59
  2543.0 93.9 reduce-scatter.57
  2643.2 93.9 reduce-scatter.63
  2742.7 93.8 reduce-scatter.61
  2843.1 98.1 reduce-scatter.45
  2947.2 97.9 reduce-scatter.37
  3051.9 98.0 reduce-scatter.31
  3155.8 98.0 reduce-scatter.35
  3260.5 97.9 reduce-scatter.33
  3364.7 118.1 reduce-scatter.43
  3490.3 134.7 reduce-scatter.49
  3631.4 134.6 reduce-scatter.47
  3773.5 134.5 reduce-scatter.41
  3914.6 134.7 reduce-scatter.39
where the time goes:
time: 4080 us; the launch traced here: 4060 us
  waiting for transfers between devices  1660 us (41%)
  matrix products  1200 us (29%)
  blocking collectives  493 us (12%)
  local copies, waits for them, and re-layouts  402 us (10%)
  other arithmetic  184 us (5%)
  loops' own time  89.2 us (2%)
    dot_general x3, matrix products, local_ssm(): state_imag = jnp.einsum('bsc,scn->bcn', pieces, end_imag, precision=HIGHEST)  351 us
    unnamed x36, waiting for transfers between devices  246 us
    dot_general x3, matrix products, inject_ssm(): jnp.einsum('tcn,bcn->btc', out_real, start_real, precision=HIGHEST)  193 us
    dot_general x3, matrix products, inject_ssm(): jnp.einsum('tcn,bcn->btc', out_imag, start_imag, precision=HIGHEST)  172 us
    reduce_scatter x1, waiting for transfers between devices, shards(): lax.psum_scatter(grad_down_two, ('seq', 'dp'), scatter_dimension=0, tiled...  142 us
    reduce_scatter x1, waiting for transfers between devices, shards(): lax.psum_scatter(grad_down_one, ('seq', 'dp'), scatter_dimension=0, tiled...  142 us
    reduce_scatter x1, waiting for transfers between devices, shards(): lax.psum_scatter(grad_up_one, ('seq', 'dp'), scatter_dimension=0, tiled=T...  141 us
    reduce_scatter x1, waiting for transfers between devices, shards(): lax.psum_scatter(grad_up_two, ('seq', 'dp'), scatter_dimension=0, tiled=T...  141 us
  transfers between devices with their start and end apart: 31, of which 20 were waited for; matrix products, arithmetic and copies ran while one was open for 29% of the time, Pallas kernels for 0%

commit v1 on v0

v1 whole, which is shorter than its diff:
```python
from functools import partial

import jax
import jax.numpy as jnp
from jax import lax
from jax.experimental import pallas as pl
from jax.experimental.pallas import tpu as pltpu
from jax.sharding import PartitionSpec as P

HEADS = 12
HDIM = 64
EPSILON = 1e-05
HIGHEST = lax.Precision.HIGHEST
MASKED = -1e30
BOTH = ("seq", "dp")
MESH = pl.DeviceIdType.MESH
MIB = 1024 * 1024
F32 = jnp.float32
BF16 = jnp.bfloat16


def grouped(fast):
    return lax.axis_size("seq") == 4 and lax.axis_size("dp") == 8


def coordinates():
    seq, dp = lax.axis_index("seq"), lax.axis_index("dp")
    return seq // 2, seq % 2, dp // 2, dp % 2


def slot_of(y, c, z, x):
    return (y * 2 + c) * 8 + z * 2 + x


def device_of(y, c, z, x):
    return (y * 2 + c, z * 2 + x)


def greet(peers):
    barrier = pltpu.get_barrier_semaphore()
    for peer in peers:
        pl.semaphore_signal(barrier, inc=1, device_id=peer, device_id_type=MESH)
    pl.semaphore_wait(barrier, len(peers))


def six_peers(y, c, z, x):
    return [device_of(y, c, (z + k) % 4, x) for k in (1, 2, 3)] + [
        device_of(y, c, z, 1 - x),
        device_of(1 - y, c, z, x),
        device_of(y, 1 - c, z, x),
    ]


def gather_body(parts, count, *refs):
    sources, gathered = refs[:count], refs[count : 2 * count]
    local_sem, send_sem, recv_sem = refs[2 * count :]
    y, c, z, x = coordinates()
    greet(six_peers(y, c, z, x))
    me = slot_of(y, c, z, x)
    across_x = device_of(y, c, z, 1 - x)
    across_y = device_of(1 - y, c, z, x)
    other_core = device_of(y, 1 - c, z, x)
    own = [
        pltpu.make_async_copy(sources[i], gathered[i].at[me], local_sem.at[i])
        for i in range(count)
    ]
    for copy in own:
        copy.start()

    def place(p, slot):
        i, row, rows, column, columns, _ = parts[p]
        return gathered[i].at[slot, pl.ds(row, rows), pl.ds(column, columns)]

    def source(p):
        i, row, rows, column, columns, _ = parts[p]
        return sources[i].at[pl.ds(row, rows), pl.ds(column, columns)]

    def send(p, slot, target, first=False):
        pltpu.make_async_remote_copy(
            src_ref=source(p) if first else place(p, slot),
            dst_ref=place(p, slot),
            send_sem=send_sem.at[p],
            recv_sem=recv_sem.at[p, slot],
            device_id=target,
            device_id_type=MESH,
        ).start()

    def arrived(p, slot):
        pltpu.make_async_copy(place(p, slot), place(p, slot), recv_sem.at[p, slot]).wait()

    every = range(len(parts))
    for p in every:
        for k in (1, 3, 2):
            send(p, me, device_of(y, c, (z + k) % 4, x), True)
        send(p, me, across_x, True)
        send(p, me, across_y, True)
        send(p, me, other_core, True)

    def after_z(p):
        for k in (3, 1, 2):
            slot = slot_of(y, c, (z + k) % 4, x)
            arrived(p, slot)
            send(p, slot, across_x)
            send(p, slot, across_y)
            send(p, slot, other_core)

    def after_first(p):
        x_first = parts[p][5]
        for k in (0, 3, 1, 2):
            by_x = slot_of(y, c, (z + k) % 4, 1 - x)
            by_y = slot_of(1 - y, c, (z + k) % 4, x)
            arrived(p, by_x)
            if x_first:
                send(p, by_x, across_y)
            send(p, by_x, other_core)
            arrived(p, by_y)
            if not x_first:
                send(p, by_y, across_x)
            send(p, by_y, other_core)

    def after_second(p):
        for k in (0, 3, 1, 2):
            slot = slot_of(1 - y, c, (z + k) % 4, 1 - x)
            arrived(p, slot)
            send(p, slot, other_core)

    for p in range(len(parts) + 2):
        if p < len(parts):
            after_z(p)
        if 0 <= p - 1 < len(parts):
            after_first(p - 1)
        if 0 <= p - 2 < len(parts):
            after_second(p - 2)
    for p in every:
        for side in (0, 1):
            for zz in range(4):
                for xx in (0, 1):
                    arrived(p, slot_of(side, 1 - c, zz, xx))
    for copy in own:
        copy.wait()
    for p in every:
        i, row, rows, column, columns, _ = parts[p]
        sent = gathered[i].at[pl.ds(0, 31), pl.ds(row, rows), pl.ds(column, columns)]
        pltpu.make_async_copy(sent, sent, send_sem.at[p]).wait()


def cut(arrays):
    parts = []
    for i, (rows, columns) in enumerate(arrays):
        if columns > 1536:
            width = 1536 if columns % 1536 == 0 else 768
            pieces = [(0, rows, w, width) for w in range(0, columns, width)]
        elif rows > 48:
            pieces = [(r, 48, 0, columns) for r in range(0, rows, 48)]
        else:
            pieces = [(0, rows, 0, columns)]
        for piece in pieces:
            parts.append((i,) + piece + (len(parts) % 2 == 0,))
    return parts


def gather_all(arrays, collective_id):
    if not grouped(None):
        return [lax.all_gather(a, BOTH, axis=0) for a in arrays]
    count = len(arrays)
    parts = cut([a.shape for a in arrays])
    return pl.pallas_call(
        partial(gather_body, parts, count),
        out_shape=[jax.ShapeDtypeStruct((32,) + a.shape, a.dtype) for a in arrays],
        in_specs=[pl.BlockSpec(memory_space=pl.ANY)] * count,
        out_specs=[pl.BlockSpec(memory_space=pl.ANY)] * count,
        scratch_shapes=[
            pltpu.SemaphoreType.DMA((count,)),
            pltpu.SemaphoreType.DMA((len(parts),)),
            pltpu.SemaphoreType.DMA((len(parts), 32)),
        ],
        compiler_params=pltpu.CompilerParams(
            collective_id=collective_id, has_side_effects=True
        ),
    )(*arrays)


def reduce_body(parts, count, *refs):
    terms, totals = refs[:count], refs[count : 2 * count]
    buffers = refs[2 * count : 2 * count + 4 * len(parts)]
    send_sem, recv_sem = refs[2 * count + 4 * len(parts) :]
    y, c, z, x = coordinates()
    greet(six_peers(y, c, z, x))

    def term(p, core):
        i, row, rows, column, columns, _ = parts[p]
        return terms[i].at[:, core, :, :, pl.ds(row, rows), pl.ds(column, columns)]

    def copies(p, stage):
        one, two, three, four = buffers[4 * p : 4 * p + 4]
        x_last = parts[p][5]
        if stage == 0:
            pairs = [(term(p, 1 - c), one, device_of(y, 1 - c, z, x))]
        elif stage == 1 and x_last:
            pairs = [(one.at[1 - y], two, device_of(1 - y, c, z, x))]
        elif stage == 1:
            pairs = [(one.at[:, :, 1 - x], two, device_of(y, c, z, 1 - x))]
        elif stage == 2 and x_last:
            pairs = [(two.at[:, 1 - x], three, device_of(y, c, z, 1 - x))]
        elif stage == 2:
            pairs = [(two.at[1 - y], three, device_of(1 - y, c, z, x))]
        else:
            pairs = [
                (three.at[(z + k) % 4], four.at[k - 1], device_of(y, c, (z + k) % 4, x))
                for k in (1, 2, 3)
            ]
        return [
            pltpu.make_async_remote_copy(
                src_ref=src,
                dst_ref=dst,
                send_sem=send_sem.at[p, stage + n],
                recv_sem=recv_sem.at[p, stage + n],
                device_id=target,
                device_id_type=MESH,
            )
            for n, (src, dst, target) in enumerate(pairs)
        ]

    def add(p, stage):
        one, two, three, four = buffers[4 * p : 4 * p + 4]
        i, row, rows, column, columns, x_last = parts[p]
        total = lambda a, b: (a.astype(F32) + b.astype(F32)).astype(one.dtype)
        if stage == 0:

            def add_one(k, _):
                b, zz = k // 4, k % 4
                for xx in (0, 1):
                    mine = terms[i][b, c, zz, xx, pl.ds(row, rows), pl.ds(column, columns)]
                    one[b, zz, xx] = total(one[b, zz, xx], mine)
                return 0

            lax.fori_loop(0, 8, add_one, 0)
        elif stage == 1:

            def add_two(k, _):
                for h in (0, 1):
                    mine = one[y, k, h] if x_last else one[h, k, x]
                    if x_last:
                        two[k, h] = total(two[k, h], mine)
                    else:
                        two[h, k] = total(two[h, k], mine)
                return 0

            lax.fori_loop(0, 4, add_two, 0)
        elif stage == 2:

            def add_three(k, _):
                mine = two[k, x] if x_last else two[y, k]
                three[k] = total(three[k], mine)
                return 0

            lax.fori_loop(0, 4, add_three, 0)
        else:
            totals[i][pl.ds(row, rows), pl.ds(column, columns)] = (
                three[z].astype(F32)
                + four[0].astype(F32)
                + four[1].astype(F32)
                + four[2].astype(F32)
            )

    for p in range(len(parts)):
        for copy in copies(p, 0):
            copy.start()
    for step in range(len(parts) + 3):
        for stage in range(4):
            p = step - stage
            if 0 <= p < len(parts):
                for copy in copies(p, stage):
                    copy.wait_recv()
                add(p, stage)
                if stage < 3:
                    for copy in copies(p, stage + 1):
                        copy.start()
    for p in range(len(parts)):
        for stage in range(4):
            for copy in copies(p, stage):
                copy.wait_send()


def reduce_all(arrays, collective_id):
    if not grouped(None):
        return [
            lax.psum_scatter(a, BOTH, scatter_dimension=0, tiled=False).astype(F32)
            for a in arrays
        ]
    count = len(arrays)
    parts = cut([a.shape[1:] for a in arrays])
    scratch = []
    for i, _, rows, _, columns, x_last in parts:
        kind = arrays[i].dtype
        scratch += [
            pltpu.VMEM((2, 4, 2, rows, columns), kind),
            pltpu.VMEM(((4, 2) if x_last else (2, 4)) + (rows, columns), kind),
            pltpu.VMEM((4, rows, columns), kind),
            pltpu.VMEM((3, rows, columns), kind),
        ]
    return pl.pallas_call(
        partial(reduce_body, parts, count),
        out_shape=[jax.ShapeDtypeStruct(a.shape[1:], F32) for a in arrays],
        in_specs=[pl.BlockSpec(memory_space=pltpu.VMEM)] * count,
        out_specs=[pl.BlockSpec(memory_space=pltpu.VMEM)] * count,
        scratch_shapes=scratch
        + [
            pltpu.SemaphoreType.DMA((len(parts), 6)),
            pltpu.SemaphoreType.DMA((len(parts), 6)),
        ],
        compiler_params=pltpu.CompilerParams(
            collective_id=collective_id, has_side_effects=True, vmem_limit_bytes=58 * MIB
        ),
    )(*[a.reshape((2, 2, 4, 2) + a.shape[1:]) for a in arrays])


def swap_body(src, dst, local_sem, send_sem, recv_sem):
    rows, groups = lax.axis_size("seq"), lax.axis_size("dp")
    count = rows * groups
    me = lax.axis_index("seq") * groups + lax.axis_index("dp")
    others = [lax.rem(me + k, count) for k in range(1, count)]
    places = [(o // groups, lax.rem(o, groups)) for o in others]
    own = pltpu.make_async_copy(src.at[me], dst.at[me], local_sem)
    own.start()
    greet(places)
    for o, place in zip(others, places):
        pltpu.make_async_remote_copy(
            src_ref=src.at[o],
            dst_ref=dst.at[me],
            send_sem=send_sem,
            recv_sem=recv_sem,
            device_id=place,
            device_id_type=MESH,
        ).start()
    most = pl.ds(0, count - 1)
    pltpu.make_async_copy(src.at[most], dst.at[most], recv_sem).wait()
    pltpu.make_async_copy(src.at[most], dst.at[most], send_sem).wait()
    own.wait()


def swap_all(value, collective_id):
    if not grouped(None):
        return lax.all_to_all(value, BOTH, 0, 0, tiled=True)
    return pl.pallas_call(
        swap_body,
        out_shape=jax.ShapeDtypeStruct(value.shape, value.dtype),
        in_specs=[pl.BlockSpec(memory_space=pltpu.VMEM)],
        out_specs=pl.BlockSpec(memory_space=pltpu.VMEM),
        scratch_shapes=[pltpu.SemaphoreType.DMA(())] * 3,
        compiler_params=pltpu.CompilerParams(
            collective_id=collective_id, has_side_effects=True
        ),
    )(value)


def line_body(src, dst, local_sem, send_sem, recv_sem):
    y, c, z, x = coordinates()
    me, mate, far, last = y * 2 + c, y * 2 + 1 - c, (1 - y) * 2 + c, (1 - y) * 2 + 1 - c
    own = pltpu.make_async_copy(src, dst.at[me], local_sem)
    own.start()
    core, side = device_of(y, 1 - c, z, x), device_of(1 - y, c, z, x)
    greet([core, side])

    def copy(n, source, slot, target):
        return pltpu.make_async_remote_copy(
            src_ref=source,
            dst_ref=dst.at[slot],
            send_sem=send_sem.at[n],
            recv_sem=recv_sem.at[n],
            device_id=target,
            device_id_type=MESH,
        )

    first = copy(0, src, me, side)
    second = copy(1, src, me, core)
    third = copy(2, dst.at[far], far, core)
    first.start()
    second.start()
    first.wait_recv()
    third.start()
    second.wait_recv()
    third.wait_recv()
    for each in (first, second, third):
        each.wait_send()
    own.wait()


def gather_line(value, collective_id):
    if not grouped(None):
        return lax.all_gather(value, "seq", axis=0)
    return pl.pallas_call(
        line_body,
        out_shape=jax.ShapeDtypeStruct((4,) + value.shape, value.dtype),
        in_specs=[pl.BlockSpec(memory_space=pltpu.VMEM)],
        out_specs=pl.BlockSpec(memory_space=pltpu.VMEM),
        scratch_shapes=[
            pltpu.SemaphoreType.DMA(()),
            pltpu.SemaphoreType.DMA((3,)),
            pltpu.SemaphoreType.DMA((3,)),
        ],
        compiler_params=pltpu.CompilerParams(
            collective_id=collective_id, has_side_effects=True
        ),
    )(value)


def line_sum_body(src, dst, one, two, send_sem, recv_sem):
    y, c, z, x = coordinates()
    core, side = device_of(y, 1 - c, z, x), device_of(1 - y, c, z, x)
    greet([core, side])

    def copy(n, source, target, where):
        return pltpu.make_async_remote_copy(
            src_ref=source,
            dst_ref=where,
            send_sem=send_sem.at[n],
            recv_sem=recv_sem.at[n],
            device_id=target,
            device_id_type=MESH,
        )

    far = copy(0, src.at[1 - y, 1 - c], core, one.at[1 - y])
    near = copy(1, src.at[y, 1 - c], core, one.at[y])
    far.start()
    near.start()
    far.wait_recv()
    one[1 - y] = (one[1 - y].astype(F32) + src[1 - y, c].astype(F32)).astype(one.dtype)
    onward = copy(2, one.at[1 - y], side, two)
    onward.start()
    near.wait_recv()
    onward.wait_recv()
    dst[...] = (one[y].astype(F32) + src[y, c].astype(F32)) + two[...].astype(F32)
    for each in (far, near, onward):
        each.wait_send()


def sum_line(value, collective_id):
    if not grouped(None):
        return lax.psum_scatter(value, "seq", scatter_dimension=0).astype(F32)
    return pl.pallas_call(
        line_sum_body,
        out_shape=jax.ShapeDtypeStruct(value.shape[1:], F32),
        in_specs=[pl.BlockSpec(memory_space=pltpu.VMEM)],
        out_specs=pl.BlockSpec(memory_space=pltpu.VMEM),
        scratch_shapes=[
            pltpu.VMEM((2,) + value.shape[1:], value.dtype),
            pltpu.VMEM(value.shape[1:], value.dtype),
            pltpu.SemaphoreType.DMA((3,)),
            pltpu.SemaphoreType.DMA((3,)),
        ],
        compiler_params=pltpu.CompilerParams(
            collective_id=collective_id, has_side_effects=True, vmem_limit_bytes=32 * MIB
        ),
    )(value.reshape((2, 2) + value.shape[1:]))


def layer_norm(residual, scale_gain):
    average = jnp.mean(residual, axis=-1, keepdims=True)
    centered = residual - average
    variance = jnp.mean(centered * centered, axis=-1, keepdims=True)
    return centered * lax.rsqrt(variance + EPSILON) * scale_gain


def contract(left_side, right_side, left_dim, right_dim):
    return lax.dot_general(
        left_side,
        right_side,
        (((left_dim,), (right_dim,)), ((), ())),
        preferred_element_type=F32,
    )


def product(left_side, right_side):
    return contract(left_side, right_side, 1, 0)


def product_back(left_side, right_side):
    return contract(left_side, right_side, 1, 1)


def product_sum(left_side, right_side):
    return contract(left_side, right_side, 0, 0)


def feed_forward(residual, scale_gain, up_weight, down_weight):
    normed = layer_norm(residual, scale_gain).astype(BF16)
    pre_act = product(normed, up_weight)
    activated = jax.nn.gelu(pre_act).astype(BF16)
    return (residual + product(activated, down_weight), (normed, pre_act, activated))


def feed_back(residual, scale_gain, up_weight, down_weight, stored, grad_residual):
    normed, pre_act, activated = stored
    grad_branch = grad_residual.astype(BF16)
    grad_down = product_sum(activated, grad_branch)
    grad_activated = product_back(grad_branch, down_weight)
    gelu_pull = jax.vjp(jax.nn.gelu, pre_act)[1]
    grad_pre = gelu_pull(grad_activated)[0].astype(BF16)
    grad_up = product_sum(normed, grad_pre)
    grad_normed = product_back(grad_pre, up_weight)
    norm_pull = jax.vjp(layer_norm, residual, scale_gain)[1]
    grad_input, grad_gain = norm_pull(grad_normed)
    return (grad_residual + grad_input, grad_gain, grad_up, grad_down)


def ssm_kernel(decay_log, turn_angle, mix_real, mix_imag, length):
    rate = jnp.exp(decay_log)[:, :, None]
    angle = turn_angle[:, :, None]
    step = 32

    def powers(times):
        return (
            jnp.exp(-times * rate) * jnp.cos(times * angle),
            jnp.exp(-times * rate) * jnp.sin(times * angle),
        )

    low_real, low_imag = powers(jnp.arange(step, dtype=F32)[None, None])
    high_real, high_imag = powers(
        (step * jnp.arange(length // step, dtype=jnp.int32)).astype(F32)[None, None]
    )
    real, imag = mix_real[:, :, None], mix_imag[:, :, None]
    high = jnp.concatenate(
        [real * high_real - imag * high_imag, -(real * high_imag + imag * high_real)], axis=1
    )
    low = jnp.concatenate([low_real, low_imag], axis=1)
    kernel = jnp.einsum("cna,cnb->cab", high, low, precision=HIGHEST)
    return kernel.reshape(decay_log.shape[0], length)


def toeplitz(row, rows):
    spread = jnp.broadcast_to(row, (rows, row.shape[1]))
    return pltpu.roll(spread, 0, 1, stride=1, stride_axis=0)


def block_sum(mixed, blocks, groups, rows):
    total = mixed[:, :rows]
    for d in range(1, blocks):
        piece = mixed[: (blocks - d) * groups, d * rows : (d + 1) * rows]
        total = total + jnp.concatenate(
            [jnp.zeros((d * groups, rows), piece.dtype), piece], axis=0
        )
    return total


def block_spread(value, blocks, lags, groups, rows):
    pieces = [value]
    for d in range(1, lags):
        pieces.append(
            jnp.concatenate(
                [value[d * groups :], jnp.zeros((d * groups, rows), value.dtype)], axis=0
            )
        )
    return jnp.concatenate(pieces, axis=1)


def mixer_body(blocks, groups, rows, k_ref, v_ref, taps_ref, kernel_ref, skip_ref, shifted_ref, out_ref):
    channels = k_ref.shape[0]
    span = blocks * rows
    for ch in range(channels):
        taps = toeplitz(taps_ref[ch : ch + 1, :], rows)[:, : 2 * rows].astype(BF16)
        longer = toeplitz(kernel_ref[ch : ch + 1, :], rows)[:, :span].astype(BF16)
        near = product(k_ref[ch], taps)
        shifted = near[:, :rows] + jnp.concatenate(
            [jnp.zeros((groups, rows), F32), near[: (blocks - 1) * groups, rows:]], axis=0
        )
        signal = shifted * v_ref[ch].astype(F32)
        mixed = product(signal.astype(BF16), longer)
        total = block_sum(mixed, blocks, groups, rows)
        shifted_ref[ch] = shifted
        out_ref[ch] = (total + skip_ref[ch : ch + 1, :1] * signal).astype(BF16)


def mixer_back_body(
    blocks, groups, rows,
    grad_ref, k_ref, v_ref, shifted_ref, taps_ref, kernel_ref, skip_ref,
    grad_k_ref, grad_v_ref, kernel_grad_ref, taps_grad_ref, skip_grad_ref,
):
    channels = k_ref.shape[0]
    span = blocks * rows
    wide, narrow = kernel_ref.shape[1], taps_ref.shape[1]
    turned = (
        lax.broadcasted_iota(jnp.int32, (rows, rows), 0)
        + lax.broadcasted_iota(jnp.int32, (rows, rows), 1)
        == rows - 1
    ).astype(BF16)

    def lag_sums(earlier, spread, lanes):
        backward = product(earlier, turned).astype(BF16)
        pairs = product_sum(backward, spread)
        padded = jnp.concatenate(
            [pairs, jnp.zeros((rows, lanes - pairs.shape[1]), F32)], axis=1
        )
        return jnp.sum(
            pltpu.roll(padded, lanes - rows + 1, 1, stride=1, stride_axis=0),
            axis=0,
            keepdims=True,
        )

    for ch in range(channels):
        taps = toeplitz(taps_ref[ch : ch + 1, :], rows)[:, : 2 * rows].astype(BF16)
        longer = toeplitz(kernel_ref[ch : ch + 1, :], rows)[:, :span].astype(BF16)
        out_grad = grad_ref[ch]
        skip = skip_ref[ch : ch + 1, :1]
        values = v_ref[ch].astype(F32)
        shifted = shifted_ref[ch]
        signal = shifted * values
        wide_grad = out_grad.astype(F32)
        later = block_spread(wide_grad, blocks, blocks, groups, rows).astype(BF16)
        signal_grad = product_back(later, longer) + skip * wide_grad
        kernel_grad_ref[ch : ch + 1, :] = lag_sums(signal.astype(BF16), later, wide)
        skip_grad_ref[ch : ch + 1, :] = jnp.broadcast_to(
            jnp.sum(jnp.sum(signal * wide_grad, axis=0, keepdims=True), axis=1, keepdims=True),
            (1, 128),
        )
        shifted_grad = values * signal_grad
        grad_v_ref[ch] = (shifted * signal_grad).astype(BF16)
        next_two = block_spread(shifted_grad, blocks, 2, groups, rows).astype(BF16)
        grad_k_ref[ch] = product_back(next_two, taps).astype(BF16)
        taps_grad_ref[ch : ch + 1, :] = lag_sums(k_ref[ch], next_two, narrow)


def allowed_keys(place, length, rows, keys):
    row_places = place * rows + lax.broadcasted_iota(jnp.int32, (rows, keys), 0)
    key_places = lax.broadcasted_iota(jnp.int32, (rows, keys), 1)
    return (key_places <= row_places) & (key_places < length)


def attend_body(where_ref, q_ref, kv_ref, out_ref, log_ref):
    rows, features = q_ref.shape
    keys = kv_ref.shape[0]
    allowed = allowed_keys(where_ref[0], where_ref[1], rows, keys)
    for head in range(HEADS):
        own = slice(head * HDIM, (head + 1) * HDIM)
        values = slice(features + head * HDIM, features + (head + 1) * HDIM)
        scores = product_back(q_ref[:, own], kv_ref[:, own]) * HDIM ** (-0.5)
        scores = jnp.where(allowed, scores, MASKED)
        most = jnp.max(scores, axis=1, keepdims=True)
        powers = jnp.exp(scores - most)
        total = jnp.sum(powers, axis=1, keepdims=True)
        weights = (powers * (1.0 / total)).astype(BF16)
        out_ref[:, own] = product(weights, kv_ref[:, values]).astype(BF16)
        log_ref[:, head : head + 1] = most + jnp.log(total)


def attend_back_body(where_ref, q_ref, kv_ref, log_ref, grad_ref, grad_q_ref, grad_kv_ref):
    rows, features = q_ref.shape
    keys = kv_ref.shape[0]
    allowed = allowed_keys(where_ref[0], where_ref[1], rows, keys)
    scale = HDIM ** (-0.5)
    for head in range(HEADS):
        own = slice(head * HDIM, (head + 1) * HDIM)
        values = slice(features + head * HDIM, features + (head + 1) * HDIM)
        queries, grads = q_ref[:, own], grad_ref[:, own]
        scores = product_back(queries, kv_ref[:, own]) * scale
        probs = jnp.where(allowed, jnp.exp(scores - log_ref[:, head : head + 1]), 0.0)
        prob_grad = product_back(grads, kv_ref[:, values])
        delta = jnp.sum(probs * prob_grad, axis=1, keepdims=True)
        grad_scores = (probs * (prob_grad - delta)).astype(BF16)
        grad_q_ref[:, own] = (product(grad_scores, kv_ref[:, own]) * scale).astype(BF16)
        grad_kv_ref[:, own] = (product_sum(grad_scores, queries) * scale).astype(BF16)
        grad_kv_ref[:, values] = product_sum(probs.astype(BF16), grads).astype(BF16)


def local_call(body, out_shape, *operands, scalars=0, limit=48):
    vmem = pl.BlockSpec(memory_space=pltpu.VMEM)
    smem = pl.BlockSpec(memory_space=pltpu.SMEM)
    return pl.pallas_call(
        body,
        out_shape=out_shape,
        in_specs=[smem] * scalars + [vmem] * (len(operands) - scalars),
        out_specs=jax.tree.map(lambda _: vmem, out_shape),
        compiler_params=pltpu.CompilerParams(vmem_limit_bytes=limit * MIB),
    )(*operands)


def shards(
    tokens, lengths, norm_one, query_one, key_one, value_one, shift_taps, decay_log,
    turn_angle, mix_real, mix_imag, skip_gain, out_one, norm_two, up_one, down_one,
    norm_three, qkv_weight, out_two, norm_four, up_two, down_two, cotangent,
):
    blocks, groups = lax.axis_size("seq"), lax.axis_size("dp")
    devices = blocks * groups
    rows, features = tokens.shape[1], tokens.shape[2]
    channels = features // devices
    place = lax.axis_index("seq")
    length = lengths[0]
    row_places = place * rows + jnp.arange(rows, dtype=jnp.int32)
    live_mask = (row_places < length).astype(F32)[:, None]
    live_lane = (row_places < length).astype(F32)[None, :]

    gains = jnp.stack([norm_one, norm_two, norm_three, norm_four]).astype(F32)
    gains = jnp.pad(gains, ((0, 4), (0, 128 - channels)))
    late_up, late_down = (
        lax.all_gather(up_two, BOTH, axis=0, tiled=True),
        lax.all_gather(down_two, BOTH, axis=0, tiled=True),
    )
    everything = gather_all(
        [gains, query_one, key_one, value_one, out_one, up_one, down_one, qkv_weight, out_two], 1
    )
    gains = everything[0][:, :4, :channels].transpose(1, 0, 2).reshape(4, features)
    gain_one, gain_two, gain_three, gain_four = gains[0], gains[1], gains[2], gains[3]
    query_all, key_all, value_all, out_one_all, up_one_all, down_one_all, qkv_all, out_two_all = [
        g.reshape((-1, g.shape[2])) for g in everything[1:]
    ]

    kernel, kernel_pull = jax.vjp(
        partial(ssm_kernel, length=rows * blocks),
        *[a.astype(F32) for a in (decay_log, turn_angle, mix_real, mix_imag)],
    )
    wide = -(-(blocks + 1) * rows // 128) * 128
    kernel_row = jnp.pad(kernel, ((0, 0), (0, wide - kernel.shape[1])))
    narrow = -(-3 * rows // 128) * 128
    tap_row = jnp.pad(
        shift_taps.astype(F32), ((0, 0), (0, narrow - shift_taps.shape[1]))
    )
    skip_row = jnp.broadcast_to(skip_gain.astype(F32)[:, None], (channels, 128))

    residual_zero = tokens[0].astype(F32)
    normed_one = layer_norm(residual_zero, gain_one).astype(BF16)
    queries = product(normed_one, query_all)
    keys = contract(key_all, normed_one, 0, 1).astype(BF16)
    values = (contract(value_all, normed_one, 0, 1) * live_lane).astype(BF16)

    def to_channels(pieces, collective_id):
        sent = jnp.stack([p.reshape(devices, channels, rows) for p in pieces], axis=1)
        came = swap_all(sent, collective_id)
        came = came.transpose(1, 2, 0, 3)
        return [came[n] for n in range(len(pieces))]

    def to_rows(pieces, collective_id):
        sent = jnp.stack([p.transpose(1, 0, 2) for p in pieces], axis=1)
        came = swap_all(sent, collective_id)
        return [came[:, n].reshape(features, rows) for n in range(len(pieces))]

    k_own, v_own = to_channels([keys, values], 2)
    per_channel = (channels, devices, rows)
    shifted, mixed = local_call(
        partial(mixer_body, blocks, groups, rows),
        [jax.ShapeDtypeStruct(per_channel, F32), jax.ShapeDtypeStruct(per_channel, BF16)],
        k_own, v_own, tap_row, kernel_row, skip_row,
    )
    (ssm_out,) = to_rows([mixed], 3)
    ssm_out = ssm_out.T.astype(F32)
    gated = (queries * ssm_out).astype(BF16)
    residual_one = residual_zero + product(gated, out_one_all)
    residual_two, stored_two = feed_forward(residual_one, gain_two, up_one_all, down_one_all)
    normed_three = layer_norm(residual_two, gain_three).astype(BF16)
    joint = product(normed_three, qkv_all).astype(BF16)
    att_q = joint[:, :features]
    kv = gather_line(joint[:, features:], 4).reshape(blocks * rows, 2 * features)
    where = jnp.stack([place.astype(jnp.int32), length])
    attended, log_total = local_call(
        attend_body,
        [jax.ShapeDtypeStruct((rows, features), BF16), jax.ShapeDtypeStruct((rows, 128), F32)],
        where, att_q, kv, scalars=1,
    )
    residual_three = residual_two + product(attended, out_two_all)
    residual_four, stored_four = feed_forward(residual_three, gain_four, late_up, late_down)
    activations = (live_mask * residual_four).astype(BF16)

    grad_four = live_mask * cotangent[0].astype(F32)
    grad_three, grad_norm_four, grad_up_two, grad_down_two = feed_back(
        residual_three, gain_four, late_up, late_down, stored_four, grad_four
    )
    grad_up_two = lax.psum_scatter(
        grad_up_two.astype(BF16), BOTH, scatter_dimension=0, tiled=True
    ).astype(F32)
    grad_down_two = lax.psum_scatter(
        grad_down_two.astype(BF16), BOTH, scatter_dimension=0, tiled=True
    ).astype(F32)
    branch_three = grad_three.astype(BF16)
    grad_out_two = product_sum(attended, branch_three)
    grad_attended = product_back(branch_three, out_two_all).astype(BF16)
    grad_q, grad_kv = local_call(
        attend_back_body,
        [
            jax.ShapeDtypeStruct((rows, features), BF16),
            jax.ShapeDtypeStruct((blocks * rows, 2 * features), BF16),
        ],
        where, att_q, kv, log_total, grad_attended, scalars=1,
    )
    grad_kv = sum_line(grad_kv.reshape(blocks, rows, 2 * features), 5)
    grad_joint = jnp.concatenate([grad_q, grad_kv.astype(BF16)], axis=1)
    grad_qkv_weight = product_sum(normed_three, grad_joint)
    grad_normed_three = product_back(grad_joint, qkv_all)
    grad_from_three, grad_norm_three = jax.vjp(layer_norm, residual_two, gain_three)[1](
        grad_normed_three
    )
    grad_two = grad_three + grad_from_three
    grad_one, grad_norm_two, grad_up_one, grad_down_one = feed_back(
        residual_one, gain_two, up_one_all, down_one_all, stored_two, grad_two
    )
    branch_one = grad_one.astype(BF16)
    grad_out_one = product_sum(gated, branch_one)
    gated_grad = product_back(branch_one, out_one_all)
    grad_queries = (gated_grad * ssm_out).astype(BF16)
    ssm_grad = (gated_grad * queries).T.astype(BF16)
    (grad_own,) = to_channels([ssm_grad], 6)
    grad_k_own, grad_v_own, kernel_grad, taps_grad, skip_grad = local_call(
        partial(mixer_back_body, blocks, groups, rows),
        [
            jax.ShapeDtypeStruct(per_channel, BF16),
            jax.ShapeDtypeStruct(per_channel, BF16),
            jax.ShapeDtypeStruct((channels, wide), F32),
            jax.ShapeDtypeStruct((channels, narrow), F32),
            jax.ShapeDtypeStruct((channels, 128), F32),
        ],
        grad_own, k_own, v_own, shifted, tap_row, kernel_row, skip_row,
    )
    grad_keys, grad_values = to_rows([grad_k_own, grad_v_own], 7)
    grad_values = (grad_values.astype(F32) * live_lane).astype(BF16)
    grad_decay_log, grad_turn_angle, grad_mix_real, grad_mix_imag = kernel_pull(
        kernel_grad[:, : rows * blocks]
    )
    grad_shift_taps = taps_grad[:, : shift_taps.shape[1]]
    grad_skip_gain = skip_grad[:, 0]

    grad_query_one = product_sum(normed_one, grad_queries)
    grad_key_one = contract(normed_one, grad_keys, 0, 1)
    grad_value_one = contract(normed_one, grad_values, 0, 1)
    grad_normed_one = (
        product_back(grad_queries, query_all)
        + contract(grad_keys, key_all, 0, 1)
        + contract(grad_values, value_all, 0, 1)
    )
    grad_from_one, grad_norm_one = jax.vjp(layer_norm, residual_zero, gain_one)[1](
        grad_normed_one
    )
    input_grad = grad_one + grad_from_one

    gain_grads = jnp.stack([grad_norm_one, grad_norm_two, grad_norm_three, grad_norm_four])
    gain_grads = gain_grads.reshape(4, devices, channels).transpose(1, 0, 2)
    gain_grads = jnp.pad(gain_grads, ((0, 0), (0, 4), (0, 128 - channels)))

    def owned(grad):
        return grad.astype(BF16).reshape(devices, -1, grad.shape[1])

    sums = reduce_all(
        [gain_grads]
        + [
            owned(g)
            for g in (
                grad_up_one, grad_down_one, grad_qkv_weight, grad_out_two, grad_out_one,
                grad_query_one, grad_key_one, grad_value_one,
            )
        ],
        8,
    )
    gain_grads, grad_up_one, grad_down_one, grad_qkv_weight, grad_out_two, grad_out_one = sums[:6]
    grad_query_one, grad_key_one, grad_value_one = sums[6:]
    gain_grads = gain_grads[:4, :channels]
    return (
        activations[None], input_grad[None],
        gain_grads[0], grad_query_one, grad_key_one, grad_value_one,
        grad_shift_taps, grad_decay_log, grad_turn_angle, grad_mix_real, grad_mix_imag,
        grad_skip_gain, grad_out_one,
        gain_grads[1], grad_up_one, grad_down_one,
        gain_grads[2], grad_qkv_weight, grad_out_two,
        gain_grads[3], grad_up_two, grad_down_two,
    )


def solution(mesh):
    row, vector = P(BOTH, None), P(BOTH)
    whole = P("dp", "seq", None)
    weights = (
        vector, row, row, row, row, row, row, row, row, vector, row,
        vector, row, row, vector, row, row, vector, row, row,
    )
    return jax.shard_map(
        shards,
        mesh=mesh,
        in_specs=(whole, P("dp")) + weights + (whole,),
        out_specs=(whole, whole) + weights,
        check_vma=False,
    )
```

time: 4080 us -> 574 us (0.14)
  waiting for transfers between devices: 1660 us -> 1.45 us
  matrix products: 1200 us -> 79.8 us
  blocking collectives: 493 us -> 0 us
  Pallas kernels: 0 us -> 410 us
  local copies, waits for them, and re-layouts: 402 us -> 29.4 us
  other arithmetic: 184 us -> 27.7 us
  loops' own time: 89.2 us -> 0 us
    reduce_scatter x10 -> x2, waiting for transfers between devices: 1210 us -> 0.01 us  [the longest x1 0.01 us: shards(): lax.psum_scatter(grad_down_two.astype(BF16), BOTH, scatter_dimension=0, t...]
    dot_general x56 -> x33, matrix products: 1200 us -> 79.8 us  [the longest x30 77.2 us: contract(): lax.dot_general(left_side, right_side, (((left_dim,), (right_dim,)), ((),...]
    pallas_call x0 -> x12, Pallas kernels: none -> 410 us  [the longest x1 126 us: reduce_all(): pl.pallas_call(partial(reduce_body, parts, count), out_shape=[jax.ShapeDt...]
    all_gather x12 -> x0, blocking collectives: 410 us -> none  [the longest x1 67.7 us: shards(): lax.all_gather(turn_angle, ('seq', 'dp'), axis=0, tiled=True)]
    unnamed x36 -> x4, waiting for transfers between devices: 246 us -> 1.41 us
    all_gather x12 -> x2, waiting for transfers between devices: 203 us -> 0.04 us  [the longest x1 0.02 us: shards(): lax.all_gather(up_two, BOTH, axis=0, tiled=True)]
    dynamic_slice x198 -> x0, local copies, waits for them, and re-layouts: 156 us -> none  [the longest x128 96.8 us: add_tap(): lax.dynamic_slice_in_dim(tap_gains, offset, 1, 1)[:, 0]]
    dynamic_update_slice x76 -> x0, local copies, waits for them, and re-layouts: 145 us -> none  [the longest x12 140 us: local_ssm(): lax.scan(carry_block, (nothing, nothing), (state_real, state_imag))]
  transfers between devices with their start and end apart: 31 -> 4, of which waited for: 20 -> 0; matrix products, arithmetic and copies ran while one was open for 29% -> 21% of each run, Pallas kernels for 0% -> 73%
where the time goes in v1:
time: 574 us; the launch traced here: 566 us
  Pallas kernels  410 us (71%)
  matrix products  79.8 us (14%)
  local copies, waits for them, and re-layouts  29.4 us (5%)
  other arithmetic  27.7 us (5%)
  between operations  16.4 us (3%)
    pallas_call x1, Pallas kernels, reduce_all(): pl.pallas_call(partial(reduce_body, parts, count), out_shape=[jax.ShapeDt...  126 us
    pallas_call x1, Pallas kernels, gather_all(): pl.pallas_call(partial(gather_body, parts, count), out_shape=[jax.ShapeDt...  108 us
    pallas_call x4, Pallas kernels, swap_all(): pl.pallas_call(swap_body, out_shape=jax.ShapeDtypeStruct(value.shape, val...  96.8 us
    dot_general x30, matrix products, contract(): lax.dot_general(left_side, right_side, (((left_dim,), (right_dim,)), ((),...  77.2 us
    pallas_call x4, Pallas kernels, local_call(): pl.pallas_call(body, out_shape=out_shape, in_specs=[smem] * scalars + [vm...  42.6 us
    pallas_call x1, Pallas kernels, gather_line(): pl.pallas_call(line_body, out_shape=jax.ShapeDtypeStruct((4,) + value.sha...  19.6 us
    pallas_call x1, Pallas kernels, sum_line(): pl.pallas_call(line_sum_body, out_shape=jax.ShapeDtypeStruct(value.shape[...  18 us
    unnamed x241, local copies, waits for them, and re-layouts  14.8 us
  transfers between devices with their start and end apart: 4, of which 0 were waited for; matrix products, arithmetic and copies ran while one was open for 21% of the time, Pallas kernels for 73%

profile of v1, /device:TPU:0, one launch (start us, length us, event | category | flops | bytes accessed | tf_op | source)
XLA Modules:
  0.0 565.7 jit_solution(2456785874014443163)
XLA Ops:
  17.5 107.8 %shard_map.390 = (f32[32,8,128]{2,1,0:T(8,128)}, bf16[32,24,768]{2,1,0:T(8,128)(2,1)}, bf16[32,24,768]{2,1,0:T(8,128)(2,1)}, bf16[32,24,768]{2,1,0:T(8,128)(2,1)...) custom-call(f32[8,128]{1,0:T(8,128)} %fusion.89.refs_0_, ...), custom_call_target="tpu_custom_call" | custom-call | tf_op jit(solution)/shard_map/pallas_call | solution.py:167
  130.9 35.7 %shard_map.391 = bf16[32,2,24,192]{3,2,1,0:T(8,128)(2,1)} custom-call(bf16[32,2,24,192]{3,2,1,0:T(8,128)(2,1)} %pad_maximum_fusion.1.src), custom_call_target="tpu_custom_call" | custom-call | tf_op jit(solution)/shard_map/pallas_call | solution.py:345
  168.3 6.0 %shard_map.392 = (f32[24,32,192]{2,1,0:T(8,128)S(1)}, bf16[24,32,192]{2,1,0:T(8,128)(2,1)S(1)}) custom-call(bf16[24,32,192]{2,1,0:T(8,128)(2,1)S(1)} %get-tuple-element.111.k_ref, bf16[24,32,192]{2,1,0:T(8,128)(2,1)S(1)} %get-tuple-element.110.v_ref, f32[24,640]{1,0:T(8,128)S(1)} %pad_convert_fusion.taps_ref, f32[24,1024]{1,0:T(8,128)S(1)} %pad.24.kernel_ref, ...), custom_call_target="tpu_custom_call" | custom-call | tf_op jit(solution)/shard_map/pallas_call | solution.py:668
  175.2 16.9 %shard_map.393 = bf16[32,1,24,192]{3,2,1,0:T(8,128)(2,1)} custom-call(bf16[32,1,24,192]{3,2,1,0:T(8,128)(2,1)} %bitcast.201), custom_call_target="tpu_custom_call" | custom-call | tf_op jit(solution)/shard_map/pallas_call | solution.py:345
  193.5 2.8 fusion.34
  197.2 3.6 fusion.104
  205.9 19.6 %shard_map.394 = bf16[4,192,1536]{2,1,0:T(8,128)(2,1)} custom-call(bf16[192,1536]{1,0:T(8,128)(2,1)} %slice.87.src), custom_call_target="tpu_custom_call" | custom-call | tf_op jit(solution)/shard_map/pallas_call | solution.py:392
  227.3 6.7 %shard_map.395 = (bf16[192,768]{1,0:T(8,128)(2,1)S(1)}, f32[192,128]{1,0:T(8,128)S(1)}) custom-call(s32[2]{0:T(128)S(1)} %pad_add_fusion.where_ref, bf16[192,768]{1,0:T(8,128)(2,1)S(1)} %slice.86.q_ref, bf16[768,1536]{1,0:T(8,128)(2,1)S(1)} %bitcast.173), custom_call_target="tpu_custom_call" | custom-call | tf_op jit(solution)/shard_map/pallas_call | solution.py:668
  234.0 1.9 fusion.117
  237.0 3.7 fusion.105
  242.2 4.2 convolution_convert_fusion.1
  247.0 5.5 fusion.13
  252.5 5.6 multiply_reduce_fusion
  261.4 10.9 %shard_map.396 = (bf16[192,768]{1,0:T(8,128)(2,1)S(1)}, bf16[768,1536]{1,0:T(8,128)(2,1)S(1)}) custom-call(s32[2]{0:T(128)S(1)} %pad_add_fusion.where_ref, bf16[192,768]{1,0:T(8,128)(2,1)S(1)} %slice.86.q_ref, bf16[768,1536]{1,0:T(8,128)(2,1)S(1)} %bitcast.174, f32[192,128]{1,0:T(8,128)S(1)} %get-tuple-element.62.log_ref, ...), custom_call_target="tpu_custom_call" | custom-call | tf_op jit(solution)/shard_map/pallas_call | solution.py:668
  272.3 18.0 %shard_map.397 = f32[192,1536]{1,0:T(8,128)S(1)} custom-call(bf16[2,2,192,1536]{3,2,1,0:T(8,128)(2,1)S(1)} %bitcast.175), custom_call_target="tpu_custom_call" | custom-call | tf_op jit(solution)/shard_map/pallas_call | solution.py:441
  293.9 2.5 fusion.6
  296.4 2.6 multiply_reduce_fusion.2
  306.2 19.7 %shard_map.398 = bf16[32,1,24,192]{3,2,1,0:T(8,128)(2,1)} custom-call(bf16[32,1,24,192]{3,2,1,0:T(8,128)(2,1)} %bitcast.202), custom_call_target="tpu_custom_call" | custom-call | tf_op jit(solution)/shard_map/pallas_call | solution.py:345
  327.0 19.1 %shard_map.399 = (bf16[24,32,192]{2,1,0:T(8,128)(2,1)S(1)}, bf16[24,32,192]{2,1,0:T(8,128)(2,1)S(1)}, f32[24,1024]{1,0:T(8,128)S(1)}, f32[24,640]{1,0:T(8,128)S(1)}, f32[24,128]{1,0:T(8,128)S(1)}) custom-call(bf16[24,32,192]{2,1,0:T(8,128)(2,1)S(1)} %bitcast.176, bf16[24,32,192]{2,1,0:T(8,128)(2,1)S(1)} %get-tuple-element.111.k_ref, ...), custom_call_target="tpu_custom_call" | custom-call | tf_op jit(solution)/shard_map/pallas_call | solution.py:668
  347.6 24.5 %shard_map.400 = bf16[32,2,24,192]{3,2,1,0:T(8,128)(2,1)} custom-call(bf16[32,2,24,192]{3,2,1,0:T(8,128)(2,1)} %pad_maximum_fusion.2.src), custom_call_target="tpu_custom_call" | custom-call | tf_op jit(solution)/shard_map/pallas_call | solution.py:345
  374.5 2.8 fusion.120
  377.3 5.0 convolution_convert_fusion.2
  384.2 2.1 convolution_add_fusion.1
  390.5 2.7 convolution_convert_fusion.8
  393.2 2.7 convolution_convert_fusion.6
  399.2 3.1 convolution_convert_fusion
  402.3 3.7 convolution_convert_fusion.4
  406.0 4.2 convolution_convert_fusion.3
  410.2 125.5 %shard_map.401 = (f32[8,128]{1,0:T(8,128)}, f32[24,3072]{1,0:T(8,128)}, f32[96,768]{1,0:T(8,128)}, f32[24,2304]{1,0:T(8,128)}, f32[24,768]{1,0:T(8,128)}, /*inde...) custom-call(f32[2,2,4,2,8,128]{5,4,3,2,1,0:T(8,128)} %bitcast.210, ...), custom_call_target="tpu_custom_call" | custom-call | tf_op jit(solution)/shard_map/pallas_call | solution.py:302
  536.7 1.9 fusion.52
  541.4 1.9 multiply_reduce_fusion.10
  545.6 4.7 fusion.17
  (355 shorter events, 71.8 us)
Async XLA Ops:
  7.2 229.8 %all-gather.3.cloned.1.call-start = ((), (), s32[]{:S(2)}) async-start(), calls=%async_computation.2 | async-start | bytes 4866048 | tf_op jit(solution)/shard_map/all_gather | solution.py:695
  8.0 118.9 %copy-start.2 = (bf16[1,192,768]{2,1,0:T(8,128)(2,1)S(1)}, bf16[1,192,768]{2,1,0:T(8,128)(2,1)}, u32[]{:S(2)}) copy-start(bf16[1,192,768]{2,1,0:T(8,128)(2,1)} %param.23) | copy-start | bytes 884740
  8.0 239.0 %all-gather.5.cloned.1.call-start = ((), (), s32[]{:S(2)}) async-start(), calls=%async_computation.3 | async-start | bytes 4866048 | tf_op jit(solution)/shard_map/all_gather | solution.py:696
  8.7 541.6 %reduce-scatter.5.cloned.1.call-start = ((), (), s32[]{:S(2)}) async-start(), calls=%async_computation.5 | async-start | bytes 4866048 | tf_op jit(solution)/shard_map/reduce_scatter | solution.py:769
  126.8 165.5 %copy-start.89 = (f32[192]{0:T(256)}, f32[192]{0:T(256)S(1)}, u32[]{:S(2)}) copy-start(f32[192]{0:T(256)S(1)} %compare_convert_fusion) | copy-start | bytes 2308
  127.0 66.5 %copy-start.68 = (f32[192]{0:T(256)}, f32[192]{0:T(256)S(1)}, u32[]{:S(2)}) copy-start(f32[192]{0:T(256)S(1)} %broadcast_multiply_fusion.3) | copy-start | bytes 2308
  127.2 66.2 %copy-start.77 = (f32[192]{0:T(256)}, f32[192]{0:T(256)S(1)}, u32[]{:S(2)}) copy-start(f32[192]{0:T(256)S(1)} %fusion.93) | copy-start | bytes 2308
  129.8 38.3 %copy-start.96 = (bf16[24,64]{1,0:T(8,128)(2,1)S(1)}, bf16[24,64]{1,0:T(8,128)(2,1)}, u32[]{:S(2)}) copy-start(bf16[24,64]{1,0:T(8,128)(2,1)} %param.29) | copy-start | bytes 9220
  130.9 37.3 %copy-start.109 = (bf16[24]{0:T(256)(128)(2,1)S(1)}, bf16[24]{0:T(256)(128)(2,1)}, u32[]{:S(2)}) copy-start(bf16[24]{0:T(256)(128)(2,1)} %param.34) | copy-start | bytes 148
  196.9 103.5 %copy-start.73 = (f32[192]{0:T(256)}, f32[192]{0:T(256)S(1)}, u32[]{:S(2)}) copy-start(f32[192]{0:T(256)S(1)} %broadcast_multiply_fusion.2) | copy-start | bytes 2308
  197.2 103.3 %copy-start.80 = (f32[192]{0:T(256)}, f32[192]{0:T(256)S(1)}, u32[]{:S(2)}) copy-start(f32[192]{0:T(256)S(1)} %fusion.94) | copy-start | bytes 2308
  202.6 89.5 %copy-start.84 = (f32[192]{0:T(256)}, f32[192]{0:T(256)S(1)}, u32[]{:S(2)}) copy-start(f32[192]{0:T(256)S(1)} %broadcast_multiply_fusion.1) | copy-start | bytes 2308
  202.8 89.2 %copy-start.86 = (f32[192]{0:T(256)}, f32[192]{0:T(256)S(1)}, u32[]{:S(2)}) copy-start(f32[192]{0:T(256)S(1)} %fusion.95) | copy-start | bytes 2308
  235.9 22.8 %copy-start.75 = (f32[192]{0:T(256)}, f32[192]{0:T(256)S(1)}, u32[]{:S(2)}) copy-start(f32[192]{0:T(256)S(1)} %broadcast_multiply_fusion) | copy-start | bytes 2308
  237.0 21.8 %copy-start.82 = (f32[192]{0:T(256)}, f32[192]{0:T(256)S(1)}, u32[]{:S(2)}) copy-start(f32[192]{0:T(256)S(1)} %fusion.96) | copy-start | bytes 2308
  246.5 305.5 %reduce-scatter.3.cloned.1.call-start = ((), (), s32[]{:S(2)}) async-start(), calls=%async_computation.4 | async-start | bytes 4866048 | tf_op jit(solution)/shard_map/reduce_scatter | solution.py:766
  272.3 18.1 %copy-start.8 = (f32[192,768]{1,0:T(8,128)S(1)}, f32[192,768]{1,0:T(8,128)}, u32[]{:S(2)}) copy-start(f32[192,768]{1,0:T(8,128)} %copy-done.7) | copy-start | bytes 1769476
  272.3 18.1 %copy-start.20 = (bf16[32,24,2304]{2,1,0:T(8,128)(2,1)S(1)}, bf16[32,24,2304]{2,1,0:T(8,128)(2,1)}, u32[]{:S(2)}) copy-start(bf16[32,24,2304]{2,1,0:T(8,128)(2,1)} %get-tuple-element.59) | copy-start | bytes 10616836
  346.5 28.1 %copy-start.51 = (bf16[192,768]{1,0:T(8,128)(2,1)S(1)}, bf16[192,768]{1,0:T(8,128)(2,1)}, u32[]{:S(2)}) copy-start(bf16[192,768]{1,0:T(8,128)(2,1)} %get-tuple-element.113) | copy-start | bytes 884740
  347.5 29.8 %copy-start.4 = (f32[192,768]{1,0:T(8,128)S(1)}, f32[192,768]{1,0:T(8,128)}, u32[]{:S(2)}) copy-start(f32[192,768]{1,0:T(8,128)} %copy-done.3) | copy-start | bytes 1769476
  347.5 29.8 %copy-start.76 = (f32[192]{0:T(256)S(1)}, f32[192]{0:T(256)}, u32[]{:S(2)}) copy-start(f32[192]{0:T(256)} %copy-done.75) | copy-start | bytes 2308
  347.5 29.8 %copy-start.83 = (f32[192]{0:T(256)S(1)}, f32[192]{0:T(256)}, u32[]{:S(2)}) copy-start(f32[192]{0:T(256)} %copy-done.82) | copy-start | bytes 2308
  410.2 125.7 %copy-start.22 = (f32[24,64,32]{1,2,0:T(8,128)S(1)}, f32[24,64,32]{1,2,0:T(8,128)}, u32[]{:S(2)}) copy-start(f32[24,64,32]{1,2,0:T(8,128)} %copy-done.21) | copy-start | bytes 589828
  410.2 125.7 %copy-start.24 = (f32[24,64,32]{1,2,0:T(8,128)S(1)}, f32[24,64,32]{1,2,0:T(8,128)}, u32[]{:S(2)}) copy-start(f32[24,64,32]{1,2,0:T(8,128)} %copy-done.23) | copy-start | bytes 589828
  410.2 125.7 %copy-start.36 = (f32[24,24,32]{2,1,0:T(8,128)S(1)}, f32[24,24,32]{2,1,0:T(8,128)}, u32[]{:S(2)}) copy-start(f32[24,24,32]{2,1,0:T(8,128)} %reshape.406) | copy-start | bytes 221188
  410.2 126.4 %copy-start.55 = (f32[24,64]{1,0:T(8,128)S(1)}, f32[24,64]{1,0:T(8,128)}, u32[]{:S(2)}) copy-start(f32[24,64]{1,0:T(8,128)} %copy-done.54) | copy-start | bytes 18436
  410.2 126.4 %copy-start.60 = (f32[24,64]{1,0:T(8,128)S(1)}, f32[24,64]{1,0:T(8,128)}, u32[]{:S(2)}) copy-start(f32[24,64]{1,0:T(8,128)} %copy-done.59) | copy-start | bytes 18436
  410.2 126.4 %copy-start.62 = (f32[24,64]{1,0:T(8,128)S(1)}, f32[24,64]{1,0:T(8,128)}, u32[]{:S(2)}) copy-start(f32[24,64]{1,0:T(8,128)} %copy-done.61) | copy-start | bytes 18436
  410.2 126.4 %copy-start.101 = (f32[24]{0:T(128)S(1)}, f32[24]{0:T(128)}, u32[]{:S(2)}) copy-start(f32[24]{0:T(128)} %copy-done.100) | copy-start | bytes 292
  410.2 126.4 %copy-start.103 = (f32[24]{0:T(128)S(1)}, f32[24]{0:T(128)}, u32[]{:S(2)}) copy-start(f32[24]{0:T(128)} %copy-done.102) | copy-start | bytes 292
  545.6 10.6 %copy-start.57 = (f32[24,3072]{1,0:T(8,128)S(1)}, f32[24,3072]{1,0:T(8,128)}, u32[]{:S(2)}) copy-start(f32[24,3072]{1,0:T(8,128)} %get-tuple-element.175) | copy-start | bytes 884740
  545.6 11.3 %copy-start.56 = (f32[96,768]{1,0:T(8,128)S(1)}, f32[96,768]{1,0:T(8,128)}, u32[]{:S(2)}) copy-start(f32[96,768]{1,0:T(8,128)} %get-tuple-element.176) | copy-start | bytes 884740
  (88 other events, 370.2 us)
Sparse Core Ops, SparseCore 0:
  11.1 82.2 all-gather.2
  96.3 73.6 all-gather.4
  246.6 113.3 reduce-scatter.4
  382.5 128.9 reduce-scatter.2

commit v2 on v1

--- a/solution.py
+++ b/solution.py
@@ -19,7 +19,7 @@
 BF16 = jnp.bfloat16
 
 
-def grouped(fast):
+def grouped():
     return lax.axis_size("seq") == 4 and lax.axis_size("dp") == 8
 
 
@@ -51,97 +51,112 @@
     ]
 
 
-def gather_body(parts, count, *refs):
-    sources, gathered = refs[:count], refs[count : 2 * count]
-    local_sem, send_sem, recv_sem = refs[2 * count :]
-    y, c, z, x = coordinates()
-    greet(six_peers(y, c, z, x))
-    me = slot_of(y, c, z, x)
-    across_x = device_of(y, c, z, 1 - x)
-    across_y = device_of(1 - y, c, z, x)
-    other_core = device_of(y, 1 - c, z, x)
-    own = [
-        pltpu.make_async_copy(sources[i], gathered[i].at[me], local_sem.at[i])
-        for i in range(count)
-    ]
-    for copy in own:
-        copy.start()
-
-    def place(p, slot):
-        i, row, rows, column, columns, _ = parts[p]
-        return gathered[i].at[slot, pl.ds(row, rows), pl.ds(column, columns)]
-
-    def source(p):
-        i, row, rows, column, columns, _ = parts[p]
-        return sources[i].at[pl.ds(row, rows), pl.ds(column, columns)]
-
-    def send(p, slot, target, first=False):
+class Gather:
+    def __init__(self, parts, sources, gathered, local_sem, send_sem, recv_sem, ahead=4):
+        self.parts, self.sources, self.gathered = parts, sources, gathered
+        self.send_sem, self.recv_sem, self.ahead = send_sem, recv_sem, ahead
+        self.y, self.c, self.z, self.x = y, c, z, x = coordinates()
+        self.me = slot_of(y, c, z, x)
+        self.across_x = device_of(y, c, z, 1 - x)
+        self.across_y = device_of(1 - y, c, z, x)
+        self.other_core = device_of(y, 1 - c, z, x)
+        self.own = [
+            pltpu.make_async_copy(sources[i], gathered[i].at[self.me], local_sem.at[i])
+            for i in range(len(sources))
+        ]
+        self.done = 0
+
+    def place(self, p, slot):
+        i, row, rows, column, columns, _ = self.parts[p]
+        return self.gathered[i].at[slot, pl.ds(row, rows), pl.ds(column, columns)]
+
+    def send(self, p, slot, target, first=False):
+        i, row, rows, column, columns, _ = self.parts[p]
+        source = self.sources[i].at[pl.ds(row, rows), pl.ds(column, columns)]
         pltpu.make_async_remote_copy(
-            src_ref=source(p) if first else place(p, slot),
-            dst_ref=place(p, slot),
-            send_sem=send_sem.at[p],
-            recv_sem=recv_sem.at[p, slot],
+            src_ref=source if first else self.place(p, slot),
+            dst_ref=self.place(p, slot),
+            send_sem=self.send_sem.at[p],
+            recv_sem=self.recv_sem.at[p, slot],
             device_id=target,
             device_id_type=MESH,
         ).start()
 
-    def arrived(p, slot):
-        pltpu.make_async_copy(place(p, slot), place(p, slot), recv_sem.at[p, slot]).wait()
-
-    every = range(len(parts))
-    for p in every:
+    def arrived(self, p, slot):
+        place = self.place(p, slot)
+        pltpu.make_async_copy(place, place, self.recv_sem.at[p, slot]).wait()
+
+    def first(self, p):
         for k in (1, 3, 2):
-            send(p, me, device_of(y, c, (z + k) % 4, x), True)
-        send(p, me, across_x, True)
-        send(p, me, across_y, True)
-        send(p, me, other_core, True)
-
-    def after_z(p):
+            self.send(p, self.me, device_of(self.y, self.c, (self.z + k) % 4, self.x), True)
+        self.send(p, self.me, self.across_x, True)
+        self.send(p, self.me, self.across_y, True)
+        self.send(p, self.me, self.other_core, True)
+
+    def start(self):
+        for copy in self.own:
+            copy.start()
+        for p in range(min(self.ahead, len(self.parts))):
+            self.first(p)
+
+    def after_z(self, p):
         for k in (3, 1, 2):
-            slot = slot_of(y, c, (z + k) % 4, x)
-            arrived(p, slot)
-            send(p, slot, across_x)
-            send(p, slot, across_y)
-            send(p, slot, other_core)
-
-    def after_first(p):
-        x_first = parts[p][5]
+            slot = slot_of(self.y, self.c, (self.z + k) % 4, self.x)
+            self.arrived(p, slot)
+            self.send(p, slot, self.across_x)
+            self.send(p, slot, self.across_y)
+            self.send(p, slot, self.other_core)
+
+    def after_first(self, p):
+        x_first = self.parts[p][5]
         for k in (0, 3, 1, 2):
-            by_x = slot_of(y, c, (z + k) % 4, 1 - x)
-            by_y = slot_of(1 - y, c, (z + k) % 4, x)
-            arrived(p, by_x)
+            by_x = slot_of(self.y, self.c, (self.z + k) % 4, 1 - self.x)
+            by_y = slot_of(1 - self.y, self.c, (self.z + k) % 4, self.x)
+            self.arrived(p, by_x)
             if x_first:
-                send(p, by_x, across_y)
-            send(p, by_x, other_core)
-            arrived(p, by_y)
+                self.send(p, by_x, self.across_y)
+            self.send(p, by_x, self.other_core)
+            self.arrived(p, by_y)
             if not x_first:
-                send(p, by_y, across_x)
-            send(p, by_y, other_core)
-
-    def after_second(p):
+                self.send(p, by_y, self.across_x)
+            self.send(p, by_y, self.other_core)
+
+    def after_second(self, p):
         for k in (0, 3, 1, 2):
-            slot = slot_of(1 - y, c, (z + k) % 4, 1 - x)
-            arrived(p, slot)
-            send(p, slot, other_core)
-
-    for p in range(len(parts) + 2):
-        if p < len(parts):
-            after_z(p)
-        if 0 <= p - 1 < len(parts):
-            after_first(p - 1)
-        if 0 <= p - 2 < len(parts):
-            after_second(p - 2)
-    for p in every:
+            slot = slot_of(1 - self.y, self.c, (self.z + k) % 4, 1 - self.x)
+            self.arrived(p, slot)
+            self.send(p, slot, self.other_core)
+
+    def whole(self, p):
         for side in (0, 1):
             for zz in range(4):
                 for xx in (0, 1):
-                    arrived(p, slot_of(side, 1 - c, zz, xx))
-    for copy in own:
-        copy.wait()
-    for p in every:
-        i, row, rows, column, columns, _ = parts[p]
-        sent = gathered[i].at[pl.ds(0, 31), pl.ds(row, rows), pl.ds(column, columns)]
-        pltpu.make_async_copy(sent, sent, send_sem.at[p]).wait()
+                    self.arrived(p, slot_of(side, 1 - self.c, zz, xx))
+
+    def steps(self):
+        return len(self.parts) + 3
+
+    def run(self, until):
+        while self.done < min(until, self.steps()):
+            s, count = self.done, len(self.parts)
+            if self.ahead <= s + self.ahead < count:
+                self.first(s + self.ahead)
+            for stage, act in enumerate(
+                (self.after_z, self.after_first, self.after_second, self.whole)
+            ):
+                if 0 <= s - stage < count:
+                    act(s - stage)
+            self.done += 1
+
+    def own_arrived(self, indices):
+        for i in indices:
+            self.own[i].wait()
+
+    def finish(self):
+        self.run(self.steps())
+        for p, (i, row, rows, column, columns, _) in enumerate(self.parts):
+            sent = self.gathered[i].at[pl.ds(0, 31), pl.ds(row, rows), pl.ds(column, columns)]
+            pltpu.make_async_copy(sent, sent, self.send_sem.at[p]).wait()
 
 
 def cut(arrays):
@@ -157,27 +172,6 @@
         for piece in pieces:
             parts.append((i,) + piece + (len(parts) % 2 == 0,))
     return parts
-
-
-def gather_all(arrays, collective_id):
-    if not grouped(None):
-        return [lax.all_gather(a, BOTH, axis=0) for a in arrays]
-    count = len(arrays)
-    parts = cut([a.shape for a in arrays])
-    return pl.pallas_call(
-        partial(gather_body, parts, count),
-        out_shape=[jax.ShapeDtypeStruct((32,) + a.shape, a.dtype) for a in arrays],
-        in_specs=[pl.BlockSpec(memory_space=pl.ANY)] * count,
-        out_specs=[pl.BlockSpec(memory_space=pl.ANY)] * count,
-        scratch_shapes=[
-            pltpu.SemaphoreType.DMA((count,)),
-            pltpu.SemaphoreType.DMA((len(parts),)),
-            pltpu.SemaphoreType.DMA((len(parts), 32)),
-        ],
-        compiler_params=pltpu.CompilerParams(
-            collective_id=collective_id, has_side_effects=True
-        ),
-    )(*arrays)
 
 
 def reduce_body(parts, count, *refs):
@@ -283,7 +277,7 @@
 
 
 def reduce_all(arrays, collective_id):
-    if not grouped(None):
+    if not grouped():
         return [
             lax.psum_scatter(a, BOTH, scatter_dimension=0, tiled=False).astype(F32)
             for a in arrays
@@ -315,39 +309,54 @@
     )(*[a.reshape((2, 2, 4, 2) + a.shape[1:]) for a in arrays])
 
 
-def swap_body(src, dst, local_sem, send_sem, recv_sem):
+def all_others():
     rows, groups = lax.axis_size("seq"), lax.axis_size("dp")
     count = rows * groups
     me = lax.axis_index("seq") * groups + lax.axis_index("dp")
     others = [lax.rem(me + k, count) for k in range(1, count)]
-    places = [(o // groups, lax.rem(o, groups)) for o in others]
-    own = pltpu.make_async_copy(src.at[me], dst.at[me], local_sem)
-    own.start()
-    greet(places)
-    for o, place in zip(others, places):
-        pltpu.make_async_remote_copy(
-            src_ref=src.at[o],
-            dst_ref=dst.at[me],
-            send_sem=send_sem,
-            recv_sem=recv_sem,
-            device_id=place,
-            device_id_type=MESH,
-        ).start()
-    most = pl.ds(0, count - 1)
-    pltpu.make_async_copy(src.at[most], dst.at[most], recv_sem).wait()
-    pltpu.make_async_copy(src.at[most], dst.at[most], send_sem).wait()
-    own.wait()
+    return me, others, [(o // groups, lax.rem(o, groups)) for o in others]
+
+
+class Swap:
+    def __init__(self, src, dst, send_sem, recv_sem):
+        self.src, self.dst, self.send_sem, self.recv_sem = src, dst, send_sem, recv_sem
+
+    def start(self):
+        me, others, places = all_others()
+        for o, place in zip(others, places):
+            pltpu.make_async_remote_copy(
+                src_ref=self.src.at[o],
+                dst_ref=self.dst.at[me],
+                send_sem=self.send_sem,
+                recv_sem=self.recv_sem,
+                device_id=place,
+                device_id_type=MESH,
+            ).start()
+
+    def wait(self):
+        most = pl.ds(0, self.src.shape[0] - 1)
+        me = all_others()[0]
+        pltpu.make_async_copy(self.src.at[most], self.dst.at[most], self.recv_sem).wait()
+        pltpu.make_async_copy(self.src.at[most], self.dst.at[most], self.send_sem).wait()
+        self.dst[me] = self.src[me]
+
+
+def swap_body(src, dst, send_sem, recv_sem):
+    greet(all_others()[2])
+    swap = Swap(src, dst, send_sem, recv_sem)
+    swap.start()
+    swap.wait()
 
 
 def swap_all(value, collective_id):
-    if not grouped(None):
+    if not grouped():
         return lax.all_to_all(value, BOTH, 0, 0, tiled=True)
     return pl.pallas_call(
         swap_body,
         out_shape=jax.ShapeDtypeStruct(value.shape, value.dtype),
         in_specs=[pl.BlockSpec(memory_space=pltpu.VMEM)],
         out_specs=pl.BlockSpec(memory_space=pltpu.VMEM),
-        scratch_shapes=[pltpu.SemaphoreType.DMA(())] * 3,
+        scratch_shapes=[pltpu.SemaphoreType.DMA(())] * 2,
         compiler_params=pltpu.CompilerParams(
             collective_id=collective_id, has_side_effects=True
         ),
@@ -387,7 +396,7 @@
 
 
 def gather_line(value, collective_id):
-    if not grouped(None):
+    if not grouped():
         return lax.all_gather(value, "seq", axis=0)
     return pl.pallas_call(
         line_body,
@@ -436,7 +445,7 @@
 
 
 def sum_line(value, collective_id):
-    if not grouped(None):
+    if not grouped():
         return lax.psum_scatter(value, "seq", scatter_dimension=0).astype(F32)
     return pl.pallas_call(
         line_sum_body,
@@ -554,21 +563,174 @@
     return jnp.concatenate(pieces, axis=1)
 
 
+def mix(blocks, groups, rows, keys, values, tap_row, kernel_row, skip):
+    span = blocks * rows
+    taps = toeplitz(tap_row, rows)[:, : 2 * rows].astype(BF16)
+    longer = toeplitz(kernel_row, rows)[:, :span].astype(BF16)
+    near = product(keys, taps)
+    shifted = near[:, :rows] + jnp.concatenate(
+        [jnp.zeros((groups, rows), F32), near[: (blocks - 1) * groups, rows:]], axis=0
+    )
+    signal = shifted * values.astype(F32)
+    mixed = product(signal.astype(BF16), longer)
+    return shifted, block_sum(mixed, blocks, groups, rows) + skip * signal
+
+
 def mixer_body(blocks, groups, rows, k_ref, v_ref, taps_ref, kernel_ref, skip_ref, shifted_ref, out_ref):
-    channels = k_ref.shape[0]
-    span = blocks * rows
+    for ch in range(k_ref.shape[0]):
+        row = slice(ch, ch + 1)
+        shifted_ref[ch], out = mix(
+            blocks, groups, rows, k_ref[ch], v_ref[ch],
+            taps_ref[row, :], kernel_ref[row, :], skip_ref[row, :1],
+        )
+        out_ref[ch] = out.astype(BF16)
+
+
+def flat_weight(ref):
+    wide = ref[...].astype(F32)
+    return wide.reshape(wide.shape[0] * wide.shape[1], wide.shape[2]).astype(BF16)
+
+
+def first_body(
+    parts, count, *refs,
+):
+    sources = refs[:count]
+    tokens, live, taps_ref, kernel_ref, skip_ref = refs[count : count + 5]
+    refs = refs[count + 5 :]
+    gathered = refs[:count]
+    (
+        residual_ref, standard_ref, inverse_ref, normed_ref, queries_ref, ssm_ref, gated_ref,
+        k_ref, v_ref, shifted_ref,
+    ) = refs[count : count + 10]
+    (
+        wide, sent_kv, came_kv, sent_y, came_y,
+        local_sem, send_sem, recv_sem, swap_sem,
+    ) = refs[count + 10 :]
+    gains, key_all, value_all, query_all, out_all = gathered[:5]
+    devices, channels = key_all.shape[0], key_all.shape[1]
+    rows, features = tokens.shape
+    blocks, groups = lax.axis_size("seq"), lax.axis_size("dp")
+    greet(all_others()[2])
+    gather = Gather(parts, sources, gathered, local_sem, send_sem, recv_sem)
+    gather.start()
+
+    turned = tokens[...].astype(F32).T
+    centered = turned - jnp.mean(turned, axis=0, keepdims=True)
+    inverse = lax.rsqrt(jnp.mean(centered * centered, axis=0, keepdims=True) + EPSILON)
+    inverse_ref[...] = jnp.broadcast_to(inverse, inverse_ref.shape)
+    standard_ref[...] = centered * inverse
+
+    gather.run(8)
+    gather.own_arrived(range(5))
+    gain = gains[...].reshape(features, 128)[:, :1]
+    normed_ref[...] = (standard_ref[...] * gain).astype(BF16)
+
+    def projected(weight):
+        return contract(flat_weight(weight), normed_ref[...], 0, 0)
+
+    wide[:, :channels, :] = projected(key_all).reshape(devices, channels, rows)
+    wide[:, channels:, :] = (projected(value_all) * live[...]).reshape(devices, channels, rows)
+    sent_kv[...] = wide[...].astype(BF16)
+    over = Swap(sent_kv, came_kv, swap_sem.at[0], swap_sem.at[1])
+    over.start()
+    queries_ref[...] = projected(query_all)
+    gather.run(11)
+    over.wait()
+    wide[...] = came_kv[...].astype(F32)
     for ch in range(channels):
-        taps = toeplitz(taps_ref[ch : ch + 1, :], rows)[:, : 2 * rows].astype(BF16)
-        longer = toeplitz(kernel_ref[ch : ch + 1, :], rows)[:, :span].astype(BF16)
-        near = product(k_ref[ch], taps)
-        shifted = near[:, :rows] + jnp.concatenate(
-            [jnp.zeros((groups, rows), F32), near[: (blocks - 1) * groups, rows:]], axis=0
+        row = slice(ch, ch + 1)
+        k_ref[ch] = wide[:, ch, :].astype(BF16)
+        v_ref[ch] = wide[:, channels + ch, :].astype(BF16)
+        shifted_ref[ch], out = mix(
+            blocks, groups, rows, k_ref[ch], v_ref[ch],
+            taps_ref[row, :], kernel_ref[row, :], skip_ref[row, :1],
         )
-        signal = shifted * v_ref[ch].astype(F32)
-        mixed = product(signal.astype(BF16), longer)
-        total = block_sum(mixed, blocks, groups, rows)
-        shifted_ref[ch] = shifted
-        out_ref[ch] = (total + skip_ref[ch : ch + 1, :1] * signal).astype(BF16)
+        wide[:, ch, :] = out
+        if ch == channels // 2:
+            gather.run(12)
+    sent_y[...] = wide[:, :channels, :].astype(BF16)
+    back = Swap(sent_y, came_y, swap_sem.at[2], swap_sem.at[3])
+    back.start()
+    gather.run(14)
+    back.wait()
+    ssm = came_y[...].astype(F32).reshape(features, rows)
+    ssm_ref[...] = ssm.astype(BF16)
+    gated_ref[...] = (queries_ref[...] * ssm).astype(BF16)
+    residual_ref[...] = tokens[...].astype(F32) + contract(
+        gated_ref[...], flat_weight(out_all), 0, 0
+    )
+    gather.own_arrived(range(5, count))
+    gather.finish()
+
+
+def first_layer(weights, tokens, live, tap_row, kernel_row, skip_row, collective_id):
+    count = len(weights)
+    blocks, groups = lax.axis_size("seq"), lax.axis_size("dp")
+    devices = blocks * groups
+    rows, features = tokens.shape
+    channels = features // devices
+    parts = cut([a.shape for a in weights])
+    vmem, anywhere = pl.BlockSpec(memory_space=pltpu.VMEM), pl.BlockSpec(memory_space=pl.ANY)
+    turned = (features, rows)
+    per_channel = (channels, devices, rows)
+    results = [
+        ((rows, features), F32), (turned, F32), ((8, rows), F32), (turned, BF16), (turned, F32),
+        (turned, BF16), (turned, BF16), (per_channel, BF16), (per_channel, BF16), (per_channel, F32),
+    ]
+    out = pl.pallas_call(
+        partial(first_body, parts, count),
+        out_shape=[jax.ShapeDtypeStruct((devices,) + a.shape, a.dtype) for a in weights]
+        + [jax.ShapeDtypeStruct(*r) for r in results],
+        in_specs=[anywhere] * count + [vmem] * 5,
+        out_specs=[vmem] * 5 + [anywhere] * (count - 5) + [vmem] * len(results),
+        scratch_shapes=[
+            pltpu.VMEM((devices, 2 * channels, rows), F32),
+            pltpu.VMEM((devices, 2 * channels, rows), BF16),
+            pltpu.VMEM((devices, 2 * channels, rows), BF16),
+            pltpu.VMEM((devices, channels, rows), BF16),
+            pltpu.VMEM((devices, channels, rows), BF16),
+            pltpu.SemaphoreType.DMA((count,)),
+            pltpu.SemaphoreType.DMA((len(parts),)),
+            pltpu.SemaphoreType.DMA((len(parts), devices)),
+            pltpu.SemaphoreType.DMA((4,)),
+        ],
+        compiler_params=pltpu.CompilerParams(
+            collective_id=collective_id, has_side_effects=True, vmem_limit_bytes=48 * MIB
+        ),
+    )(*weights, tokens, live, tap_row, kernel_row, skip_row)
+    return out[:count], out[count:]
+
+
+def first_layer_apart(weights, tokens, live, tap_row, kernel_row, skip_row):
+    blocks, groups = lax.axis_size("seq"), lax.axis_size("dp")
+    devices = blocks * groups
+    rows, features = tokens.shape
+    channels = features // devices
+    every = [lax.all_gather(a, BOTH, axis=0) for a in weights]
+    gain = every[0][:, :, 0].reshape(features, 1)
+    key_all, value_all, query_all, out_all = [a.reshape(features, -1) for a in every[1:5]]
+    turned = tokens.astype(F32).T
+    centered = turned - jnp.mean(turned, axis=0, keepdims=True)
+    inverse = lax.rsqrt(jnp.mean(centered * centered, axis=0, keepdims=True) + EPSILON)
+    standard = centered * inverse
+    normed = (standard * gain).astype(BF16)
+    queries = contract(query_all, normed, 0, 0)
+    keys = contract(key_all, normed, 0, 0).astype(BF16)
+    values = (contract(value_all, normed, 0, 0) * live).astype(BF16)
+    sent = jnp.stack([a.reshape(devices, channels, rows) for a in (keys, values)], axis=1)
+    k_own, v_own = lax.all_to_all(sent, BOTH, 0, 0, tiled=True).transpose(1, 2, 0, 3)
+    per_channel = (channels, devices, rows)
+    shifted, mixed = local_call(
+        partial(mixer_body, blocks, groups, rows),
+        [jax.ShapeDtypeStruct(per_channel, F32), jax.ShapeDtypeStruct(per_channel, BF16)],
+        k_own, v_own, tap_row, kernel_row, skip_row,
+    )
+    ssm = lax.all_to_all(mixed.transpose(1, 0, 2), BOTH, 0, 0, tiled=True)
+    ssm = ssm.reshape(features, rows)
+    gated = (queries * ssm.astype(F32)).astype(BF16)
+    residual = tokens.astype(F32) + contract(gated, out_all, 0, 0)
+    inverse = jnp.broadcast_to(inverse, (8, rows))
+    return every, [residual, standard, inverse, normed, queries, ssm, gated, k_own, v_own, shifted]
 
 
 def mixer_back_body(
@@ -689,21 +851,6 @@
     live_mask = (row_places < length).astype(F32)[:, None]
     live_lane = (row_places < length).astype(F32)[None, :]
 
-    gains = jnp.stack([norm_one, norm_two, norm_three, norm_four]).astype(F32)
-    gains = jnp.pad(gains, ((0, 4), (0, 128 - channels)))
-    late_up, late_down = (
-        lax.all_gather(up_two, BOTH, axis=0, tiled=True),
-        lax.all_gather(down_two, BOTH, axis=0, tiled=True),
-    )
-    everything = gather_all(
-        [gains, query_one, key_one, value_one, out_one, up_one, down_one, qkv_weight, out_two], 1
-    )
-    gains = everything[0][:, :4, :channels].transpose(1, 0, 2).reshape(4, features)
-    gain_one, gain_two, gain_three, gain_four = gains[0], gains[1], gains[2], gains[3]
-    query_all, key_all, value_all, out_one_all, up_one_all, down_one_all, qkv_all, out_two_all = [
-        g.reshape((-1, g.shape[2])) for g in everything[1:]
-    ]
-
     kernel, kernel_pull = jax.vjp(
         partial(ssm_kernel, length=rows * blocks),
         *[a.astype(F32) for a in (decay_log, turn_angle, mix_real, mix_imag)],
@@ -716,11 +863,26 @@
     )
     skip_row = jnp.broadcast_to(skip_gain.astype(F32)[:, None], (channels, 128))
 
+    gains = jnp.stack([norm_one, norm_two, norm_three, norm_four], axis=1).astype(F32)
+    gains = jnp.pad(gains, ((0, 0), (0, 124)))
+    weights = [
+        gains, key_one, value_one, query_one, out_one, up_one, down_one, qkv_weight, out_two,
+        up_two, down_two,
+    ]
+    mixer_rows = (tap_row, kernel_row, skip_row)
+    if grouped():
+        every, kept = first_layer(weights, tokens[0], live_lane, *mixer_rows, 1)
+    else:
+        every, kept = first_layer_apart(weights, tokens[0], live_lane, *mixer_rows)
+    residual_one, standard, inverse, normed_turned, queries, ssm_out, gated, k_own, v_own, shifted = kept
+    gain_one, gain_two, gain_three, gain_four = [
+        every[0][:, :, n].reshape(features) for n in range(4)
+    ]
+    (
+        key_all, value_all, query_all, out_one_all, up_one_all, down_one_all, qkv_all,
+        out_two_all, late_up, late_down,
+    ) = [g.reshape((-1, g.shape[2])) for g in every[1:]]
     residual_zero = tokens[0].astype(F32)
-    normed_one = layer_norm(residual_zero, gain_one).astype(BF16)
-    queries = product(normed_one, query_all)
-    keys = contract(key_all, normed_one, 0, 1).astype(BF16)
-    values = (contract(value_all, normed_one, 0, 1) * live_lane).astype(BF16)
 
     def to_channels(pieces, collective_id):
         sent = jnp.stack([p.reshape(devices, channels, rows) for p in pieces], axis=1)
@@ -733,17 +895,7 @@
         came = swap_all(sent, collective_id)
         return [came[:, n].reshape(features, rows) for n in range(len(pieces))]
 
-    k_own, v_own = to_channels([keys, values], 2)
     per_channel = (channels, devices, rows)
-    shifted, mixed = local_call(
-        partial(mixer_body, blocks, groups, rows),
-        [jax.ShapeDtypeStruct(per_channel, F32), jax.ShapeDtypeStruct(per_channel, BF16)],
-        k_own, v_own, tap_row, kernel_row, skip_row,
-    )
-    (ssm_out,) = to_rows([mixed], 3)
-    ssm_out = ssm_out.T.astype(F32)
-    gated = (queries * ssm_out).astype(BF16)
-    residual_one = residual_zero + product(gated, out_one_all)
     residual_two, stored_two = feed_forward(residual_one, gain_two, up_one_all, down_one_all)
     normed_three = layer_norm(residual_two, gain_three).astype(BF16)
     joint = product(normed_three, qkv_all).astype(BF16)
@@ -792,10 +944,10 @@
         residual_one, gain_two, up_one_all, down_one_all, stored_two, grad_two
     )
     branch_one = grad_one.astype(BF16)
-    grad_out_one = product_sum(gated, branch_one)
-    gated_grad = product_back(branch_one, out_one_all)
-    grad_queries = (gated_grad * ssm_out).astype(BF16)
-    ssm_grad = (gated_grad * queries).T.astype(BF16)
+    grad_out_one = product(gated, branch_one)
+    gated_grad = contract(out_one_all, branch_one, 1, 1)
+    grad_queries = (gated_grad * ssm_out.astype(F32)).astype(BF16)
+    ssm_grad = (gated_grad * queries).astype(BF16)
     (grad_own,) = to_channels([ssm_grad], 6)
     grad_k_own, grad_v_own, kernel_grad, taps_grad, skip_grad = local_call(
         partial(mixer_back_body, blocks, groups, rows),
@@ -816,11 +968,11 @@
     grad_shift_taps = taps_grad[:, : shift_taps.shape[1]]
     grad_skip_gain = skip_grad[:, 0]
 
-    grad_query_one = product_sum(normed_one, grad_queries)
-    grad_key_one = contract(normed_one, grad_keys, 0, 1)
-    grad_value_one = contract(normed_one, grad_values, 0, 1)
+    grad_query_one = contract(normed_turned, grad_queries, 1, 1)
+    grad_key_one = contract(normed_turned, grad_keys, 1, 1)
+    grad_value_one = contract(normed_turned, grad_values, 1, 1)
     grad_normed_one = (
-        product_back(grad_queries, query_all)
+        contract(grad_queries, query_all, 0, 1)
         + contract(grad_keys, key_all, 0, 1)
         + contract(grad_values, value_all, 0, 1)
     )

time: 574 us -> 532 us (0.927)
  Pallas kernels: 410 us -> 384 us
    pallas_call x4 -> x2, Pallas kernels: 96.8 us -> 41.9 us  [swap_all(): pl.pallas_call(swap_body, out_shape=jax.ShapeDtypeStruct(value.shape, val...]
    pallas_call x1, Pallas kernels: 108 us -> 150 us  [first_layer(): pl.pallas_call(partial(first_body, parts, count), out_shape=[jax.ShapeDty...]
    pallas_call x1, Pallas kernels: 126 us -> 116 us  [reduce_all(): pl.pallas_call(partial(reduce_body, parts, count), out_shape=[jax.ShapeDt...]
    pallas_call x4 -> x3, Pallas kernels: 42.6 us -> 37 us  [local_call(): pl.pallas_call(body, out_shape=out_shape, in_specs=[smem] * scalars + [vm...]
    dot_general x30 -> x26, matrix products: 77.2 us -> 72.2 us  [contract(): lax.dot_general(left_side, right_side, (((left_dim,), (right_dim,)), ((),...]
    unnamed x241 -> x253, local copies, waits for them, and re-layouts: 14.8 us -> 17.2 us
  transfers between devices with their start and end apart: 4 -> 2, of which waited for: 0 -> 0; matrix products, arithmetic and copies ran while one was open for 21% -> 15% of each run, Pallas kernels for 73% -> 39%
where the time goes in v2:
time: 532 us; the launch traced here: 527 us
  Pallas kernels  384 us (72%)
  matrix products  74.8 us (14%)
  other arithmetic  26.5 us (5%)
  local copies, waits for them, and re-layouts  25 us (5%)
  between operations  16.8 us (3%)
    pallas_call x1, Pallas kernels, first_layer(): pl.pallas_call(partial(first_body, parts, count), out_shape=[jax.ShapeDty...  150 us
    pallas_call x1, Pallas kernels, reduce_all(): pl.pallas_call(partial(reduce_body, parts, count), out_shape=[jax.ShapeDt...  116 us
    dot_general x26, matrix products, contract(): lax.dot_general(left_side, right_side, (((left_dim,), (right_dim,)), ((),...  72.2 us
    pallas_call x2, Pallas kernels, swap_all(): pl.pallas_call(swap_body, out_shape=jax.ShapeDtypeStruct(value.shape, val...  41.9 us
    pallas_call x3, Pallas kernels, local_call(): pl.pallas_call(body, out_shape=out_shape, in_specs=[smem] * scalars + [vm...  37 us
    pallas_call x1, Pallas kernels, gather_line(): pl.pallas_call(line_body, out_shape=jax.ShapeDtypeStruct((4,) + value.sha...  20.3 us
    pallas_call x1, Pallas kernels, sum_line(): pl.pallas_call(line_sum_body, out_shape=jax.ShapeDtypeStruct(value.shape[...  18 us
    unnamed x253, local copies, waits for them, and re-layouts  17.2 us
  transfers between devices with their start and end apart: 2, of which 0 were waited for; matrix products, arithmetic and copies ran while one was open for 15% of the time, Pallas kernels for 39%

profile of v2, /device:TPU:0, one launch (start us, length us, event | category | flops | bytes accessed | tf_op | source)
XLA Modules:
  0.0 527.3 jit_solution(7090040554697443241)
XLA Ops:
  16.6 150.4 %shard_map.390 = (f32[32,24,128]{2,1,0:T(8,128)S(1)}, bf16[32,24,768]{2,1,0:T(8,128)(2,1)}, bf16[32,24,768]{2,1,0:T(8,128)(2,1)}, bf16[32,24,768]{2,1,0:T(8,128)...) custom-call(f32[24,128]{1,0:T(8,128)S(1)} %pad_convert_fusion.1.refs, ...), custom_call_target="tpu_custom_call" | custom-call | tf_op jit(solution)/shard_map/pallas_call | solution.py:680
  168.7 3.5 fusion.83
  172.2 4.8 fusion.88
  179.4 20.3 %shard_map.391 = bf16[4,192,1536]{2,1,0:T(8,128)(2,1)} custom-call(bf16[192,1536]{1,0:T(8,128)(2,1)} %slice.66.src), custom_call_target="tpu_custom_call" | custom-call | tf_op jit(solution)/shard_map/pallas_call | solution.py:401
  199.7 1.7 copy-done
  201.4 6.7 %shard_map.392 = (bf16[192,768]{1,0:T(8,128)(2,1)S(1)}, f32[192,128]{1,0:T(8,128)S(1)}) custom-call(s32[2]{0:T(128)S(1)} %pad_add_fusion.where_ref, bf16[192,768]{1,0:T(8,128)(2,1)S(1)} %slice.65.q_ref, bf16[768,1536]{1,0:T(8,128)(2,1)S(1)} %bitcast.125), custom_call_target="tpu_custom_call" | custom-call | tf_op jit(solution)/shard_map/pallas_call | solution.py:830
  208.1 1.6 fusion.89
  210.5 3.5 fusion.84
  215.5 4.2 convolution_convert_fusion.1
  220.7 5.7 %fusion.13 = bf16[192,3072]{1,0:T(8,128)(2,1)S(1)} fusion(f32[192,3072]{1,0:T(8,128)} %copy-done.52, bf16[3072,768]{1,0:T(8,128)(2,1)} %bitcast.161, bf16[1,192,768]{2,1,0:T(8,128)(2,1)S(1)} %copy-done.65, f32[192]{0:T(256)} %copy-done.97), kind=kOutput, calls=%fused_computation.23 | convolution fusion | flops 918208512 | bytes 8553216 | tf_op jit(solution)/shard_map/dot_general | solution.py:475
  227.4 3.8 convolution_convert_fusion.2
  231.9 5.5 %multiply_reduce_fusion = (f32[768]{0:T(1024)}, f32[192]{0:T(256)S(1)}, f32[192,768]{1,0:T(8,128)S(1)}) fusion(f32[192,768]{1,0:T(8,128)} %copy-done.22, f32[192]{0:T(256)S(1)} %copy-done.93, f32[192]{0:T(256)S(1)} %copy-done.87, f32[768]{0:T(1024)S(1)} %mul.691, bf16[192,3072]{1,0:T(8,128)(2,1)} %copy-done.62, bf16[768,3072]{1,0:T(8,128)(2,1)} %bitcast.137), kind=kOutput, calls=%fused_computation.67 | convolution fusion | flops 907000896 | bytes 7086336 | tf_op jit(solution)/shard_map/dot_general | solution.py:475
  239.5 11.1 %shard_map.393 = (bf16[192,768]{1,0:T(8,128)(2,1)S(1)}, bf16[768,1536]{1,0:T(8,128)(2,1)S(1)}) custom-call(s32[2]{0:T(128)S(1)} %pad_add_fusion.where_ref, bf16[192,768]{1,0:T(8,128)(2,1)S(1)} %slice.65.q_ref, bf16[768,1536]{1,0:T(8,128)(2,1)S(1)} %bitcast.126, f32[192,128]{1,0:T(8,128)S(1)} %copy-done.16, ...), custom_call_target="tpu_custom_call" | custom-call | tf_op jit(solution)/shard_map/pallas_call | solution.py:830
  250.7 18.0 %shard_map.394 = f32[192,1536]{1,0:T(8,128)S(1)} custom-call(bf16[2,2,192,1536]{3,2,1,0:T(8,128)(2,1)S(1)} %bitcast.128), custom_call_target="tpu_custom_call" | custom-call | tf_op jit(solution)/shard_map/pallas_call | solution.py:450
  272.1 5.2 fusion.6
  277.4 1.9 multiply_reduce_fusion.2
  282.1 19.3 %shard_map.395 = bf16[32,1,24,192]{3,2,1,0:T(8,128)(2,1)} custom-call(bf16[32,1,24,192]{3,2,1,0:T(8,128)(2,1)} %bitcast.151), custom_call_target="tpu_custom_call" | custom-call | tf_op jit(solution)/shard_map/pallas_call | solution.py:354
  305.6 19.2 %shard_map.396 = (bf16[24,32,192]{2,1,0:T(8,128)(2,1)S(1)}, bf16[24,32,192]{2,1,0:T(8,128)(2,1)S(1)}, f32[24,1024]{1,0:T(8,128)S(1)}, f32[24,640]{1,0:T(8,128)S(1)}, f32[24,128]{1,0:T(8,128)S(1)}) custom-call(bf16[24,32,192]{2,1,0:T(8,128)(2,1)S(1)} %bitcast.129, bf16[24,32,192]{2,1,0:T(8,128)(2,1)S(1)} %copy-done.5, bf16[24,32,192]{2,1,0:T(8,128)(2,1)S(1)} %copy-done.7, ...), custom_call_target="tpu_custom_call" | custom-call | tf_op jit(solution)/shard_map/pallas_call | solution.py:830
  326.3 22.6 %shard_map.397 = bf16[32,2,24,192]{3,2,1,0:T(8,128)(2,1)} custom-call(bf16[32,2,24,192]{3,2,1,0:T(8,128)(2,1)} %pad_maximum_fusion.1.src), custom_call_target="tpu_custom_call" | custom-call | tf_op jit(solution)/shard_map/pallas_call | solution.py:354
  349.0 1.9 multiply_convert_fusion.2
  350.8 2.1 slice_convert_fusion
  354.8 2.3 fusion.81
  362.4 2.7 convolution_convert_fusion.7
  369.7 3.1 convolution_convert_fusion
  372.8 3.7 convolution_convert_fusion.4
  376.5 4.3 convolution_convert_fusion.3
  380.8 116.2 %shard_map.398 = (f32[8,128]{1,0:T(8,128)}, f32[24,3072]{1,0:T(8,128)}, f32[96,768]{1,0:T(8,128)}, f32[24,2304]{1,0:T(8,128)}, f32[24,768]{1,0:T(8,128)}, /*inde...) custom-call(f32[2,2,4,2,8,128]{5,4,3,2,1,0:T(8,128)} %bitcast.156, ...), custom_call_target="tpu_custom_call" | custom-call | tf_op jit(solution)/shard_map/pallas_call | solution.py:296
  497.9 1.9 fusion.46
  502.7 1.9 multiply_reduce_fusion.10
  506.9 4.7 fusion.16
  511.5 1.7 convert_element_type.236
  513.2 1.6 convert_element_type.233
  (345 shorter events, 53.5 us)
Async XLA Ops:
  7.2 9.3 %copy-start.2 = (bf16[1,192,768]{2,1,0:T(8,128)(2,1)S(1)}, bf16[1,192,768]{2,1,0:T(8,128)(2,1)}, u32[]{:S(2)}) copy-start(bf16[1,192,768]{2,1,0:T(8,128)(2,1)} %param.23) | copy-start | bytes 884740
  7.2 9.3 %copy-start.13 = (bf16[96,768]{1,0:T(8,128)(2,1)S(1)}, bf16[96,768]{1,0:T(8,128)(2,1)}, u32[]{:S(2)}) copy-start(bf16[96,768]{1,0:T(8,128)(2,1)} %refs_10_.1) | copy-start | bytes 442372
  7.2 9.3 %copy-start.12 = (bf16[24,3072]{1,0:T(8,128)(2,1)S(1)}, bf16[24,3072]{1,0:T(8,128)(2,1)}, u32[]{:S(2)}) copy-start(bf16[24,3072]{1,0:T(8,128)(2,1)} %refs_9_.1) | copy-start | bytes 442372
  7.2 9.3 %copy-start.21 = (bf16[24,768]{1,0:T(8,128)(2,1)S(1)}, bf16[24,768]{1,0:T(8,128)(2,1)}, u32[]{:S(2)}) copy-start(bf16[24,768]{1,0:T(8,128)(2,1)} %refs_8_.1) | copy-start | bytes 110596
  7.2 9.3 %copy-start.14 = (bf16[24,2304]{1,0:T(8,128)(2,1)S(1)}, bf16[24,2304]{1,0:T(8,128)(2,1)}, u32[]{:S(2)}) copy-start(bf16[24,2304]{1,0:T(8,128)(2,1)} %refs_7_.1) | copy-start | bytes 331780
  7.2 9.3 %copy-start.11 = (bf16[96,768]{1,0:T(8,128)(2,1)S(1)}, bf16[96,768]{1,0:T(8,128)(2,1)}, u32[]{:S(2)}) copy-start(bf16[96,768]{1,0:T(8,128)(2,1)} %refs_6_.1) | copy-start | bytes 442372
  7.3 9.3 %copy-start.10 = (bf16[24,3072]{1,0:T(8,128)(2,1)S(1)}, bf16[24,3072]{1,0:T(8,128)(2,1)}, u32[]{:S(2)}) copy-start(bf16[24,3072]{1,0:T(8,128)(2,1)} %refs_5_.1) | copy-start | bytes 442372
  7.3 9.3 %copy-start.20 = (bf16[24,768]{1,0:T(8,128)(2,1)S(1)}, bf16[24,768]{1,0:T(8,128)(2,1)}, u32[]{:S(2)}) copy-start(bf16[24,768]{1,0:T(8,128)(2,1)} %refs_4_.1) | copy-start | bytes 110596
  7.3 9.3 %copy-start.18 = (bf16[24,768]{1,0:T(8,128)(2,1)S(1)}, bf16[24,768]{1,0:T(8,128)(2,1)}, u32[]{:S(2)}) copy-start(bf16[24,768]{1,0:T(8,128)(2,1)} %refs_2_.1) | copy-start | bytes 110596
  7.3 9.3 %copy-start.17 = (bf16[24,768]{1,0:T(8,128)(2,1)S(1)}, bf16[24,768]{1,0:T(8,128)(2,1)}, u32[]{:S(2)}) copy-start(bf16[24,768]{1,0:T(8,128)(2,1)} %refs_1_.1) | copy-start | bytes 110596
  7.3 9.3 %copy-start.19 = (bf16[24,768]{1,0:T(8,128)(2,1)S(1)}, bf16[24,768]{1,0:T(8,128)(2,1)}, u32[]{:S(2)}) copy-start(bf16[24,768]{1,0:T(8,128)(2,1)} %refs_3_.1) | copy-start | bytes 110596
  7.3 504.2 %reduce-scatter.5.cloned.1.call-start = ((), (), s32[]{:S(2)}) async-start(), calls=%async_computation.3 | async-start | bytes 4866048 | tf_op jit(solution)/shard_map/reduce_scatter | solution.py:921
  179.3 34.7 %copy-start.97 = (f32[192]{0:T(256)}, f32[192]{0:T(256)S(1)}, u32[]{:S(2)}) copy-start(f32[192]{0:T(256)S(1)} %compare_convert_fusion.1) | copy-start | bytes 2308
  219.8 293.5 %reduce-scatter.3.cloned.1.call-start = ((), (), s32[]{:S(2)}) async-start(), calls=%async_computation.2 | async-start | bytes 4866048 | tf_op jit(solution)/shard_map/reduce_scatter | solution.py:918
  250.7 18.2 %copy-start.27 = (f32[192,768]{1,0:T(8,128)S(1)}, f32[192,768]{1,0:T(8,128)}, u32[]{:S(2)}) copy-start(f32[192,768]{1,0:T(8,128)} %copy-done.26) | copy-start | bytes 1769476
  250.7 18.2 %copy-start.37 = (bf16[32,24,2304]{2,1,0:T(8,128)(2,1)S(1)}, bf16[32,24,2304]{2,1,0:T(8,128)(2,1)}, u32[]{:S(2)}) copy-start(bf16[32,24,2304]{2,1,0:T(8,128)(2,1)} %get-tuple-element.63) | copy-start | bytes 10616836
  250.7 18.2 %copy-start.95 = (f32[192]{0:T(256)S(1)}, f32[192]{0:T(256)}, u32[]{:S(2)}) copy-start(f32[192]{0:T(256)} %copy-done.94) | copy-start | bytes 2308
  250.7 18.2 %copy-start.101 = (f32[192]{0:T(256)S(1)}, f32[192]{0:T(256)}, u32[]{:S(2)}) copy-start(f32[192]{0:T(256)} %copy-done.100) | copy-start | bytes 2308
  324.9 24.1 %copy-start.99 = (f32[192]{0:T(256)S(1)}, f32[192]{0:T(256)}, u32[]{:S(2)}) copy-start(f32[192]{0:T(256)} %copy-done.97) | copy-start | bytes 2308
  326.3 26.6 %copy-start.82 = (f32[32,24]{1,0:T(8,128)S(1)}, f32[32,24]{1,0:T(8,128)}, u32[]{:S(2)}) copy-start(f32[32,24]{1,0:T(8,128)} %get-tuple-element.108) | copy-start | bytes 9220
  326.3 26.7 %copy-start.111 = (f32[768]{0:T(1024)S(1)}, f32[768]{0:T(1024)}, u32[]{:S(2)}) copy-start(f32[768]{0:T(1024)} %get-tuple-element.100) | copy-start | bytes 9220
  380.8 116.4 %copy-start.39 = (f32[24,64,32]{1,2,0:T(8,128)S(1)}, f32[24,64,32]{1,2,0:T(8,128)}, u32[]{:S(2)}) copy-start(f32[24,64,32]{1,2,0:T(8,128)} %copy-done.38) | copy-start | bytes 589828
  380.8 116.4 %copy-start.41 = (f32[24,64,32]{1,2,0:T(8,128)S(1)}, f32[24,64,32]{1,2,0:T(8,128)}, u32[]{:S(2)}) copy-start(f32[24,64,32]{1,2,0:T(8,128)} %copy-done.40) | copy-start | bytes 589828
  380.8 116.4 %copy-start.49 = (f32[24,24,32]{2,1,0:T(8,128)S(1)}, f32[24,24,32]{2,1,0:T(8,128)}, u32[]{:S(2)}) copy-start(f32[24,24,32]{2,1,0:T(8,128)} %reshape.313) | copy-start | bytes 221188
  380.8 117.1 %copy-start.74 = (f32[24,64]{1,0:T(8,128)S(1)}, f32[24,64]{1,0:T(8,128)}, u32[]{:S(2)}) copy-start(f32[24,64]{1,0:T(8,128)} %copy-done.73) | copy-start | bytes 18436
  380.8 117.1 %copy-start.76 = (f32[24,64]{1,0:T(8,128)S(1)}, f32[24,64]{1,0:T(8,128)}, u32[]{:S(2)}) copy-start(f32[24,64]{1,0:T(8,128)} %copy-done.75) | copy-start | bytes 18436
  380.8 117.1 %copy-start.115 = (f32[24]{0:T(128)S(1)}, f32[24]{0:T(128)}, u32[]{:S(2)}) copy-start(f32[24]{0:T(128)} %copy-done.114) | copy-start | bytes 292
  380.8 117.1 %copy-start.117 = (f32[24]{0:T(128)S(1)}, f32[24]{0:T(128)}, u32[]{:S(2)}) copy-start(f32[24]{0:T(128)} %copy-done.116) | copy-start | bytes 292
  506.8 9.3 %copy-start.79 = (f32[24,768]{1,0:T(8,128)S(1)}, f32[24,768]{1,0:T(8,128)}, u32[]{:S(2)}) copy-start(f32[24,768]{1,0:T(8,128)} %get-tuple-element.181) | copy-start | bytes 221188
  506.8 9.9 %copy-start.78 = (f32[24,768]{1,0:T(8,128)S(1)}, f32[24,768]{1,0:T(8,128)}, u32[]{:S(2)}) copy-start(f32[24,768]{1,0:T(8,128)} %get-tuple-element.188) | copy-start | bytes 221188
  506.9 10.6 %copy-start.71 = (f32[24,3072]{1,0:T(8,128)S(1)}, f32[24,3072]{1,0:T(8,128)}, u32[]{:S(2)}) copy-start(f32[24,3072]{1,0:T(8,128)} %get-tuple-element.190) | copy-start | bytes 884740
  506.9 11.3 %copy-start.70 = (f32[96,768]{1,0:T(8,128)S(1)}, f32[96,768]{1,0:T(8,128)}, u32[]{:S(2)}) copy-start(f32[96,768]{1,0:T(8,128)} %get-tuple-element.191) | copy-start | bytes 884740
  (92 other events, 354.0 us)
Sparse Core Ops, SparseCore 0:
  219.9 105.3 reduce-scatter.4
  331.7 112.8 reduce-scatter.2

commit v3 on v2

--- a/solution.py
+++ b/solution.py
@@ -15,6 +15,10 @@
 BOTH = ("seq", "dp")
 MESH = pl.DeviceIdType.MESH
 MIB = 1024 * 1024
+LAGS = (0, 2, 4, 6)
+PLACES = (5, 6, 7, 8, 11)
+RUNS = (8, 11, 12, 14)
+AHEAD = 4
 F32 = jnp.float32
 BF16 = jnp.bfloat16
 
@@ -52,9 +56,9 @@
 
 
 class Gather:
-    def __init__(self, parts, sources, gathered, local_sem, send_sem, recv_sem, ahead=4):
+    def __init__(self, parts, sources, gathered, local_sem, send_sem, recv_sem, ahead=None):
         self.parts, self.sources, self.gathered = parts, sources, gathered
-        self.send_sem, self.recv_sem, self.ahead = send_sem, recv_sem, ahead
+        self.send_sem, self.recv_sem, self.ahead = send_sem, recv_sem, ahead or AHEAD
         self.y, self.c, self.z, self.x = y, c, z, x = coordinates()
         self.me = slot_of(y, c, z, x)
         self.across_x = device_of(y, c, z, 1 - x)
@@ -174,30 +178,42 @@
     return parts
 
 
-def reduce_body(parts, count, *refs):
-    terms, totals = refs[:count], refs[count : 2 * count]
-    buffers = refs[2 * count : 2 * count + 4 * len(parts)]
-    send_sem, recv_sem = refs[2 * count + 4 * len(parts) :]
-    y, c, z, x = coordinates()
-    greet(six_peers(y, c, z, x))
-
-    def term(p, core):
-        i, row, rows, column, columns, _ = parts[p]
-        return terms[i].at[:, core, :, :, pl.ds(row, rows), pl.ds(column, columns)]
-
-    def copies(p, stage):
-        one, two, three, four = buffers[4 * p : 4 * p + 4]
-        x_last = parts[p][5]
+class Reduce:
+    def __init__(self, parts, terms, totals, buffers, mine, send_sem, recv_sem, mine_sem):
+        self.parts, self.terms, self.totals, self.buffers = parts, terms, totals, buffers
+        self.send_sem, self.recv_sem, self.mine_sem = send_sem, recv_sem, mine_sem
+        self.y, self.c, self.z, self.x = coordinates()
+        self.mine, self.kinds = mine, {}
+        for p, part in enumerate(parts):
+            if part[0] < len(mine[0]):
+                self.kinds.setdefault((part[2], part[4]), []).append(p)
+        self.done = 0
+
+    def term(self, p, core):
+        i, row, rows, column, columns, _ = self.parts[p]
+        return self.terms[i].at[:, core, :, :, pl.ds(row, rows), pl.ds(column, columns)]
+
+    def fetch(self, p):
+        kind = (self.parts[p][2], self.parts[p][4])
+        place = self.kinds[kind].index(p)
+        held = self.mine[1][kind].at[place % 2]
+        return pltpu.make_async_copy(self.term(p, self.c), held, self.mine_sem.at[p]), held
+
+    def copies(self, p, stage):
+        one, two, three, four = self.buffers[4 * p : 4 * p + 4]
+        y, c, z, x = self.y, self.c, self.z, self.x
+        across_x, across_y = device_of(y, c, z, 1 - x), device_of(1 - y, c, z, x)
+        x_last = self.parts[p][5]
         if stage == 0:
-            pairs = [(term(p, 1 - c), one, device_of(y, 1 - c, z, x))]
+            pairs = [(self.term(p, 1 - c), one, device_of(y, 1 - c, z, x))]
         elif stage == 1 and x_last:
-            pairs = [(one.at[1 - y], two, device_of(1 - y, c, z, x))]
+            pairs = [(one.at[1 - y], two, across_y)]
         elif stage == 1:
-            pairs = [(one.at[:, :, 1 - x], two, device_of(y, c, z, 1 - x))]
+            pairs = [(one.at[:, :, 1 - x], two, across_x)]
         elif stage == 2 and x_last:
-            pairs = [(two.at[:, 1 - x], three, device_of(y, c, z, 1 - x))]
+            pairs = [(two.at[:, 1 - x], three, across_x)]
         elif stage == 2:
-            pairs = [(two.at[1 - y], three, device_of(1 - y, c, z, x))]
+            pairs = [(two.at[1 - y], three, across_y)]
         else:
             pairs = [
                 (three.at[(z + k) % 4], four.at[k - 1], device_of(y, c, (z + k) % 4, x))
@@ -207,106 +223,100 @@
             pltpu.make_async_remote_copy(
                 src_ref=src,
                 dst_ref=dst,
-                send_sem=send_sem.at[p, stage + n],
-                recv_sem=recv_sem.at[p, stage + n],
+                send_sem=self.send_sem.at[p, stage + n],
+                recv_sem=self.recv_sem.at[p, stage + n],
                 device_id=target,
                 device_id_type=MESH,
             )
             for n, (src, dst, target) in enumerate(pairs)
         ]
 
-    def add(p, stage):
-        one, two, three, four = buffers[4 * p : 4 * p + 4]
-        i, row, rows, column, columns, x_last = parts[p]
-        total = lambda a, b: (a.astype(F32) + b.astype(F32)).astype(one.dtype)
+    def add(self, p, stage):
+        one, two, three, four = self.buffers[4 * p : 4 * p + 4]
+        y, c, z, x = self.y, self.c, self.z, self.x
+        i, row, rows, column, columns, x_last = self.parts[p]
+
+        def total(a, b):
+            return (a.astype(F32) + b.astype(F32)).astype(a.dtype)
+
         if stage == 0:
+            if i < len(self.mine[0]):
+                copy, held = self.fetch(p)
+                copy.wait()
+            else:
+                held = self.term(p, c)
 
             def add_one(k, _):
                 b, zz = k // 4, k % 4
                 for xx in (0, 1):
-                    mine = terms[i][b, c, zz, xx, pl.ds(row, rows), pl.ds(column, columns)]
-                    one[b, zz, xx] = total(one[b, zz, xx], mine)
+                    one[b, zz, xx] = total(one[b, zz, xx], held[b, zz, xx])
                 return 0
 
             lax.fori_loop(0, 8, add_one, 0)
+            if i < len(self.mine[0]):
+                same = self.kinds[(rows, columns)]
+                later = same.index(p) + 2
+                if later < len(same):
+                    self.fetch(same[later])[0].start()
         elif stage == 1:
 
             def add_two(k, _):
                 for h in (0, 1):
-                    mine = one[y, k, h] if x_last else one[h, k, x]
                     if x_last:
-                        two[k, h] = total(two[k, h], mine)
+                        two[k, h] = total(two[k, h], one[y, k, h])
                     else:
-                        two[h, k] = total(two[h, k], mine)
+                        two[h, k] = total(two[h, k], one[h, k, x])
                 return 0
 
             lax.fori_loop(0, 4, add_two, 0)
         elif stage == 2:
 
             def add_three(k, _):
-                mine = two[k, x] if x_last else two[y, k]
-                three[k] = total(three[k], mine)
+                three[k] = total(three[k], two[k, x] if x_last else two[y, k])
                 return 0
 
             lax.fori_loop(0, 4, add_three, 0)
         else:
-            totals[i][pl.ds(row, rows), pl.ds(column, columns)] = (
+            self.totals[i][pl.ds(row, rows), pl.ds(column, columns)] = (
                 three[z].astype(F32)
                 + four[0].astype(F32)
                 + four[1].astype(F32)
                 + four[2].astype(F32)
             )
 
-    for p in range(len(parts)):
-        for copy in copies(p, 0):
-            copy.start()
-    for step in range(len(parts) + 3):
-        for stage in range(4):
-            p = step - stage
-            if 0 <= p < len(parts):
-                for copy in copies(p, stage):
-                    copy.wait_recv()
-                add(p, stage)
-                if stage < 3:
-                    for copy in copies(p, stage + 1):
-                        copy.start()
-    for p in range(len(parts)):
-        for stage in range(4):
-            for copy in copies(p, stage):
-                copy.wait_send()
-
-
-def reduce_all(arrays, collective_id):
-    if not grouped():
-        return [
-            lax.psum_scatter(a, BOTH, scatter_dimension=0, tiled=False).astype(F32)
-            for a in arrays
-        ]
-    count = len(arrays)
-    parts = cut([a.shape[1:] for a in arrays])
-    scratch = []
-    for i, _, rows, _, columns, x_last in parts:
-        kind = arrays[i].dtype
-        scratch += [
-            pltpu.VMEM((2, 4, 2, rows, columns), kind),
-            pltpu.VMEM(((4, 2) if x_last else (2, 4)) + (rows, columns), kind),
-            pltpu.VMEM((4, rows, columns), kind),
-            pltpu.VMEM((3, rows, columns), kind),
-        ]
-    return pl.pallas_call(
-        partial(reduce_body, parts, count),
-        out_shape=[jax.ShapeDtypeStruct(a.shape[1:], F32) for a in arrays],
-        in_specs=[pl.BlockSpec(memory_space=pltpu.VMEM)] * count,
-        out_specs=[pl.BlockSpec(memory_space=pltpu.VMEM)] * count,
-        scratch_shapes=scratch
-        + [
-            pltpu.SemaphoreType.DMA((len(parts), 6)),
-            pltpu.SemaphoreType.DMA((len(parts), 6)),
-        ],
-        compiler_params=pltpu.CompilerParams(
-            collective_id=collective_id, has_side_effects=True, vmem_limit_bytes=58 * MIB
-        ),
-    )(*[a.reshape((2, 2, 4, 2) + a.shape[1:]) for a in arrays])
+    def start(self, arrays):
+        for p, part in enumerate(self.parts):
+            if part[0] in arrays:
+                for copy in self.copies(p, 0):
+                    copy.start()
+
+    def fetch_first(self):
+        for same in self.kinds.values():
+            for p in same[:2]:
+                self.fetch(p)[0].start()
+
+    def steps(self):
+        return len(self.parts) + LAGS[3]
+
+    def run(self, until):
+        while self.done < min(until, self.steps()):
+            for stage in range(4):
+                p = self.done - LAGS[stage]
+                if 0 <= p < len(self.parts):
+                    for copy in self.copies(p, stage):
+                        copy.wait_recv()
+                    self.add(p, stage)
+                    if stage < 3:
+                        for copy in self.copies(p, stage + 1):
+                            copy.start()
+            self.done += 1
+
+    def finish(self):
+        self.run(self.steps())
+        for p in range(len(self.parts)):
+            for stage in range(4):
+                for copy in self.copies(p, stage):
+                    copy.wait_send()
 
 
 def all_others():
@@ -339,28 +349,6 @@
         pltpu.make_async_copy(self.src.at[most], self.dst.at[most], self.recv_sem).wait()
         pltpu.make_async_copy(self.src.at[most], self.dst.at[most], self.send_sem).wait()
         self.dst[me] = self.src[me]
-
-
-def swap_body(src, dst, send_sem, recv_sem):
-    greet(all_others()[2])
-    swap = Swap(src, dst, send_sem, recv_sem)
-    swap.start()
-    swap.wait()
-
-
-def swap_all(value, collective_id):
-    if not grouped():
-        return lax.all_to_all(value, BOTH, 0, 0, tiled=True)
-    return pl.pallas_call(
-        swap_body,
-        out_shape=jax.ShapeDtypeStruct(value.shape, value.dtype),
-        in_specs=[pl.BlockSpec(memory_space=pltpu.VMEM)],
-        out_specs=pl.BlockSpec(memory_space=pltpu.VMEM),
-        scratch_shapes=[pltpu.SemaphoreType.DMA(())] * 2,
-        compiler_params=pltpu.CompilerParams(
-            collective_id=collective_id, has_side_effects=True
-        ),
-    )(value)
 
 
 def line_body(src, dst, local_sem, send_sem, recv_sem):
@@ -620,7 +608,7 @@
     inverse_ref[...] = jnp.broadcast_to(inverse, inverse_ref.shape)
     standard_ref[...] = centered * inverse
 
-    gather.run(8)
+    gather.run(RUNS[0])
     gather.own_arrived(range(5))
     gain = gains[...].reshape(features, 128)[:, :1]
     normed_ref[...] = (standard_ref[...] * gain).astype(BF16)
@@ -634,7 +622,7 @@
     over = Swap(sent_kv, came_kv, swap_sem.at[0], swap_sem.at[1])
     over.start()
     queries_ref[...] = projected(query_all)
-    gather.run(11)
+    gather.run(RUNS[1])
     over.wait()
     wide[...] = came_kv[...].astype(F32)
     for ch in range(channels):
@@ -647,11 +635,11 @@
         )
         wide[:, ch, :] = out
         if ch == channels // 2:
-            gather.run(12)
+            gather.run(RUNS[2])
     sent_y[...] = wide[:, :channels, :].astype(BF16)
     back = Swap(sent_y, came_y, swap_sem.at[2], swap_sem.at[3])
     back.start()
-    gather.run(14)
+    gather.run(RUNS[3])
     back.wait()
     ssm = came_y[...].astype(F32).reshape(features, rows)
     ssm_ref[...] = ssm.astype(BF16)
@@ -733,14 +721,10 @@
     return every, [residual, standard, inverse, normed, queries, ssm, gated, k_own, v_own, shifted]
 
 
-def mixer_back_body(
-    blocks, groups, rows,
-    grad_ref, k_ref, v_ref, shifted_ref, taps_ref, kernel_ref, skip_ref,
-    grad_k_ref, grad_v_ref, kernel_grad_ref, taps_grad_ref, skip_grad_ref,
+def mix_back(
+    blocks, groups, rows, out_grad, keys, values, shifted, tap_row, kernel_row, skip
 ):
-    channels = k_ref.shape[0]
     span = blocks * rows
-    wide, narrow = kernel_ref.shape[1], taps_ref.shape[1]
     turned = (
         lax.broadcasted_iota(jnp.int32, (rows, rows), 0)
         + lax.broadcasted_iota(jnp.int32, (rows, rows), 1)
@@ -759,27 +743,219 @@
             keepdims=True,
         )
 
+    taps = toeplitz(tap_row, rows)[:, : 2 * rows].astype(BF16)
+    longer = toeplitz(kernel_row, rows)[:, :span].astype(BF16)
+    values = values.astype(F32)
+    signal = shifted * values
+    later = block_spread(out_grad, blocks, blocks, groups, rows).astype(BF16)
+    signal_grad = product_back(later, longer) + skip * out_grad
+    kernel_grad = lag_sums(signal.astype(BF16), later, kernel_row.shape[1])
+    skip_grad = jnp.sum(jnp.sum(signal * out_grad, axis=0, keepdims=True), axis=1, keepdims=True)
+    shifted_grad = values * signal_grad
+    next_two = block_spread(shifted_grad, blocks, 2, groups, rows).astype(BF16)
+    return (
+        product_back(next_two, taps),
+        shifted * signal_grad,
+        kernel_grad,
+        lag_sums(keys, next_two, tap_row.shape[1]),
+        skip_grad,
+    )
+
+
+def mixer_back_body(
+    blocks, groups, rows,
+    grad_ref, k_ref, v_ref, shifted_ref, taps_ref, kernel_ref, skip_ref,
+    grad_k_ref, grad_v_ref, kernel_grad_ref, taps_grad_ref, skip_grad_ref,
+):
+    for ch in range(k_ref.shape[0]):
+        row = slice(ch, ch + 1)
+        grad_k, grad_v, kernel_grad_ref[row, :], taps_grad_ref[row, :], skip_grad = mix_back(
+            blocks, groups, rows, grad_ref[ch].astype(F32), k_ref[ch], v_ref[ch], shifted_ref[ch],
+            taps_ref[row, :], kernel_ref[row, :], skip_ref[row, :1],
+        )
+        grad_k_ref[ch], grad_v_ref[ch] = grad_k.astype(BF16), grad_v.astype(BF16)
+        skip_grad_ref[row, :] = jnp.broadcast_to(skip_grad, (1, 128))
+
+
+def last_body(parts, count, kinds, *refs):
+    early = refs[:count]
+    (
+        gain_in, branch, grad_one, live, gated, normed, queries, ssm, standard, inverse,
+        gains, key_all, value_all, query_all, out_all,
+        k_ref, v_ref, shifted_ref, taps_ref, kernel_ref, skip_ref,
+    ) = refs[count : count + 21]
+    refs = refs[count + 21 :]
+    totals = refs[: count + 5]
+    input_grad, kernel_grad_ref, taps_grad_ref, skip_grad_ref = refs[count + 5 : count + 9]
+    refs = refs[count + 9 :]
+    out_term, query_term, key_term, value_term, gain_term = own_terms = refs[:5]
+    buffers = refs[5 : 5 + 4 * len(parts)]
+    refs = refs[5 + 4 * len(parts) :]
+    held = dict(zip(kinds, refs[: len(kinds)]))
+    (
+        wide, sent_g, came_g, sent_kv, came_kv, query_grad,
+        send_sem, recv_sem, mine_sem, swap_sem,
+    ) = refs[len(kinds) :]
+    devices, channels = key_all.shape[0], key_all.shape[1]
+    rows, features = branch.shape
+    blocks, groups = lax.axis_size("seq"), lax.axis_size("dp")
+    greet(all_others()[2])
+    reduce = Reduce(
+        parts, early + own_terms, totals, buffers, (early, held), send_sem, recv_sem, mine_sem
+    )
+    reduce.fetch_first()
+
+    def slots(value, columns):
+        return value.reshape(2, 2, 4, 2, channels, columns)
+
+    gated_grad = contract(flat_weight(out_all), branch[...], 1, 1)
+    sent_g[...] = (gated_grad * queries[...]).reshape(devices, channels, rows).astype(BF16)
+    over = Swap(sent_g, came_g, swap_sem.at[0], swap_sem.at[1])
+    over.start()
+    reduce.start(range(count))
+    query_grad[...] = (gated_grad * ssm[...].astype(F32)).astype(BF16)
+    out_term[...] = slots(product(gated[...], branch[...]), features).astype(BF16)
+    query_term[...] = slots(contract(normed[...], query_grad[...], 1, 1), features).astype(BF16)
+    reduce.start((count, count + 1))
+    reduce.run(PLACES[0])
+    over.wait()
+    wide[:, :channels, :] = came_g[...].astype(F32)
     for ch in range(channels):
-        taps = toeplitz(taps_ref[ch : ch + 1, :], rows)[:, : 2 * rows].astype(BF16)
-        longer = toeplitz(kernel_ref[ch : ch + 1, :], rows)[:, :span].astype(BF16)
-        out_grad = grad_ref[ch]
-        skip = skip_ref[ch : ch + 1, :1]
-        values = v_ref[ch].astype(F32)
-        shifted = shifted_ref[ch]
-        signal = shifted * values
-        wide_grad = out_grad.astype(F32)
-        later = block_spread(wide_grad, blocks, blocks, groups, rows).astype(BF16)
-        signal_grad = product_back(later, longer) + skip * wide_grad
-        kernel_grad_ref[ch : ch + 1, :] = lag_sums(signal.astype(BF16), later, wide)
-        skip_grad_ref[ch : ch + 1, :] = jnp.broadcast_to(
-            jnp.sum(jnp.sum(signal * wide_grad, axis=0, keepdims=True), axis=1, keepdims=True),
-            (1, 128),
+        row = slice(ch, ch + 1)
+        grad_k, grad_v, kernel_grad_ref[row, :], taps_grad_ref[row, :], skip_grad = mix_back(
+            blocks, groups, rows, wide[:, ch, :], k_ref[ch], v_ref[ch], shifted_ref[ch],
+            taps_ref[row, :], kernel_ref[row, :], skip_ref[row, :1],
         )
-        shifted_grad = values * signal_grad
-        grad_v_ref[ch] = (shifted * signal_grad).astype(BF16)
-        next_two = block_spread(shifted_grad, blocks, 2, groups, rows).astype(BF16)
-        grad_k_ref[ch] = product_back(next_two, taps).astype(BF16)
-        taps_grad_ref[ch : ch + 1, :] = lag_sums(k_ref[ch], next_two, narrow)
+        wide[:, ch, :], wide[:, channels + ch, :] = grad_k, grad_v
+        skip_grad_ref[row, :] = jnp.broadcast_to(skip_grad, (1, 128))
+        if ch % 8 == 7:
+            reduce.run(PLACES[1 + ch // 8])
+    sent_kv[...] = wide[...].astype(BF16)
+    back = Swap(sent_kv, came_kv, swap_sem.at[2], swap_sem.at[3])
+    back.start()
+    reduce.run(PLACES[4])
+    back.wait()
+    wide[...] = came_kv[...].astype(F32)
+    key_grad = wide[:, :channels, :].reshape(features, rows).astype(BF16)
+    value_grad = (wide[:, channels:, :].reshape(features, rows) * live[...]).astype(BF16)
+    key_term[...] = slots(contract(normed[...], key_grad, 1, 1), features).astype(BF16)
+    value_term[...] = slots(contract(normed[...], value_grad, 1, 1), features).astype(BF16)
+    reduce.start((count + 2, count + 3))
+    normed_grad = product(flat_weight(query_all), query_grad[...])
+    normed_grad += product(flat_weight(key_all), key_grad)
+    normed_grad += product(flat_weight(value_all), value_grad)
+    gain_grad = jnp.sum(normed_grad * standard[...], axis=1, keepdims=True)
+    lane = lax.broadcasted_iota(jnp.int32, (features, 128), 1)
+    gain_term[...] = slots(jnp.where(lane == 0, gain_grad, gain_in[...]), 128)
+    reduce.start((count + 4,))
+    scaled = normed_grad * gains[...].reshape(features, 128)[:, :1]
+    scaled = (
+        scaled
+        - jnp.mean(scaled, axis=0, keepdims=True)
+        - standard[...] * jnp.mean(scaled * standard[...], axis=0, keepdims=True)
+    )
+    input_grad[...] = grad_one[...] + (scaled * inverse[:1, :]).T
+    reduce.finish()
+
+
+def last_layer(terms, gain_in, branch, grad_one, live, kept, weights, mixer_rows, collective_id):
+    standard, inverse, normed, queries, ssm, gated, k_own, v_own, shifted = kept
+    gains, key_all, value_all, query_all, out_all = weights
+    devices, channels, features = key_all.shape
+    rows = branch.shape[0]
+    count = len(terms)
+    square = (channels, features)
+    shapes = [a.shape[1:] for a in terms] + [square] * 4 + [(channels, 128)]
+    types = [BF16] * (count + 4) + [F32]
+    parts = cut(shapes)
+    kinds = sorted({(part[2], part[4]) for part in parts if part[0] < count})
+    scratch = [pltpu.VMEM((2, 2, 4, 2) + s, t) for s, t in zip(shapes[count:], types[count:])]
+    for i, _, part_rows, _, columns, x_last in parts:
+        for lead in ((2, 4, 2), (4, 2) if x_last else (2, 4), (4,), (3,)):
+            scratch.append(pltpu.VMEM(lead + (part_rows, columns), types[i]))
+    scratch += [pltpu.VMEM((2, 2, 4, 2) + kind, BF16) for kind in kinds]
+    scratch += [
+        pltpu.VMEM((devices, 2 * channels, rows), F32),
+        pltpu.VMEM((devices, channels, rows), BF16),
+        pltpu.VMEM((devices, channels, rows), BF16),
+        pltpu.VMEM((devices, 2 * channels, rows), BF16),
+        pltpu.VMEM((devices, 2 * channels, rows), BF16),
+        pltpu.VMEM((features, rows), BF16),
+        pltpu.SemaphoreType.DMA((len(parts), 6)),
+        pltpu.SemaphoreType.DMA((len(parts), 6)),
+        pltpu.SemaphoreType.DMA((len(parts),)),
+        pltpu.SemaphoreType.DMA((4,)),
+    ]
+    vmem, anywhere = pl.BlockSpec(memory_space=pltpu.VMEM), pl.BlockSpec(memory_space=pl.ANY)
+    results = [jax.ShapeDtypeStruct(s, F32) for s in shapes]
+    results.append(jax.ShapeDtypeStruct((rows, features), F32))
+    results += [jax.ShapeDtypeStruct(a.shape, F32) for a in (mixer_rows[1], mixer_rows[0])]
+    results.append(jax.ShapeDtypeStruct((channels, 128), F32))
+    out = pl.pallas_call(
+        partial(last_body, parts, count, kinds),
+        out_shape=results,
+        in_specs=[anywhere] * count + [vmem] * 21,
+        out_specs=[vmem] * len(results),
+        scratch_shapes=scratch,
+        compiler_params=pltpu.CompilerParams(
+            collective_id=collective_id, has_side_effects=True, vmem_limit_bytes=62 * MIB
+        ),
+    )(
+        *[a.reshape((2, 2, 4, 2) + a.shape[1:]) for a in terms],
+        gain_in, branch, grad_one, live, gated, normed, queries, ssm, standard, inverse,
+        gains, key_all, value_all, query_all, out_all,
+        k_own, v_own, shifted, *mixer_rows,
+    )
+    return out[: count + 5], out[count + 5 :]
+
+
+def last_layer_apart(terms, gain_in, branch, grad_one, live, kept, weights, mixer_rows):
+    standard, inverse, normed, queries, ssm, gated, k_own, v_own, shifted = kept
+    gains, key_all, value_all, query_all, out_all = weights
+    devices, channels, features = key_all.shape
+    rows = branch.shape[0]
+    blocks, groups = lax.axis_size("seq"), lax.axis_size("dp")
+    key_all, value_all, query_all, out_all = [
+        a.reshape(features, features) for a in (key_all, value_all, query_all, out_all)
+    ]
+    gated_grad = contract(out_all, branch, 1, 1)
+    query_grad = (gated_grad * ssm.astype(F32)).astype(BF16)
+    sent = (gated_grad * queries).reshape(devices, channels, rows).astype(BF16)
+    own = lax.all_to_all(sent, BOTH, 0, 0, tiled=True).transpose(1, 0, 2)
+    per_channel = jax.ShapeDtypeStruct(own.shape, BF16)
+    grad_k, grad_v, kernel_grad, taps_grad, skip_grad = local_call(
+        partial(mixer_back_body, blocks, groups, rows),
+        [per_channel, per_channel]
+        + [jax.ShapeDtypeStruct(a.shape, F32) for a in (mixer_rows[1], mixer_rows[0])]
+        + [jax.ShapeDtypeStruct((channels, 128), F32)],
+        own, k_own, v_own, shifted, *mixer_rows,
+    )
+    sent = jnp.stack([grad_k.transpose(1, 0, 2), grad_v.transpose(1, 0, 2)], axis=1)
+    came = lax.all_to_all(sent, BOTH, 0, 0, tiled=True)
+    key_grad = came[:, 0].reshape(features, rows)
+    value_grad = (came[:, 1].reshape(features, rows) * live).astype(BF16)
+    normed_grad = (
+        product(query_all, query_grad) + product(key_all, key_grad) + product(value_all, value_grad)
+    )
+    gain_grad = jnp.sum(normed_grad * standard, axis=1, keepdims=True)
+    lane = lax.broadcasted_iota(jnp.int32, (features, 128), 1)
+    gain_term = jnp.where(lane == 0, gain_grad, gain_in)
+    scaled = normed_grad * gains.reshape(features, 128)[:, :1]
+    scaled = (
+        scaled
+        - jnp.mean(scaled, axis=0, keepdims=True)
+        - standard * jnp.mean(scaled * standard, axis=0, keepdims=True)
+    )
+    input_grad = grad_one + (scaled * inverse[:1]).T
+    last = [product(gated, branch)]
+    last += [contract(normed, g, 1, 1) for g in (query_grad, key_grad, value_grad)]
+    last = [a.reshape(devices, channels, features).astype(BF16) for a in last]
+    last.append(gain_term.reshape(devices, channels, 128))
+    sums = [
+        lax.psum_scatter(a, BOTH, scatter_dimension=0, tiled=False).astype(F32)
+        for a in list(terms) + last
+    ]
+    return sums, [input_grad, kernel_grad, taps_grad, skip_grad]
 
 
 def allowed_keys(place, length, rows, keys):
@@ -874,28 +1050,14 @@
         every, kept = first_layer(weights, tokens[0], live_lane, *mixer_rows, 1)
     else:
         every, kept = first_layer_apart(weights, tokens[0], live_lane, *mixer_rows)
-    residual_one, standard, inverse, normed_turned, queries, ssm_out, gated, k_own, v_own, shifted = kept
+    residual_one = kept[0]
     gain_one, gain_two, gain_three, gain_four = [
         every[0][:, :, n].reshape(features) for n in range(4)
     ]
-    (
-        key_all, value_all, query_all, out_one_all, up_one_all, down_one_all, qkv_all,
-        out_two_all, late_up, late_down,
-    ) = [g.reshape((-1, g.shape[2])) for g in every[1:]]
-    residual_zero = tokens[0].astype(F32)
-
-    def to_channels(pieces, collective_id):
-        sent = jnp.stack([p.reshape(devices, channels, rows) for p in pieces], axis=1)
-        came = swap_all(sent, collective_id)
-        came = came.transpose(1, 2, 0, 3)
-        return [came[n] for n in range(len(pieces))]
-
-    def to_rows(pieces, collective_id):
-        sent = jnp.stack([p.transpose(1, 0, 2) for p in pieces], axis=1)
-        came = swap_all(sent, collective_id)
-        return [came[:, n].reshape(features, rows) for n in range(len(pieces))]
-
-    per_channel = (channels, devices, rows)
+    up_one_all, down_one_all, qkv_all, out_two_all, late_up, late_down = [
+        g.reshape((-1, g.shape[2])) for g in every[5:]
+    ]
+
     residual_two, stored_two = feed_forward(residual_one, gain_two, up_one_all, down_one_all)
     normed_three = layer_norm(residual_two, gain_three).astype(BF16)
     joint = product(normed_three, qkv_all).astype(BF16)
@@ -915,12 +1077,6 @@
     grad_three, grad_norm_four, grad_up_two, grad_down_two = feed_back(
         residual_three, gain_four, late_up, late_down, stored_four, grad_four
     )
-    grad_up_two = lax.psum_scatter(
-        grad_up_two.astype(BF16), BOTH, scatter_dimension=0, tiled=True
-    ).astype(F32)
-    grad_down_two = lax.psum_scatter(
-        grad_down_two.astype(BF16), BOTH, scatter_dimension=0, tiled=True
-    ).astype(F32)
     branch_three = grad_three.astype(BF16)
     grad_out_two = product_sum(attended, branch_three)
     grad_attended = product_back(branch_three, out_two_all).astype(BF16)
@@ -944,64 +1100,30 @@
         residual_one, gain_two, up_one_all, down_one_all, stored_two, grad_two
     )
     branch_one = grad_one.astype(BF16)
-    grad_out_one = product(gated, branch_one)
-    gated_grad = contract(out_one_all, branch_one, 1, 1)
-    grad_queries = (gated_grad * ssm_out.astype(F32)).astype(BF16)
-    ssm_grad = (gated_grad * queries).astype(BF16)
-    (grad_own,) = to_channels([ssm_grad], 6)
-    grad_k_own, grad_v_own, kernel_grad, taps_grad, skip_grad = local_call(
-        partial(mixer_back_body, blocks, groups, rows),
-        [
-            jax.ShapeDtypeStruct(per_channel, BF16),
-            jax.ShapeDtypeStruct(per_channel, BF16),
-            jax.ShapeDtypeStruct((channels, wide), F32),
-            jax.ShapeDtypeStruct((channels, narrow), F32),
-            jax.ShapeDtypeStruct((channels, 128), F32),
-        ],
-        grad_own, k_own, v_own, shifted, tap_row, kernel_row, skip_row,
-    )
-    grad_keys, grad_values = to_rows([grad_k_own, grad_v_own], 7)
-    grad_values = (grad_values.astype(F32) * live_lane).astype(BF16)
+    gain_in = jnp.stack(
+        [jnp.zeros_like(grad_norm_two), grad_norm_two, grad_norm_three, grad_norm_four], axis=1
+    )
+    gain_in = jnp.pad(gain_in, ((0, 0), (0, 124)))
+    terms = [
+        g.astype(BF16).reshape(devices, -1, g.shape[1])
+        for g in (
+            grad_up_two, grad_down_two, grad_qkv_weight, grad_out_two, grad_up_one, grad_down_one
+        )
+    ]
+    last = (terms, gain_in, branch_one, grad_one, live_lane, kept[1:], every[:5], mixer_rows)
+    if grouped():
+        sums, rest = last_layer(*last, 2)
+    else:
+        sums, rest = last_layer_apart(*last)
+    grad_up_two, grad_down_two, grad_qkv_weight, grad_out_two, grad_up_one, grad_down_one = sums[:6]
+    grad_out_one, grad_query_one, grad_key_one, grad_value_one, gain_grads = sums[6:]
+    gain_grads = gain_grads[:, :4].T
+    input_grad, kernel_grad, taps_grad, skip_grad = rest
     grad_decay_log, grad_turn_angle, grad_mix_real, grad_mix_imag = kernel_pull(
         kernel_grad[:, : rows * blocks]
     )
     grad_shift_taps = taps_grad[:, : shift_taps.shape[1]]
     grad_skip_gain = skip_grad[:, 0]
-
-    grad_query_one = contract(normed_turned, grad_queries, 1, 1)
-    grad_key_one = contract(normed_turned, grad_keys, 1, 1)
-    grad_value_one = contract(normed_turned, grad_values, 1, 1)
-    grad_normed_one = (
-        contract(grad_queries, query_all, 0, 1)
-        + contract(grad_keys, key_all, 0, 1)
-        + contract(grad_values, value_all, 0, 1)
-    )
-    grad_from_one, grad_norm_one = jax.vjp(layer_norm, residual_zero, gain_one)[1](
-        grad_normed_one
-    )
-    input_grad = grad_one + grad_from_one
-
-    gain_grads = jnp.stack([grad_norm_one, grad_norm_two, grad_norm_three, grad_norm_four])
-    gain_grads = gain_grads.reshape(4, devices, channels).transpose(1, 0, 2)
-    gain_grads = jnp.pad(gain_grads, ((0, 0), (0, 4), (0, 128 - channels)))
-
-    def owned(grad):
-        return grad.astype(BF16).reshape(devices, -1, grad.shape[1])
-
-    sums = reduce_all(
-        [gain_grads]
-        + [
-            owned(g)
-            for g in (
-                grad_up_one, grad_down_one, grad_qkv_weight, grad_out_two, grad_out_one,
-                grad_query_one, grad_key_one, grad_value_one,
-            )
-        ],
-        8,
-    )
-    gain_grads, grad_up_one, grad_down_one, grad_qkv_weight, grad_out_two, grad_out_one = sums[:6]
-    grad_query_one, grad_key_one, grad_value_one = sums[6:]
-    gain_grads = gain_grads[:4, :channels]
     return (
         activations[None], input_grad[None],
         gain_grads[0], grad_query_one, grad_key_one, grad_value_one,

time: 532 us -> 468 us (0.88)
  matrix products: 74.8 us -> 52.1 us
  Pallas kernels: 384 us -> 366 us
  between operations: 16.8 us -> 2.82 us
  other arithmetic: 26.5 us -> 15.9 us
    dot_general x26 -> x18, matrix products: 72.2 us -> 49.5 us  [contract(): lax.dot_general(left_side, right_side, (((left_dim,), (right_dim,)), ((),...]
    pallas_call x3 -> x2, Pallas kernels: 37 us -> 17.4 us  [local_call(): pl.pallas_call(body, out_shape=out_shape, in_specs=[smem] * scalars + [vm...]
    convert_element_type x5 -> x1, other arithmetic: 8.5 us -> 1.04 us  [shards(): branch_one = grad_one.astype(BF16)]
    pallas_call x1, Pallas kernels: 150 us -> 157 us  [first_layer(): pl.pallas_call(partial(first_body, parts, count), out_shape=[jax.ShapeDty...]
    pallas_call x3 -> x1, Pallas kernels: 158 us -> 154 us  [last_layer(): pl.pallas_call(partial(last_body, parts, count, kinds), out_shape=results...]
    unnamed x253 -> x169, local copies, waits for them, and re-layouts: 17.2 us -> 16.9 us
  transfers between devices with their start and end apart: 2 -> 0, of which waited for: 0 -> 0; matrix products, arithmetic and copies ran while one was open for 15% -> 0% of each run, Pallas kernels for 39% -> 0%
where the time goes in v3:
time: 468 us; the launch traced here: 463 us
  Pallas kernels  366 us (78%)
  matrix products  52.1 us (11%)
  local copies, waits for them, and re-layouts  26.3 us (6%)
  other arithmetic  15.9 us (3%)
    pallas_call x1, Pallas kernels, first_layer(): pl.pallas_call(partial(first_body, parts, count), out_shape=[jax.ShapeDty...  157 us
    pallas_call x1, Pallas kernels, last_layer(): pl.pallas_call(partial(last_body, parts, count, kinds), out_shape=results...  154 us
    dot_general x18, matrix products, contract(): lax.dot_general(left_side, right_side, (((left_dim,), (right_dim,)), ((),...  49.5 us
    pallas_call x1, Pallas kernels, gather_line(): pl.pallas_call(line_body, out_shape=jax.ShapeDtypeStruct((4,) + value.sha...  20 us
    pallas_call x1, Pallas kernels, sum_line(): pl.pallas_call(line_sum_body, out_shape=jax.ShapeDtypeStruct(value.shape[...  18 us
    pallas_call x2, Pallas kernels, local_call(): pl.pallas_call(body, out_shape=out_shape, in_specs=[smem] * scalars + [vm...  17.4 us
    unnamed x169, local copies, waits for them, and re-layouts  16.9 us

profile of v3, /device:TPU:0, one launch (start us, length us, event | category | flops | bytes accessed | tf_op | source)
XLA Modules:
  0.0 463.2 jit_solution(4114014470882056301)
XLA Ops:
  7.3 1.2 multiply_subtract_fusion
  8.6 1.4 fusion.30
  11.2 157.0 %shard_map.390 = (f32[32,24,128]{2,1,0:T(8,128)S(1)}, bf16[32,24,768]{2,1,0:T(8,128)(2,1)}, bf16[32,24,768]{2,1,0:T(8,128)(2,1)}, bf16[32,24,768]{2,1,0:T(8,128)...) custom-call(f32[24,128]{1,0:T(8,128)S(1)} %pad_convert_fusion.1.refs, ...), custom_call_target="tpu_custom_call" | custom-call | tf_op jit(solution)/shard_map/pallas_call | solution.py:668
  174.9 3.5 fusion.68
  178.4 4.9 %fusion.74 = (f32[192]{0:T(256)S(1)}, f32[192,768]{1,0:T(8,128)S(1)}) fusion(f32[192,768]{1,0:T(8,128)S(1)} %get-tuple-element.62, bf16[3072,768]{1,0:T(8,128)(2,1)} %bitcast.96, f32[192,3072]{1,0:T(8,128)S(1)} %fusion.68), kind=kOutput, calls=%fused_computation.158 | convolution fusion | flops 911572800 | bytes 8258304 | tf_op jit(solution)/shard_map/dot_general | solution.py:463
  185.4 20.0 %shard_map.391 = bf16[4,192,1536]{2,1,0:T(8,128)(2,1)} custom-call(bf16[192,1536]{1,0:T(8,128)(2,1)} %slice.53.src), custom_call_target="tpu_custom_call" | custom-call | tf_op jit(solution)/shard_map/pallas_call | solution.py:389
  205.4 1.7 copy-done
  207.0 6.6 %shard_map.392 = (bf16[192,768]{1,0:T(8,128)(2,1)S(1)}, f32[192,128]{1,0:T(8,128)S(1)}) custom-call(s32[2]{0:T(128)S(1)} %pad_add_fusion.where_ref, bf16[192,768]{1,0:T(8,128)(2,1)S(1)} %slice.52.q_ref, bf16[768,1536]{1,0:T(8,128)(2,1)S(1)} %bitcast.69), custom_call_target="tpu_custom_call" | custom-call | tf_op jit(solution)/shard_map/pallas_call | solution.py:1006
  213.7 1.8 fusion.75
  215.7 3.6 fusion.69
  219.4 2.3 fusion.16
  221.7 2.4 fusion.13
  224.1 1.9 multiply_reduce_fusion.1
  228.2 10.7 %shard_map.393 = (bf16[192,768]{1,0:T(8,128)(2,1)S(1)}, bf16[768,1536]{1,0:T(8,128)(2,1)S(1)}) custom-call(s32[2]{0:T(128)S(1)} %pad_add_fusion.where_ref, bf16[192,768]{1,0:T(8,128)(2,1)S(1)} %slice.52.q_ref, bf16[768,1536]{1,0:T(8,128)(2,1)S(1)} %bitcast.70, f32[192,128]{1,0:T(8,128)S(1)} %get-tuple-element.71.log_ref, ...), custom_call_target="tpu_custom_call" | custom-call | tf_op jit(solution)/shard_map/pallas_call | solution.py:1006
  239.0 18.0 %shard_map.394 = f32[192,1536]{1,0:T(8,128)S(1)} custom-call(bf16[2,2,192,1536]{3,2,1,0:T(8,128)(2,1)S(1)} %bitcast.71), custom_call_target="tpu_custom_call" | custom-call | tf_op jit(solution)/shard_map/pallas_call | solution.py:438
  257.1 1.5 multiply_reduce_fusion.2
  259.5 1.0 copy-done.37
  260.5 2.6 fusion.6
  263.2 1.9 multiply_reduce_fusion
  265.5 1.0 fusion.70
  267.5 1.6 convolution_convert_fusion.6
  269.1 5.3 %convolution_convert_fusion.1 = bf16[3072,768]{1,0:T(8,128)(2,1)} fusion(f32[192,768]{1,0:T(8,128)} %copy-done.41, f32[192,3072]{1,0:T(8,128)S(1)} %copy-done.38), kind=kOutput, calls=%fused_computation.1 | convolution fusion | flops 913784832 | bytes 7667712 | tf_op jit(solution)/shard_map/dot_general | solution.py:463
  274.3 3.0 convolution_convert_fusion
  277.4 4.2 convolution_convert_fusion.3
  281.5 3.7 convolution_convert_fusion.2
  285.2 3.7 convolution_convert_fusion.4
  288.9 153.8 %shard_map.395 = (f32[24,3072]{1,0:T(8,128)}, f32[96,768]{1,0:T(8,128)}, f32[24,2304]{1,0:T(8,128)}, f32[24,768]{1,0:T(8,128)}, f32[24,3072]{1,0:T(8,128)}, /*in...) custom-call(bf16[2,2,4,2,24,3072]{5,4,3,2,1,0:T(8,128)(2,1)} %bitcas, ...), custom_call_target="tpu_custom_call" | custom-call | tf_op jit(solution)/shard_map/pallas_call | solution.py:894
  442.8 1.4 slice_reduce_fusion.7
  445.6 1.3 slice.46
  448.7 1.0 fusion.58
  449.7 1.9 multiply_reduce_fusion.10
  451.7 1.9 fusion.37
  (234 shorter events, 32.8 us)
Async XLA Ops:
  0.7 10.4 %copy-start.15 = (bf16[96,768]{1,0:T(8,128)(2,1)S(1)}, bf16[96,768]{1,0:T(8,128)(2,1)}, u32[]{:S(2)}) copy-start(bf16[96,768]{1,0:T(8,128)(2,1)} %refs_10_.1) | copy-start | bytes 442372
  0.7 10.4 %copy-start.14 = (bf16[24,3072]{1,0:T(8,128)(2,1)S(1)}, bf16[24,3072]{1,0:T(8,128)(2,1)}, u32[]{:S(2)}) copy-start(bf16[24,3072]{1,0:T(8,128)(2,1)} %refs_9_.1) | copy-start | bytes 442372
  0.7 10.4 %copy-start.22 = (bf16[24,768]{1,0:T(8,128)(2,1)S(1)}, bf16[24,768]{1,0:T(8,128)(2,1)}, u32[]{:S(2)}) copy-start(bf16[24,768]{1,0:T(8,128)(2,1)} %refs_8_.1) | copy-start | bytes 110596
  0.7 10.4 %copy-start.17 = (bf16[24,2304]{1,0:T(8,128)(2,1)S(1)}, bf16[24,2304]{1,0:T(8,128)(2,1)}, u32[]{:S(2)}) copy-start(bf16[24,2304]{1,0:T(8,128)(2,1)} %refs_7_.1) | copy-start | bytes 331780
  0.7 10.4 %copy-start.13 = (bf16[96,768]{1,0:T(8,128)(2,1)S(1)}, bf16[96,768]{1,0:T(8,128)(2,1)}, u32[]{:S(2)}) copy-start(bf16[96,768]{1,0:T(8,128)(2,1)} %refs_6_.1) | copy-start | bytes 442372
  0.7 10.4 %copy-start.12 = (bf16[24,3072]{1,0:T(8,128)(2,1)S(1)}, bf16[24,3072]{1,0:T(8,128)(2,1)}, u32[]{:S(2)}) copy-start(bf16[24,3072]{1,0:T(8,128)(2,1)} %refs_5_.1) | copy-start | bytes 442372
  0.7 10.4 %copy-start.21 = (bf16[24,768]{1,0:T(8,128)(2,1)S(1)}, bf16[24,768]{1,0:T(8,128)(2,1)}, u32[]{:S(2)}) copy-start(bf16[24,768]{1,0:T(8,128)(2,1)} %refs_4_.1) | copy-start | bytes 110596
  0.7 10.4 %copy-start.19 = (bf16[24,768]{1,0:T(8,128)(2,1)S(1)}, bf16[24,768]{1,0:T(8,128)(2,1)}, u32[]{:S(2)}) copy-start(bf16[24,768]{1,0:T(8,128)(2,1)} %refs_2_.1) | copy-start | bytes 110596
  0.7 10.4 %copy-start.18 = (bf16[24,768]{1,0:T(8,128)(2,1)S(1)}, bf16[24,768]{1,0:T(8,128)(2,1)}, u32[]{:S(2)}) copy-start(bf16[24,768]{1,0:T(8,128)(2,1)} %refs_1_.1) | copy-start | bytes 110596
  0.8 10.4 %copy-start.20 = (bf16[24,768]{1,0:T(8,128)(2,1)S(1)}, bf16[24,768]{1,0:T(8,128)(2,1)}, u32[]{:S(2)}) copy-start(bf16[24,768]{1,0:T(8,128)(2,1)} %refs_3_.1) | copy-start | bytes 110596
  0.8 10.4 %copy-start.11 = (bf16[1,192,768]{2,1,0:T(8,128)(2,1)S(1)}, bf16[1,192,768]{2,1,0:T(8,128)(2,1)}, u32[]{:S(2)}) copy-start(bf16[1,192,768]{2,1,0:T(8,128)(2,1)} %param.23) | copy-start | bytes 884740
  1.7 8.3 %copy-start.68 = (f32[32]{0:T(128)}, f32[32]{0:T(128)S(1)}, u32[]{:S(2)}) copy-start(f32[32]{0:T(128)S(1)} %iota_negate_fusion) | copy-start | bytes 388
  2.2 166.0 %copy-start.23 = (f32[1,192]{1,0:T(1,128)}, f32[1,192]{1,0:T(1,128)S(1)}, u32[]{:S(2)}) copy-start(f32[1,192]{1,0:T(1,128)S(1)} %compare_convert_fusion.refs_12_.refs_9_) | copy-start | bytes 2308
  6.6 161.7 %copy-start.16 = (f32[24,128]{1,0:T(8,128)}, f32[24,128]{1,0:T(8,128)S(1)}, u32[]{:S(2)}) copy-start(f32[24,128]{1,0:T(8,128)S(1)} %broadcast_in_dim.18.refs_15_.refs_26_) | copy-start | bytes 36868
  7.3 161.0 %copy-start.5 = (f32[24,640]{1,0:T(8,128)}, f32[24,640]{1,0:T(8,128)S(1)}, u32[]{:S(2)}) copy-start(f32[24,640]{1,0:T(8,128)S(1)} %pad_convert_fusion.refs_13_.refs_24_) | copy-start | bytes 184324
  11.2 167.2 %copy-start.2 = (f32[24,1024]{1,0:T(8,128)}, f32[24,1024]{1,0:T(8,128)S(1)}, u32[]{:S(2)}) copy-start(f32[24,1024]{1,0:T(8,128)S(1)} %pad.24.refs_14_.refs_25_) | copy-start | bytes 294916
  239.0 18.1 %copy-start.27 = (bf16[32,24,2304]{2,1,0:T(8,128)(2,1)S(1)}, bf16[32,24,2304]{2,1,0:T(8,128)(2,1)}, u32[]{:S(2)}) copy-start(bf16[32,24,2304]{2,1,0:T(8,128)(2,1)} %get-tuple-element.66) | copy-start | bytes 10616836
  288.9 159.0 %copy-start.29 = (f32[24,64,32]{1,2,0:T(8,128)S(1)}, f32[24,64,32]{1,2,0:T(8,128)}, u32[]{:S(2)}) copy-start(f32[24,64,32]{1,2,0:T(8,128)} %copy-done.28) | copy-start | bytes 589828
  288.9 159.7 %copy-start.31 = (f32[24,64,24]{1,2,0:T(8,128)S(1)}, f32[24,64,24]{1,2,0:T(8,128)}, u32[]{:S(2)}) copy-start(f32[24,64,24]{1,2,0:T(8,128)} %copy-done.30) | copy-start | bytes 442372
  288.9 159.8 %copy-start.33 = (f32[24,64,24]{1,2,0:T(8,128)S(1)}, f32[24,64,24]{1,2,0:T(8,128)}, u32[]{:S(2)}) copy-start(f32[24,64,24]{1,2,0:T(8,128)} %copy-done.32) | copy-start | bytes 442372
  442.7 8.9 %copy-start.57 = (f32[24,64]{1,0:T(8,128)S(1)}, f32[24,64]{1,0:T(8,128)}, u32[]{:S(2)}) copy-start(f32[24,64]{1,0:T(8,128)} %copy-done.56) | copy-start | bytes 18436
  442.7 8.9 %copy-start.59 = (f32[24,64]{1,0:T(8,128)S(1)}, f32[24,64]{1,0:T(8,128)}, u32[]{:S(2)}) copy-start(f32[24,64]{1,0:T(8,128)} %copy-done.58) | copy-start | bytes 18436
  442.8 8.9 %copy-start.67 = (f32[24]{0:T(128)S(1)}, f32[24]{0:T(128)}, u32[]{:S(2)}) copy-start(f32[24]{0:T(128)} %copy-done.66) | copy-start | bytes 292
  448.6 8.2 %copy-start.63 = (f32[24,768]{1,0:T(8,128)S(1)}, f32[24,768]{1,0:T(8,128)}, u32[]{:S(2)}) copy-start(f32[24,768]{1,0:T(8,128)} %get-tuple-element.174) | copy-start | bytes 221188
  448.7 8.9 %copy-start.62 = (f32[24,768]{1,0:T(8,128)S(1)}, f32[24,768]{1,0:T(8,128)}, u32[]{:S(2)}) copy-start(f32[24,768]{1,0:T(8,128)} %get-tuple-element.175) | copy-start | bytes 221188
  448.7 9.5 %copy-start.61 = (f32[24,768]{1,0:T(8,128)S(1)}, f32[24,768]{1,0:T(8,128)}, u32[]{:S(2)}) copy-start(f32[24,768]{1,0:T(8,128)} %get-tuple-element.182) | copy-start | bytes 221188
  448.7 10.1 %copy-start.54 = (f32[24,3072]{1,0:T(8,128)S(1)}, f32[24,3072]{1,0:T(8,128)}, u32[]{:S(2)}) copy-start(f32[24,3072]{1,0:T(8,128)} %get-tuple-element.184) | copy-start | bytes 884740
  449.7 9.8 %copy-start.53 = (f32[96,768]{1,0:T(8,128)S(1)}, f32[96,768]{1,0:T(8,128)}, u32[]{:S(2)}) copy-start(f32[96,768]{1,0:T(8,128)} %get-tuple-element.185) | copy-start | bytes 884740
  449.7 10.5 %copy-start.55 = (f32[24,2304]{1,0:T(8,128)S(1)}, f32[24,2304]{1,0:T(8,128)}, u32[]{:S(2)}) copy-start(f32[24,2304]{1,0:T(8,128)} %get-tuple-element.187) | copy-start | bytes 663556
  451.7 9.3 %copy-start.60 = (f32[24,768]{1,0:T(8,128)S(1)}, f32[24,768]{1,0:T(8,128)}, u32[]{:S(2)}) copy-start(f32[24,768]{1,0:T(8,128)} %get-tuple-element.188) | copy-start | bytes 221188
  451.7 9.9 %copy-start.52 = (f32[24,3072]{1,0:T(8,128)S(1)}, f32[24,3072]{1,0:T(8,128)}, u32[]{:S(2)}) copy-start(f32[24,3072]{1,0:T(8,128)} %get-tuple-element.190) | copy-start | bytes 884740
  453.6 8.7 %copy-start.51 = (f32[96,768]{1,0:T(8,128)S(1)}, f32[96,768]{1,0:T(8,128)}, u32[]{:S(2)}) copy-start(f32[96,768]{1,0:T(8,128)} %get-tuple-element.191) | copy-start | bytes 884740
  (47 other events, 154.3 us)
